TPU v7x, 128 devices: a whole 4x4x4 slice. The times are simulated.
128 devices in a mesh: seq: 4 (over x), ctx: 16 (over z, y), fsdp: 2 (over core).
Axes of the slice: x: 4, y: 4, z: 4, core: 2. Of those that a mesh axis runs over, the one named last changes fastest.
Arguments:
- tokens: bfloat16 [8, 2560, 1024], P(('seq', 'fsdp'), 'ctx'), may hold values from -6 to 6
- pairs: int32 [8, 16], P(('seq', 'fsdp')), may hold values from 0 to 15, each once within a row
- w_query: bfloat16 [1024, 1024], P(('ctx', 'fsdp')), may hold values from -0.1875 to 0.1875
- w_key: bfloat16 [1024, 512], P(('ctx', 'fsdp')), may hold values from -0.1875 to 0.1875
- w_value: bfloat16 [1024, 512], P(('ctx', 'fsdp')), may hold values from -0.1875 to 0.1875
- w_out: bfloat16 [1024, 1024], P(('ctx', 'fsdp')), may hold values from -2.5 to 2.5
- w_gate: bfloat16 [1024, 4608], P(('ctx', 'fsdp')), may hold values from -0.1875 to 0.1875
- w_up: bfloat16 [1024, 4608], P(('ctx', 'fsdp')), may hold values from -0.1875 to 0.1875
- w_down: bfloat16 [4608, 1024], P(('ctx', 'fsdp')), may hold values from -0.09375 to 0.09375
- g_attn: float32 [1024], replicated, may hold values from 0.1 to 1.9
- g_query: float32 [64], replicated, may hold values from 0.1 to 1.9
- g_key: float32 [64], replicated, may hold values from 0.1 to 1.9
- g_ffn: float32 [1024], replicated, may hold values from 0.1 to 1.9
- cotangent: bfloat16 [8, 2560, 1024], P(('seq', 'fsdp'), 'ctx'), may hold values from -6 to 6
Outputs:
- output: bfloat16 [8, 2560, 1024], P(('seq', 'fsdp'), 'ctx')
- grad_tokens: bfloat16 [8, 2560, 1024], P(('seq', 'fsdp'), 'ctx')
- grad_w_query: float32 [1024, 1024], P(('ctx', 'fsdp'))
- grad_w_key: float32 [1024, 512], P(('ctx', 'fsdp'))
- grad_w_value: float32 [1024, 512], P(('ctx', 'fsdp'))
- grad_w_out: float32 [1024, 1024], P(('ctx', 'fsdp'))
- grad_w_gate: float32 [1024, 4608], P(('ctx', 'fsdp'))
- grad_w_up: float32 [1024, 4608], P(('ctx', 'fsdp'))
- grad_w_down: float32 [4608, 1024], P(('ctx', 'fsdp'))
- grad_g_attn: float32 [1024], replicated
- grad_g_query: float32 [64], replicated
- grad_g_key: float32 [64], replicated
- grad_g_ffn: float32 [1024], replicated
Inputs may be any that keep to these rules, and one draw needn't show every extreme that they name: Each row of pairs holds every number of 0 to 15 once: device c of the context axis holds blocks pairs[s, c] and 31 - pairs[s, c] of sequence s, in this order, each of 80 tokens.
All inputs are finite; a program needn't handle non-finite values.
Results may differ from a plain program's by a relative error of at most 0.025.
Values may be sent and summed in bfloat16 or wider, within the bound.
A program may use at most 192 MiB of HBM per device.

v0:
```python
import functools

import jax
import jax.numpy as jnp
from jax import lax
from jax.sharding import Mesh
from jax.sharding import PartitionSpec as P

H = 16
KV = 8
HD = 64
FF = 4608
CTX = ("ctx_0", "ctx_1")
CTX_FSDP = ("ctx_0", "ctx_1", "fsdp")
SEQ_CTX_FSDP = ("seq", "ctx_0", "ctx_1", "fsdp")


EPSILON = 1e-05
ROPE_BASE = 1000000.0
NEG_LARGE = -1e30


def side_by_side(arrays, axis, dim, along):
    widths = [a.shape[along] for a in arrays]
    both = jnp.concatenate(arrays, axis=along)
    whole = lax.all_gather(both, axis, axis=dim, tiled=True)
    return tuple(jnp.split(whole, [sum(widths[:k]) for k in range(1, len(widths))], axis=along))


def in_one_piece(arrays, axis, dim, along):
    both = jnp.concatenate(arrays, axis=along)
    whole, at, outs = (lax.psum_scatter(both, axis, scatter_dimension=dim, tiled=True), 0, [])
    for a in arrays:
        outs.append(lax.slice_in_dim(whole, at, at + a.shape[along], axis=along))
        at += a.shape[along]
    return tuple(outs)


def packed_total(arrays, axis):
    ends = [0]
    for a in arrays:
        ends.append(ends[-1] + a.size)
    total = lax.psum(jnp.concatenate([a.ravel() for a in arrays]), axis)
    return tuple((total[b:e].reshape(a.shape) for a, b, e in zip(arrays, ends, ends[1:])))


def by_axis(x, axes):
    return functools.reduce(lax.psum, axes, x)


def rms_rows(values_in, gain):
    inv_rms = lax.rsqrt(jnp.mean(values_in * values_in, axis=-1, keepdims=True) + EPSILON)
    return (values_in * inv_rms * gain, inv_rms)


def rms_rows_back(values_in, gain, inv_rms, grad_in):
    weighted = grad_in * gain
    inner = jnp.mean(weighted * values_in, axis=-1, keepdims=True)
    grad_values = inv_rms * weighted - values_in * (inv_rms * inv_rms * inv_rms) * inner
    gain_terms = grad_in * values_in * inv_rms
    return (grad_values, gain_terms)


def block_positions(pair_row, block_len, ctx_size):
    blocks_of = jnp.stack([pair_row, 2 * ctx_size - 1 - pair_row], axis=1).reshape(-1)
    offsets = jnp.arange(block_len, dtype=jnp.int32)
    return (blocks_of[:, None] * block_len + offsets[None, :]).reshape(-1)


def angle_tables(positions, head_dim):
    frequencies = ROPE_BASE ** (-jnp.arange(0, head_dim // 2, dtype=jnp.float32) * 2.0 / head_dim)
    phases = positions.astype(jnp.float32)[:, None] * frequencies[None, :]
    phases = jnp.concatenate([phases, phases], axis=-1)
    return (jnp.cos(phases), jnp.sin(phases))


def rotate(values_in, cos_table, sin_table):
    half_dim = values_in.shape[-1] // 2
    turned = jnp.concatenate([-values_in[..., half_dim:], values_in[..., :half_dim]], axis=-1)
    return values_in * cos_table[:, None, :] + turned * sin_table[:, None, :]


def rotate_back(grad_in, cos_table, sin_table):
    half_dim = grad_in.shape[-1] // 2
    shifted = grad_in * sin_table[:, None, :]
    turned = jnp.concatenate([shifted[..., half_dim:], -shifted[..., :half_dim]], axis=-1)
    return grad_in * cos_table[:, None, :] + turned


def body(
    tokens,
    pairs,
    w_query,
    w_key,
    w_value,
    w_out,
    w_gate,
    w_up,
    w_down,
    g_attn,
    g_query,
    g_key,
    g_ffn,
    cotangent,
):
    local_rows = tokens.shape[1]
    ctx_size = lax.axis_size(CTX)
    length = local_rows * ctx_size
    groups = H // KV
    kv_width = KV * HD
    q_width = H * HD
    factor_qk = HD ** (-0.5)
    inputs = tokens[0].astype(jnp.float32)
    all_positions = block_positions(pairs[0], local_rows // 2, ctx_size)
    my_positions = lax.dynamic_slice_in_dim(
        all_positions, lax.axis_index(CTX) * local_rows, local_rows
    )
    cos_table, sin_table = angle_tables(my_positions, HD)
    full_query, full_key, full_value, full_out = side_by_side(
        (w_query, w_key, w_value, w_out), CTX_FSDP, 0, 1
    )
    normed_attn, inv_attn = rms_rows(inputs, g_attn)
    h_attn = normed_attn.astype(jnp.bfloat16)
    q_heads = jnp.dot(h_attn, full_query, preferred_element_type=jnp.float32).reshape(
        local_rows, H, HD
    )
    k_heads = jnp.dot(h_attn, full_key, preferred_element_type=jnp.float32).reshape(
        local_rows, KV, HD
    )
    v_local = jnp.dot(h_attn, full_value, preferred_element_type=jnp.float32).astype(jnp.bfloat16)
    q_normed, inv_query = rms_rows(q_heads, g_query)
    k_normed, inv_key = rms_rows(k_heads, g_key)
    queries = (
        rotate(q_normed, cos_table, sin_table)
        .astype(jnp.bfloat16)
        .reshape(local_rows, KV, groups, HD)
    )
    k_local = (
        rotate(k_normed, cos_table, sin_table).astype(jnp.bfloat16).reshape(local_rows, kv_width)
    )

    def key_scores(key_rows, key_positions):
        key_heads = key_rows.reshape(-1, KV, HD)
        raw_scores = (
            jnp.einsum("qkgd,nkd->kgqn", queries, key_heads, preferred_element_type=jnp.float32)
            * factor_qk
        )
        allowed = key_positions[None, :] <= my_positions[:, None]
        return (raw_scores, allowed)

    shards_per = max(1, 512 // local_rows)
    while ctx_size % shards_per:
        shards_per //= 2
    shards_per = min(shards_per, ctx_size)
    key_span = shards_per * local_rows
    block_total = length // key_span
    pieces = side_by_side((k_local, v_local), CTX, 0, 1)
    key_positions = all_positions
    row_top = jnp.full((KV, groups, local_rows), NEG_LARGE, jnp.float32)
    raw_scores, allowed = key_scores(pieces[0], key_positions)
    masked = jnp.where(allowed, raw_scores, NEG_LARGE)
    new_top = jnp.maximum(row_top, jnp.max(masked, axis=-1))
    weights_exp = jnp.where(allowed, jnp.exp(masked - new_top[..., None]), 0.0)
    row_total = jnp.sum(weights_exp, axis=-1)
    value_heads = pieces[1].reshape(-1, KV, HD)
    accum = jnp.einsum(
        "kgqn,nkd->kgqd",
        weights_exp.astype(jnp.bfloat16),
        value_heads,
        preferred_element_type=jnp.float32,
    )
    state_now = (new_top, row_total, accum)
    all_keys, all_values = side_by_side((k_local, v_local), CTX, 0, 1)
    row_top, row_total, accum = state_now
    log_total = row_top + jnp.log(row_total)
    out_heads = (accum / row_total[..., None]).transpose(2, 0, 1, 3)
    mixed = out_heads.reshape(local_rows, q_width).astype(jnp.bfloat16)
    branch = jnp.dot(mixed, full_out, preferred_element_type=jnp.float32)
    middle = inputs + branch
    normed_ffn, inv_ffn = rms_rows(middle, g_ffn)
    h_ffn = normed_ffn.astype(jnp.bfloat16)
    pieces = side_by_side((w_gate, w_up), CTX_FSDP, 0, 1)
    left_rows = h_ffn
    gate_act = jnp.dot(left_rows, pieces[0], preferred_element_type=jnp.float32)
    up_act = jnp.dot(left_rows, pieces[1], preferred_element_type=jnp.float32)
    sigmoid_gate = jax.nn.sigmoid(gate_act)
    silu_gate = gate_act * sigmoid_gate
    hidden = (silu_gate * up_act).astype(jnp.bfloat16)
    left_rows = hidden
    result = jnp.dot(
        left_rows,
        lax.all_gather(w_down, CTX_FSDP, axis=0, tiled=True),
        preferred_element_type=jnp.float32,
    )
    output = (middle + result).astype(jnp.bfloat16)[None]
    grad_result = cotangent[0]
    grad_out = grad_result.astype(jnp.float32)
    value_part = jnp.einsum(
        "rd,nd->rn",
        grad_result,
        lax.all_gather(w_down, CTX_FSDP, axis=0, tiled=True),
        preferred_element_type=jnp.float32,
    )
    grad_hidden = value_part
    grad_gate = (
        grad_hidden * up_act * (sigmoid_gate * (1.0 + gate_act * (1.0 - sigmoid_gate)))
    ).astype(jnp.bfloat16)
    grad_up = (grad_hidden * silu_gate).astype(jnp.bfloat16)
    pieces = side_by_side((w_gate, w_up), CTX_FSDP, 0, 1)
    value_part = jnp.einsum("rf,nf->rn", grad_gate, pieces[0], preferred_element_type=jnp.float32)
    value_part = value_part + jnp.einsum(
        "rf,nf->rn", grad_up, pieces[1], preferred_element_type=jnp.float32
    )
    grad_middle_norm, ffn_gain_terms = rms_rows_back(middle, g_ffn, inv_ffn, value_part)
    grad_middle = grad_out + grad_middle_norm
    grad_branch = grad_middle.astype(jnp.bfloat16)
    grad_mixed = jnp.einsum(
        "rd,hd->rh", grad_branch, full_out, preferred_element_type=jnp.float32
    ).astype(jnp.bfloat16)
    grad_heads = grad_mixed.reshape(local_rows, KV, groups, HD)
    delta = jnp.sum(grad_heads.astype(jnp.float32) * out_heads, axis=-1).transpose(1, 2, 0)

    def backward_step(grad_query, block_index):
        first_row = block_index * key_span
        key_rows = lax.dynamic_slice_in_dim(all_keys, first_row, key_span)
        value_rows = lax.dynamic_slice_in_dim(all_values, first_row, key_span)
        key_positions = lax.dynamic_slice_in_dim(all_positions, first_row, key_span)
        raw_scores, allowed = key_scores(key_rows, key_positions)
        probs = jnp.where(allowed, jnp.exp(raw_scores - log_total[..., None]), 0.0)
        value_heads = value_rows.reshape(key_span, KV, HD)
        grad_probs = jnp.einsum(
            "qkgd,nkd->kgqn", grad_heads, value_heads, preferred_element_type=jnp.float32
        )
        grad_scores = (probs * (grad_probs - delta[..., None])).astype(jnp.bfloat16)
        grad_query = grad_query + jnp.einsum(
            "kgqn,nkd->qkgd",
            grad_scores,
            key_rows.reshape(key_span, KV, HD),
            preferred_element_type=jnp.float32,
        )
        grad_key_rows = jnp.einsum(
            "kgqn,qkgd->nkd", grad_scores, queries, preferred_element_type=jnp.float32
        ).reshape(key_span, kv_width)
        grad_value_rows = jnp.einsum(
            "kgqn,qkgd->nkd",
            probs.astype(jnp.bfloat16),
            grad_heads,
            preferred_element_type=jnp.float32,
        ).reshape(key_span, kv_width)
        return (grad_query, (grad_key_rows, grad_value_rows))

    grad_query, (key_terms, value_terms) = lax.scan(
        backward_step,
        jnp.zeros((local_rows, KV, groups, HD), jnp.float32),
        jnp.arange(block_total, dtype=jnp.int32),
    )
    key_terms = key_terms.reshape(length, kv_width) * factor_qk
    value_terms = value_terms.reshape(length, kv_width)
    grad_keys_sum, grad_values_sum = tuple(
        (
            part.astype(jnp.float32)
            for part in in_one_piece(
                (key_terms.astype(jnp.bfloat16), value_terms.astype(jnp.bfloat16)), CTX, 0, 1
            )
        )
    )
    grad_q_rot = grad_query.reshape(local_rows, H, HD) * factor_qk
    grad_q_proj, query_gain_terms = rms_rows_back(
        q_heads, g_query, inv_query, rotate_back(grad_q_rot, cos_table, sin_table)
    )
    grad_k_rot = grad_keys_sum.reshape(local_rows, KV, HD)
    grad_k_proj, key_gain_terms = rms_rows_back(
        k_heads, g_key, inv_key, rotate_back(grad_k_rot, cos_table, sin_table)
    )
    grad_q_low = grad_q_proj.reshape(local_rows, q_width).astype(jnp.bfloat16)
    grad_k_low = grad_k_proj.reshape(local_rows, kv_width).astype(jnp.bfloat16)
    grad_v_low = grad_values_sum.astype(jnp.bfloat16)
    grad_h_attn = jnp.einsum(
        "rc,dc->rd", grad_q_low, full_query, preferred_element_type=jnp.float32
    )
    grad_h_attn = grad_h_attn + jnp.einsum(
        "rc,dc->rd", grad_k_low, full_key, preferred_element_type=jnp.float32
    )
    grad_h_attn = grad_h_attn + jnp.einsum(
        "rc,dc->rd", grad_v_low, full_value, preferred_element_type=jnp.float32
    )
    grad_inputs_norm, attn_gain_terms = rms_rows_back(inputs, g_attn, inv_attn, grad_h_attn)
    grad_tokens = (grad_middle + grad_inputs_norm).astype(jnp.bfloat16)[None]
    grad_qkv = jnp.concatenate([grad_q_low, grad_k_low, grad_v_low], axis=1)
    grad_gate_up = jnp.concatenate([grad_gate, grad_up], axis=1)
    input_grads = lax.psum_scatter(
        jnp.concatenate(
            [
                jnp.einsum("rc,rk->ck", h_attn, grad_qkv, preferred_element_type=jnp.float32),
                jnp.einsum("rc,rk->ck", h_ffn, grad_gate_up, preferred_element_type=jnp.float32),
            ],
            axis=1,
        ).astype(jnp.bfloat16),
        CTX_FSDP,
        scatter_dimension=0,
        tiled=True,
    ).astype(jnp.float32)
    left_rows = mixed
    output_grads = lax.psum_scatter(
        jnp.einsum("rc,rk->ck", left_rows, grad_branch, preferred_element_type=jnp.float32).astype(
            jnp.bfloat16
        ),
        CTX_FSDP,
        scatter_dimension=0,
        tiled=True,
    ).astype(jnp.float32)
    left_rows = hidden
    lower_grads = lax.psum_scatter(
        jnp.einsum("rc,rk->ck", left_rows, grad_result, preferred_element_type=jnp.float32).astype(
            jnp.bfloat16
        ),
        CTX_FSDP,
        scatter_dimension=0,
        tiled=True,
    ).astype(jnp.float32)
    input_grads, output_grads, lower_grads = tuple(
        (
            part.astype(jnp.float32)
            for part in packed_total(
                (
                    input_grads.astype(jnp.bfloat16),
                    output_grads.astype(jnp.bfloat16),
                    lower_grads.astype(jnp.bfloat16),
                ),
                "seq",
            )
        )
    )
    edge_two = q_width + kv_width
    edge_three = edge_two + kv_width
    edge_four = edge_three + FF
    grad_w_query = input_grads[:, :q_width]
    grad_w_key = input_grads[:, q_width:edge_two]
    grad_w_value = input_grads[:, edge_two:edge_three]
    grad_w_gate = input_grads[:, edge_three:edge_four]
    grad_w_up = input_grads[:, edge_four:]
    grad_g_attn, grad_g_query, grad_g_key, grad_g_ffn = (
        by_axis(jnp.sum(attn_gain_terms, axis=0), SEQ_CTX_FSDP),
        by_axis(jnp.sum(query_gain_terms, axis=(0, 1)), SEQ_CTX_FSDP),
        by_axis(jnp.sum(key_gain_terms, axis=(0, 1)), SEQ_CTX_FSDP),
        by_axis(jnp.sum(ffn_gain_terms, axis=0), SEQ_CTX_FSDP),
    )
    return (
        output,
        grad_tokens,
        grad_w_query,
        grad_w_key,
        grad_w_value,
        output_grads,
        grad_w_gate,
        grad_w_up,
        lower_grads,
        grad_g_attn,
        grad_g_query,
        grad_g_key,
        grad_g_ffn,
    )


def solution(mesh):
    finer = Mesh(
        mesh.devices.reshape(mesh.shape["seq"], 4, 4, mesh.shape["fsdp"]),
        ("seq", "ctx_0", "ctx_1", "fsdp"),
    )
    return jax.shard_map(
        body,
        mesh=finer,
        in_specs=(
            P(("seq", "fsdp"), CTX, None),
            P(("seq", "fsdp"), None),
            P(CTX_FSDP, None),
            P(CTX_FSDP, None),
            P(CTX_FSDP, None),
            P(CTX_FSDP, None),
            P(CTX_FSDP, None),
            P(CTX_FSDP, None),
            P(CTX_FSDP, None),
            P(),
            P(),
            P(),
            P(),
            P(("seq", "fsdp"), CTX, None),
        ),
        out_specs=(
            P(("seq", "fsdp"), CTX, None),
            P(("seq", "fsdp"), CTX, None),
            P(CTX_FSDP, None),
            P(CTX_FSDP, None),
            P(CTX_FSDP, None),
            P(CTX_FSDP, None),
            P(CTX_FSDP, None),
            P(CTX_FSDP, None),
            P(CTX_FSDP, None),
            P(),
            P(),
            P(),
            P(),
        ),
        check_vma=False,
    )
```

profile of v0, /device:TPU:4, one launch (start us, length us, event | category | flops | bytes accessed | tf_op | source)
XLA Modules:
  0.0 960.3 jit_solution(4656080936940625263)
XLA Ops:
  15.9 46.6 %all-gather.5.cloned.1.call-done = bf16[1024,3072]{1,0:T(8,128)(2,1)} async-done(((bf16[32,3072]{1,0:T(8,128)(2,1)}), bf16[1024,3072]{1,0:T(8,128)(2,1)}) %all-gather.5.cloned.1.call-update) | async-done | bytes 6291472 | tf_op jit(solution)/shard_map/all_gather | solution.py:26
  71.1 3.0 slice_bitcast_fusion
  74.2 4.0 copy.46
  78.2 2.4 multiply_reduce_fusion.3
  82.0 37.2 %all-gather.11.cloned.1.call-done = bf16[4608,1024]{1,0:T(8,128)(2,1)} async-done(((bf16[144,1024]{1,0:T(8,128)(2,1)}), bf16[4608,1024]{1,0:T(8,128)(2,1)}) %all-gather.11.cloned.1.call-update) | async-done | bytes 9437200 | tf_op jit(solution)/shard_map/all_gather | solution.py:192
  119.2 8.6 fusion.95
  127.8 50.1 %all-gather.7.cloned.1.call-done = bf16[2560,1024]{1,0:T(8,128)(2,1)} async-done(((bf16[160,1024]{1,0:T(8,128)(2,1)}), bf16[2560,1024]{1,0:T(8,128)(2,1)}) %all-gather.7.cloned.1.call-update) | async-done | bytes 5242896 | tf_op jit(solution)/shard_map/all_gather | solution.py:26
  177.9 5.2 fusion.114
  183.1 4.4 copy.45
  187.4 4.5 copy.47
  191.9 13.0 %fusion.14 = (f32[8,2,160]{2,1,0:T(2,128)S(1)}, f32[8,2560,160,2]{1,2,3,0:T(8,128)}) fusion(pred[160,2560]{1,0:T(8,128)(4,1)S(1)} %broadcast_compare_fusion.1, bf16[2560,8,64,1]{0,2,3,1:T(8,128)(2,1)} %bitcast.233, bf16[160,8,2,64]{0,3,2,1:T(8,128)(2,1)S(1)} %bitcast.228), kind=kOutput, calls=%fused_computation.23 | convolution fusion | flops 858519040 | bytes 29583360 | tf_op jit(solution)/shard_map/qkgd,nkd->kgqn/dot_general | solution.py:145
  205.0 14.3 %fusion.15 = f32[8,2,160]{2,1,0:T(2,128)S(1)} fusion(f32[8,2560,160,2]{1,2,3,0:T(8,128)} %get-tuple-element.245, f32[8,2,160]{2,1,0:T(2,128)S(1)} %broadcast_maximum_fusion, pred[160,2560]{1,0:T(8,128)(4,1)S(1)} %broadcast_compare_fusion.1), kind=kLoop, calls=%fused_computation.25 | loop fusion | flops 32765440 | bytes 26644480 | tf_op jit(solution)/shard_map/reduce_sum | solution.py:164
  219.3 13.7 %fusion.120 = (bf16[160,8,2,64]{0,3,2,1:T(8,128)(2,1)S(1)}, f32[160,8,2,64]{0,3,2,1:T(8,128)}) fusion(f32[160,8,2]{0,2,1:T(2,128)S(1)} %bitcast.256, bf16[2560,8,64,1]{0,2,3,1:T(8,128)(2,1)S(1)} %bitcast.237, f32[8,2560,160,2]{1,2,3,0:T(8,128)} %get-tuple-element.245, f32[8,2,160]{2,1,0:T(2,128)S(1)} %broadcast_maximum_fusion, ...), kind=kOutput, calls=%fused_computation.185 | convolution fusion | flops 871956480 | bytes 30248960 | tf_op jit(solution)/shard_map/kgqn,nkd->kgqd/dot_general | solution.py:166
  233.0 2.5 multiply_reduce_fusion.6
  236.3 21.4 %all-gather.9.cloned.1.call-done = bf16[1024,9216]{1,0:T(8,128)(2,1)} async-done(((bf16[32,9216]{1,0:T(8,128)(2,1)}), bf16[1024,9216]{1,0:T(8,128)(2,1)}) %all-gather.9.cloned.1.call-update) | async-done | bytes 18874384 | tf_op jit(solution)/shard_map/all_gather | solution.py:26
  257.7 5.5 fusion.22
  263.3 7.6 multiply_convert_fusion.2
  270.8 7.9 fusion.20
  278.8 6.7 multiply_reduce_fusion.4
  285.7 2.7 fusion.53
  288.6 2.0 multiply_reduce_fusion.2
  291.1 204.2 %while.15 = (s32[]{:T(128)}, f32[160,8,2,64]{0,3,2,1:T(8,128)S(1)}, f32[16,160,512]{2,1,0:T(8,128)}, bf16[16,160,512]{2,1,0:T(8,128)(2,1)}, s32[16]{0:T(128)}, /...) while((s32[]{:T(128)}, f32[160,8,2,64]{0,3,2,1:T(8,128)S(1)}, ...), condition=%wide.region_9.10_spmd.clone, body=%wide.region_8.9_spmd.clone.sunk | while | flops 266593280 | bytes 23068576 | solution.py:252
  296.6 2.0 fusion.176
  300.5 2.5 fusion.179
  309.4 2.0 fusion.176
  313.3 2.5 fusion.179
  322.2 2.0 fusion.176
  326.1 2.5 fusion.179
  338.8 2.5 fusion.179
  351.6 2.5 fusion.179
  360.5 2.0 fusion.176
  364.4 2.5 fusion.179
  373.3 2.0 fusion.176
  377.2 2.5 fusion.179
  386.1 2.0 fusion.176
  389.9 2.5 fusion.179
  402.7 2.5 fusion.179
  411.6 2.0 fusion.176
  415.5 2.5 fusion.179
  424.4 2.0 fusion.176
  428.3 2.5 fusion.179
  441.0 2.5 fusion.179
  453.8 2.5 fusion.179
  466.6 2.5 fusion.179
  479.3 2.5 fusion.179
  492.0 2.5 fusion.179
  495.3 3.4 multiply_convert_fusion
  498.8 3.2 pad_maximum_fusion.1
  503.0 3.1 convolution_convert_fusion.3
  506.2 6.2 convolution_convert_fusion.1
  515.6 9.5 convolution_convert_fusion
  525.0 55.9 %reduce-scatter.5.cloned.1.call-done = bf16[160,1024]{1,0:T(8,128)(2,1)} async-done(((bf16[2560,1024]{1,0:T(8,128)(2,1)}), bf16[160,1024]{1,0:T(8,128)(2,1)}) %reduce-scatter.5.cloned.1.call-update) | async-done | bytes 327696 | tf_op jit(solution)/shard_map/reduce_scatter | solution.py:32
  584.8 23.4 %pad_maximum_fusion = bf16[1024,11264]{1,0:T(8,128)(2,1)} fusion(bf16[1024,9216]{1,0:T(8,128)(2,1)} %convolution_convert_fusion, bf16[1024,2048]{1,0:T(8,128)(2,1)S(1)} %convolution_convert_fusion.2), kind=kLoop, calls=%fused_computation.24 | loop fusion | flops 46137344 | bytes 46137344 | tf_op jit(solution)/shard_map/concatenate | solution.py:292
  609.8 6.2 fusion.57
  616.0 46.6 %reduce-scatter.9.cloned.1.call-done = bf16[32,1024]{1,0:T(8,128)(2,1)} async-done(((bf16[1024,1024]{1,0:T(8,128)(2,1)}), bf16[32,1024]{1,0:T(8,128)(2,1)}) %reduce-scatter.9.cloned.1.call-update) | async-done | bytes 65552 | tf_op jit(solution)/shard_map/reduce_scatter | solution.py:304
  663.5 2.6 fusion.71
  666.1 95.2 %reduce-scatter.11.cloned.1.call-done = bf16[144,1024]{1,0:T(8,128)(2,1)} async-done(((bf16[4608,1024]{1,0:T(8,128)(2,1)}), bf16[144,1024]{1,0:T(8,128)(2,1)}) %reduce-scatter.11.cloned.1.call-update) | async-done | bytes 294928 | tf_op jit(solution)/shard_map/reduce_scatter | solution.py:313
  762.3 136.9 %reduce-scatter.7.cloned.1.call-done = bf16[32,11264]{1,0:T(8,128)(2,1)} async-done(((bf16[1024,11264]{1,0:T(8,128)(2,1)}), bf16[32,11264]{1,0:T(8,128)(2,1)}) %reduce-scatter.7.cloned.1.call-update) | async-done | bytes 720912 | tf_op jit(solution)/shard_map/reduce_scatter | solution.py:291
  903.2 2.8 fusion.87
  906.1 8.9 all-reduce.2
  914.9 10.3 %all-reduce.1 = (f32[1024]{0:T(1024)S(1)}, f32[64]{0:T(128)S(1)}, f32[64]{0:T(128)S(1)}, f32[1024]{0:T(1024)S(1)}) all-reduce(f32[1024]{0:T(1024)S(1)} %get-tuple-element.195, f32[64]{0:T(128)S(1)} %get-tuple-element.196, f32[64]{0:T(128)S(1)} %get-tuple-element.197, ...), channel_id=1, replica_groups=mesh['seq'=4,'ctx_0'=4,'ctx_1'=4,'fsdp'=2] {'ctx_0'}, use_global_device_ids=true, to_apply=%region_20.21 | all-reduce | flops 2176 | bytes 17408 | tf_op jit(solution)/shard_map/psum | solution.py:48
  925.2 8.8 all-reduce
  934.1 3.1 all-reduce.3
  938.2 8.1 all-reduce.6.cloned.1.call-done
  (554 shorter events, 179.2 us)
Async XLA Ops:
  7.2 57.2 %copy-start.7 = (bf16[1,160,1024]{2,1,0:T(8,128)(2,1)S(1)}, bf16[1,160,1024]{2,1,0:T(8,128)(2,1)}, u32[]{:S(2)}) copy-start(bf16[1,160,1024]{2,1,0:T(8,128)(2,1)} %param.16) | copy-start | bytes 983044
  7.2 57.2 %copy-start.35 = (f32[1024]{0:T(1024)S(1)}, f32[1024]{0:T(1024)}, u32[]{:S(2)}) copy-start(f32[1024]{0:T(1024)} %param.25) | copy-start | bytes 12292
  7.2 55.3 %all-gather.5.cloned.1.call-start = ((), (), s32[]{:S(2)}) async-start(), calls=%async_computation.4 | async-start | bytes 6488064 | tf_op jit(solution)/shard_map/all_gather | solution.py:26
  8.9 110.3 %all-gather.11.cloned.1.call-start = ((), (), s32[]{:S(2)}) async-start(), calls=%async_computation.7 | async-start | bytes 9732096 | tf_op jit(solution)/shard_map/all_gather | solution.py:192
  9.7 168.2 %all-gather.7.cloned.1.call-start = ((), (), s32[]{:S(2)}) async-start(), calls=%async_computation.5 | async-start | bytes 5570560 | tf_op jit(solution)/shard_map/all_gather | solution.py:26
  15.9 62.3 %copy-start.39 = (f32[160]{0:T(256)}, f32[160]{0:T(256)S(1)}, u32[]{:S(2)}) copy-start(f32[160]{0:T(256)S(1)} %get-tuple-element.237) | copy-start | bytes 1924
  15.9 49.7 %copy-start.46 = (f32[64]{0:T(128)S(1)}, f32[64]{0:T(128)}, u32[]{:S(2)}) copy-start(f32[64]{0:T(128)} %param.27) | copy-start | bytes 772
  68.6 189.1 %all-gather.9.cloned.1.call-start = ((), (), s32[]{:S(2)}) async-start(), calls=%async_computation.6 | async-start | bytes 19464192 | tf_op jit(solution)/shard_map/all_gather | solution.py:26
  69.5 511.4 %reduce-scatter.5.cloned.1.call-start = ((), (), s32[]{:S(2)}) async-start(), calls=%async_computation.8 | async-start | bytes 5570560 | tf_op jit(solution)/shard_map/reduce_scatter | solution.py:32
  205.0 14.3 %copy-start.14 = (bf16[2560,512]{0,1:T(8,128)(2,1)S(1)}, bf16[2560,512]{0,1:T(8,128)(2,1)}, u32[]{:S(2)}) copy-start(bf16[2560,512]{0,1:T(8,128)(2,1)} %copy.47) | copy-start | bytes 7864324
  235.5 50.0 %copy-start.3 = (f32[160,1024]{1,0:T(8,128)}, f32[160,1024]{1,0:T(8,128)S(1)}, u32[]{:S(2)}) copy-start(f32[160,1024]{1,0:T(8,128)S(1)} %get-tuple-element.249) | copy-start | bytes 1966084
  236.3 26.9 %copy-start.25 = (bf16[160,1024]{1,0:T(8,128)(2,1)}, bf16[160,1024]{1,0:T(8,128)(2,1)S(1)}, u32[]{:S(2)}) copy-start(bf16[160,1024]{1,0:T(8,128)(2,1)S(1)} %multiply_convert_fusion.4) | copy-start | bytes 983044
  257.7 5.5 copy-start.15
  270.8 7.9 copy-start.23
  270.8 8.0 copy-start.21
  278.8 6.7 copy-start.16
  285.7 5.4 copy-start.11
  293.0 3.6 copy-start.41
  293.0 3.6 copy-start.43
  299.8 4.1 copy-start.20
  305.8 3.6 copy-start.41
  305.8 3.6 copy-start.43
  312.5 4.1 copy-start.20
  325.3 4.1 copy-start.20
  331.3 3.6 copy-start.41
  331.3 3.6 copy-start.43
  338.1 4.1 copy-start.20
  344.1 3.6 copy-start.41
  344.1 3.6 copy-start.43
  350.8 4.1 copy-start.20
  356.8 3.6 copy-start.41
  356.8 3.6 copy-start.43
  363.6 4.1 copy-start.20
  376.4 4.1 copy-start.20
  382.4 3.6 copy-start.41
  382.4 3.6 copy-start.43
  389.2 4.1 copy-start.20
  395.2 3.6 copy-start.41
  395.2 3.6 copy-start.43
  402.0 4.1 copy-start.20
  414.7 4.1 copy-start.20
  427.5 4.1 copy-start.20
  433.5 3.6 copy-start.41
  433.5 3.6 copy-start.43
  440.3 4.1 copy-start.20
  446.3 3.6 copy-start.41
  446.3 3.6 copy-start.43
  453.1 4.1 copy-start.20
  465.8 4.1 copy-start.20
  478.6 4.1 copy-start.20
  491.2 4.1 copy-start.20
  502.0 4.2 copy-start.5
  502.0 160.7 %reduce-scatter.9.cloned.1.call-start = ((), (), s32[]{:S(2)}) async-start(), calls=%async_computation.10 | async-start | bytes 2162688 | tf_op jit(solution)/shard_map/reduce_scatter | solution.py:304
  506.1 255.1 %reduce-scatter.11.cloned.1.call-start = ((), (), s32[]{:S(2)}) async-start(), calls=%async_computation.11 | async-start | bytes 9732096 | tf_op jit(solution)/shard_map/reduce_scatter | solution.py:313
  512.5 386.7 %reduce-scatter.7.cloned.1.call-start = ((), (), s32[]{:S(2)}) async-start(), calls=%async_computation.9 | async-start | bytes 23789568 | tf_op jit(solution)/shard_map/reduce_scatter | solution.py:291
  525.0 57.5 %copy-start.10 = (f32[160,8,64]{0,2,1:T(8,128)S(1)}, f32[160,8,64]{0,2,1:T(8,128)}, u32[]{:S(2)}) copy-start(f32[160,8,64]{0,2,1:T(8,128)} %copy-done.9) | copy-start | bytes 983044
  525.0 57.5 %copy-start.34 = (f32[160,8]{0,1:T(8,128)S(1)}, f32[160,8]{0,1:T(8,128)}, u32[]{:S(2)}) copy-start(f32[160,8]{0,1:T(8,128)} %copy-done.33) | copy-start | bytes 15364
  525.0 57.5 %copy-start.47 = (f32[64]{0:T(128)S(1)}, f32[64]{0:T(128)}, u32[]{:S(2)}) copy-start(f32[64]{0:T(128)} %param.27) | copy-start | bytes 772
  608.2 338.1 %all-reduce.6.cloned.1.call-start = ((), (), s32[]{:S(2)}) async-start(), calls=%async_computation.12 | async-start | bytes 2162688 | tf_op jit(solution)/shard_map/psum | solution.py:43
  666.1 235.4 %copy-start.28 = (bf16[160,1024]{1,0:T(8,128)(2,1)S(1)}, bf16[160,1024]{1,0:T(8,128)(2,1)}, u32[]{:S(2)}) copy-start(bf16[160,1024]{1,0:T(8,128)(2,1)} %reduce-scatter.5.cloned.1.call-done) | copy-start | bytes 983044
  901.5 4.6 copy-start.49
  901.5 4.6 copy-start.50
  903.2 34.0 %copy-start.13 = (f32[160,1024]{1,0:T(8,128)S(1)}, f32[160,1024]{1,0:T(8,128)}, u32[]{:S(2)}) copy-start(f32[160,1024]{1,0:T(8,128)} %copy-done.11) | copy-start | bytes 1966084
  903.2 34.0 %copy-start.48 = (f32[160]{0:T(256)S(1)}, f32[160]{0:T(256)}, u32[]{:S(2)}) copy-start(f32[160]{0:T(256)} %get-tuple-element.236) | copy-start | bytes 1924
  (86 other events, 179.0 us)
Sparse Core Ops, SparseCore 0:
  10.9 51.6 all-gather.4
  64.8 54.3 all-gather.10
  121.9 55.9 all-gather.6
  180.6 77.0 all-gather.8
  502.1 78.8 reduce-scatter.4
  584.3 78.2 reduce-scatter.8
  666.4 94.8 reduce-scatter.10
  765.8 133.3 reduce-scatter.6
  901.6 44.6 all-reduce.5
where the time goes:
time: 967 us; the launch traced here: 960 us
  waiting for transfers between devices  499 us (52%)
  matrix products  203 us (21%)
  local copies, waits for them, and re-layouts  119 us (12%)
  other arithmetic  80.1 us (8%)
  blocking collectives  31.1 us (3%)
  between operations  14.9 us (2%)
  loops' own time  12.4 us (1%)
    reduce_scatter x1, waiting for transfers between devices, body(): lax.psum_scatter(jnp.concatenate([jnp.einsum('rc,rk->ck', h_attn, grad_qk...  137 us
    all_gather x3, waiting for transfers between devices, side_by_side(): whole = lax.all_gather(both, axis, axis=dim, tiled=True)  118 us
    reduce_scatter x1, waiting for transfers between devices, body(): lax.psum_scatter(jnp.einsum('rc,rk->ck', left_rows, grad_result, preferre...  95.2 us
    reduce_scatter x1, waiting for transfers between devices, in_one_piece(): lax.psum_scatter(both, axis, scatter_dimension=dim, tiled=True)  55.9 us
    reduce_scatter x1, waiting for transfers between devices, body(): lax.psum_scatter(jnp.einsum('rc,rk->ck', left_rows, grad_branch, preferre...  46.6 us
    dot_general x16, matrix products, backward_step(): jnp.einsum('kgqn,qkgd->nkd', probs.astype(jnp.bfloat16), grad_heads, pref...  40.8 us
    all_gather x1, waiting for transfers between devices, body(): lax.all_gather(w_down, CTX_FSDP, axis=0, tiled=True)  37.2 us
    dot_general x16, matrix products, backward_step(): jnp.einsum('qkgd,nkd->kgqn', grad_heads, value_heads, preferred_element_t...  31.5 us
  transfers between devices with their start and end apart: 9, of which 9 were waited for; matrix products, arithmetic and copies ran while one was open for 16% of the time, Pallas kernels for 0%

commit v1 on v0

v1 whole, which is shorter than its diff:
```python
import functools

import jax
import jax.numpy as jnp
import numpy as np
from jax import lax
from jax.experimental import pallas as pl
from jax.experimental.pallas import tpu as pltpu
from jax.sharding import Mesh
from jax.sharding import PartitionSpec as P

D = 1024
H = 16
KV = 8
HD = 64
FF = 4608
LEN = 2560
BLK = 80
ROWS = 2 * BLK
NX = 4
FX = FF // NX
QX = H * HD // NX
KX = KV * HD // NX
TILE = 512
N_TILES = LEN // TILE
CTX = ("ctx_0", "ctx_1")
CTX_FSDP = ("ctx_0", "ctx_1", "fsdp")
SEQ_CTX_FSDP = ("seq", "ctx_0", "ctx_1", "fsdp")
EPSILON = 1e-05
ROPE_BASE = 1000000.0
MESH = pl.DeviceIdType.MESH
BF16 = jnp.bfloat16
F32 = jnp.float32
VMEM_BYTES = 56 * 1024 * 1024


SIZE = {"x": 4, "c": 16, "p": 32, "t": 16, "r": 16, "d": 4}


def coords():
    return tuple(lax.axis_index(a) for a in SEQ_CTX_FSDP)


def target(group, t):
    s, z, y, c = coords()
    if group == "x":
        return (t, z, y, c), s
    if group == "c":
        return (s, t // 4, lax.rem(t, 4), c), z * 4 + y
    if group == "p":
        return (s, t // 8, lax.rem(t // 2, 4), lax.rem(t, 2)), (z * 4 + y) * 2 + c
    if group == "t":
        return (z, t // 4, lax.rem(t, 4), c), s * 4 + y
    if group == "d":
        return (t, s, y, c), z
    return (t // 4, s, lax.rem(t, 4), c), z * 4 + y


def source(group, t):
    s, z, y, c = coords()
    if group == "t":
        return (t // 4, s, lax.rem(t, 4), c)
    if group == "r":
        return (z, t // 4, lax.rem(t, 4), c)
    if group == "d":
        return (z, t, y, c)
    return target(group, t)[0]


def own(group):
    s, z, y, c = coords()
    if group == "t":
        return s == z, z * 4 + y, s * 4 + y
    if group == "r":
        return s == z, s * 4 + y, z * 4 + y
    if group == "d":
        return s == z, s, z
    me = target(group, 0)[1]
    return None, me, me


def exchange_kernel(items, *refs):
    n = len(items)
    srcs, outs, sems = refs[:n], refs[n : 2 * n], refs[2 * n :]
    barrier = pltpu.get_barrier_semaphore()
    expected = 0
    starts = []
    for i, (g, _) in enumerate(items):
        has_own, sent, _ = own(g)
        size = SIZE[g]
        if has_own is None:
            starts.append((jnp.int32(1), sent))
            expected = expected + size - 1
        else:
            starts.append((has_own.astype(jnp.int32), sent))
            expected = expected + size - has_own.astype(jnp.int32)
        place = own(g)[2]
        first = starts[i][0]

        def greet(k, carry, g=g, size=size, place=place):
            dev = source(g, lax.rem(place + k, size))
            pl.semaphore_signal(barrier, inc=1, device_id=dev, device_id_type=MESH)
            return carry

        lax.fori_loop(first, size, greet, 0)

    def own_copy(i):
        g, mode = items[i]
        _, sent, place = own(g)
        src = srcs[i] if mode == "ag" else srcs[i].at[sent]
        return pltpu.make_async_copy(src, outs[i].at[place], sems[3 * i + 2])

    for i, (g, _) in enumerate(items):
        if own(g)[0] is None:
            own_copy(i).start()
        else:
            pl.when(own(g)[0])(lambda i=i: own_copy(i).start())
    pl.semaphore_wait(barrier, expected)

    def remote(i, t, place):
        g, mode = items[i]
        dev, there = target(g, t)
        src = srcs[i] if mode == "ag" else srcs[i].at[t]
        return pltpu.make_async_remote_copy(
            src_ref=src,
            dst_ref=outs[i].at[there if place is None else place],
            send_sem=sems[3 * i].at[t],
            recv_sem=sems[3 * i + 1].at[there if place is None else place],
            device_id=dev,
            device_id_type=MESH,
        )

    for i, (g, _) in enumerate(items):
        first, sent = starts[i]

        def send(k, carry, i=i, g=g, sent=sent):
            remote(i, lax.rem(sent + k, SIZE[g]), None).start()
            return carry

        lax.fori_loop(first, SIZE[g], send, 0)
    for i, (g, _) in enumerate(items):
        first, sent = starts[i]
        place = own(g)[2]

        def drain(k, carry, i=i, g=g, sent=sent, place=place):
            remote(i, lax.rem(sent + k, SIZE[g]), None).wait_send()
            remote(i, lax.rem(sent + k, SIZE[g]), lax.rem(place + k, SIZE[g])).wait_recv()
            return carry

        lax.fori_loop(first, SIZE[g], drain, 0)
        if own(g)[0] is None:
            own_copy(i).wait()
        else:
            pl.when(own(g)[0])(lambda i=i: own_copy(i).wait())


def exchange(number, name, *parts):
    items = tuple((g, m) for g, m, _ in parts)
    arrays = [a for _, _, a in parts]
    outs = [
        jax.ShapeDtypeStruct((SIZE[g],) + (a.shape if m == "ag" else a.shape[1:]), a.dtype)
        for g, m, a in parts
    ]
    scratch = []
    for g, _ in items:
        scratch += [
            pltpu.SemaphoreType.DMA((SIZE[g],)),
            pltpu.SemaphoreType.DMA((SIZE[g],)),
            pltpu.SemaphoreType.DMA,
        ]
    return pl.pallas_call(
        functools.partial(exchange_kernel, items),
        out_shape=outs,
        in_specs=[pl.BlockSpec(memory_space=pl.ANY)] * len(arrays),
        out_specs=[pl.BlockSpec(memory_space=pl.ANY)] * len(arrays),
        scratch_shapes=scratch,
        compiler_params=pltpu.CompilerParams(collective_id=number, has_side_effects=True),
        name=name,
    )(*arrays)


def lanes(shape):
    return lax.broadcasted_iota(jnp.int32, shape, len(shape) - 1)


def low_half(shape):
    return lanes(shape) < HD


def swap(v):
    return pltpu.roll(v, HD, 1)


def swap_halves(v):
    first = lax.rem(lanes(v.shape), HD) < HD // 2
    return jnp.where(first, pltpu.roll(v, 2 * HD - HD // 2, 1), pltpu.roll(v, HD // 2, 1))


def head_mean(v):
    m = low_half(v.shape)
    a = jnp.sum(jnp.where(m, v, 0.0), axis=-1, keepdims=True)
    b = jnp.sum(jnp.where(m, 0.0, v), axis=-1, keepdims=True)
    return jnp.where(m, a, b) * (1.0 / HD)


def nt(a, b):
    return lax.dot_general(a, b, (((1,), (1,)), ((), ())), preferred_element_type=F32)


def nn(a, b):
    return lax.dot_general(a, b, (((1,), (0,)), ((), ())), preferred_element_type=F32)


def tn(a, b):
    return lax.dot_general(a, b, (((0,), (0,)), ((), ())), preferred_element_type=F32)


def rows_of(block):
    return pl.ds(pl.multiple_of(block * BLK, 16), BLK)


def rope_rows(blocks, table, s):
    return jnp.concatenate([table[rows_of(blocks[2 * s]), :], table[rows_of(blocks[2 * s + 1]), :]], 0)


def project_kernel(blocks, h, w, cos_t, sin_t, g_q, g_k, send, raw, acc):
    acc[...] = nn(h[...], w[...])
    m = low_half((ROWS, 2 * HD))
    mh = low_half((BLK, 2 * HD))
    for s in range(NX):
        at = slice(s * ROWS, (s + 1) * ROWS)
        cos_r, sin_r = rope_rows(blocks, cos_t, s), rope_rows(blocks, sin_t, s)
        raw[at, :] = acc[at, : QX + KX]
        turned = []
        for p in range(3):
            v = acc[at, p * 128 : (p + 1) * 128]
            gain = g_q[...] if p < 2 else g_k[...]
            normed = v * lax.rsqrt(head_mean(v * v) + EPSILON) * gain
            turned.append(normed * cos_r + swap_halves(normed) * sin_r)
        keys = turned[2]
        swapped_keys = swap(keys)
        values = acc[at, 3 * 128 :]
        top, bottom = values[:BLK], values[BLK:]
        packed = (jnp.where(mh, top, swap(bottom)), jnp.where(mh, swap(top), bottom))
        for hh in range(4):
            q = turned[hh // 2]
            q = q if hh % 2 == 0 else swap(q)
            k = swapped_keys if hh < 2 else keys
            send[s * 4 + hh, :ROWS, :] = jnp.where(m, q, k).astype(BF16)
            send[s * 4 + hh, ROWS:, :] = packed[hh // 2].astype(BF16)


def project(blocks, h, w, cos_t, sin_t, g_q, g_k):
    return pl.pallas_call(
        project_kernel,
        grid_spec=pltpu.PrefetchScalarGridSpec(
            num_scalar_prefetch=1,
            in_specs=[pl.BlockSpec(memory_space=pltpu.VMEM)] * 6,
            out_specs=[pl.BlockSpec(memory_space=pltpu.VMEM)] * 2,
            scratch_shapes=[pltpu.VMEM((NX * ROWS, QX + 2 * KX), F32)],
        ),
        out_shape=[
            jax.ShapeDtypeStruct((16, ROWS + BLK, 2 * HD), BF16),
            jax.ShapeDtypeStruct((NX * ROWS, QX + KX), F32),
        ],
        compiler_params=pltpu.CompilerParams(vmem_limit_bytes=VMEM_BYTES),
        name="project",
    )(blocks, h, w, cos_t, sin_t, g_q, g_k)


def attend_kernel(pair, recv, out, q_s, k_s, v_s, o_t, inv, o_s, v_t):
    m = low_half((BLK, 2 * HD))
    for j in range(16):
        packed = recv[j, ROWS:, :].astype(F32)
        for half in range(2):
            block = pair[j] if half == 0 else 31 - pair[j]
            both = recv[j, half * BLK : (half + 1) * BLK, :].astype(F32)
            vals = packed if half == 0 else swap(packed)
            q_s[rows_of(block), :] = jnp.where(m, both * HD**-0.5, 0.0).astype(BF16)
            k_s[rows_of(block), :] = jnp.where(m, swap(both), 0.0).astype(BF16)
            v_s[rows_of(block), :] = jnp.where(m, vals, 0.0).astype(BF16)
    for t in range(N_TILES):
        at = slice(t * TILE, (t + 1) * TILE)
        v_t[:, at] = v_s[at, :].T[:HD]
    causal = lax.broadcasted_iota(jnp.int32, (TILE, TILE), 0) <= lanes((TILE, TILE))
    for i in range(N_TILES):
        at = slice(i * TILE, (i + 1) * TILE)
        q = q_s[at, :]

        e = jnp.where(causal, jnp.exp(nt(k_s[at, :], q)), 0.0)
        first = (jnp.sum(e, axis=0, keepdims=True), nn(v_t[:, at], e.astype(BF16)))

        def step(t, carry, q=q):
            total, acc = carry
            there = pl.ds(pl.multiple_of(t * TILE, TILE), TILE)
            e = jnp.exp(nt(k_s[there, :], q))
            total = total + jnp.sum(e, axis=0, keepdims=True)
            return total, acc + nn(v_t[:, there], e.astype(BF16))

        total, acc = lax.fori_loop(0, i, step, first) if i else first
        over = 1.0 / total
        attended = acc * over
        o_t[:, at] = attended
        inv[:, at] = jnp.broadcast_to(over, (8, TILE))
        o_s[at, :] = jnp.concatenate([attended, jnp.zeros_like(attended)], 0).T
    for j in range(16):
        low_rows = o_s[rows_of(pair[j]), :]
        high_rows = o_s[rows_of(31 - pair[j]), :]
        out[j, :, :] = (low_rows + swap(high_rows)).astype(BF16)


def attend(pair, recv):
    wide = jax.ShapeDtypeStruct((LEN, 2 * HD), BF16)
    return pl.pallas_call(
        attend_kernel,
        grid_spec=pltpu.PrefetchScalarGridSpec(
            num_scalar_prefetch=1,
            in_specs=[pl.BlockSpec(memory_space=pltpu.VMEM)],
            out_specs=[pl.BlockSpec(memory_space=pltpu.VMEM)] * 6,
            scratch_shapes=[pltpu.VMEM((LEN, 2 * HD), F32), pltpu.VMEM((HD, LEN), BF16)],
        ),
        out_shape=[
            jax.ShapeDtypeStruct((16, BLK, 2 * HD), BF16),
            wide,
            wide,
            wide,
            jax.ShapeDtypeStruct((HD, LEN), F32),
            jax.ShapeDtypeStruct((8, LEN), F32),
        ],
        compiler_params=pltpu.CompilerParams(vmem_limit_bytes=VMEM_BYTES),
        name="attend",
    )(pair, recv)


def attend_back_kernel(pair, recv, q_s, k_s, v_s, o_t, inv, out, g_s, k_t, delta, dq_t, dk_s, dv_s):
    m = low_half((BLK, 2 * HD))
    for j in range(16):
        packed = recv[j, :, :].astype(F32)
        g_s[rows_of(pair[j]), :] = jnp.where(m, packed, 0.0).astype(BF16)
        g_s[rows_of(31 - pair[j]), :] = jnp.where(m, swap(packed), 0.0).astype(BF16)
    for t in range(N_TILES):
        at = slice(t * TILE, (t + 1) * TILE)
        k_t[:, at] = k_s[at, :].T[:HD]
        g_t = g_s[at, :].astype(F32).T[:HD]
        row = jnp.sum(g_t * o_t[:, at], axis=0, keepdims=True)
        delta[:, at] = jnp.broadcast_to(row, (8, TILE))
    dq_t[...] = jnp.zeros_like(dq_t)
    causal = lax.broadcasted_iota(jnp.int32, (TILE, TILE), 0) <= lanes((TILE, TILE))
    for i in range(N_TILES):
        at = slice(i * TILE, (i + 1) * TILE)
        k, v, kt = k_s[at, :], v_s[at, :], k_t[:, at]

        def pair_of_tiles(there, masked, k=k, v=v, kt=kt):
            q, g = q_s[there, :], g_s[there, :]
            e = jnp.exp(nt(k, q))
            if masked:
                e = jnp.where(causal, e, 0.0)
            probs = e * inv[0:1, there]
            ds = (probs * (nt(v, g) - delta[0:1, there])).astype(BF16)
            dq_t[:, there] = dq_t[:, there] + nn(kt, ds)
            return nn(ds, q), nn(probs.astype(BF16), g)

        first = pair_of_tiles(at, True)

        def step(t, carry, pair_of_tiles=pair_of_tiles):
            dk, dv = pair_of_tiles(pl.ds(pl.multiple_of(t * TILE, TILE), TILE), False)
            return carry[0] + dk, carry[1] + dv

        dk, dv = lax.fori_loop(i + 1, N_TILES, step, first) if i + 1 < N_TILES else first
        dk_s[at, :] = dk
        dv_s[at, :] = dv
    for i in range(N_TILES):
        at = slice(i * TILE, (i + 1) * TILE)
        dq = dq_t[:, at] * HD**-0.5
        dk_s[at, :] = jnp.concatenate([dq, jnp.zeros_like(dq)], 0).T + swap(dk_s[at, :])
    for j in range(16):
        for half in range(2):
            block = pair[j] if half == 0 else 31 - pair[j]
            out[j, half * BLK : (half + 1) * BLK, :] = dk_s[rows_of(block), :].astype(BF16)
        out[j, ROWS:, :] = (dv_s[rows_of(pair[j]), :] + swap(dv_s[rows_of(31 - pair[j]), :])).astype(BF16)


def attend_back(pair, recv, q_s, k_s, v_s, o_t, inv):
    return pl.pallas_call(
        attend_back_kernel,
        grid_spec=pltpu.PrefetchScalarGridSpec(
            num_scalar_prefetch=1,
            in_specs=[pl.BlockSpec(memory_space=pltpu.VMEM)] * 6,
            out_specs=pl.BlockSpec(memory_space=pltpu.VMEM),
            scratch_shapes=[
                pltpu.VMEM((LEN, 2 * HD), BF16),
                pltpu.VMEM((HD, LEN), BF16),
                pltpu.VMEM((8, LEN), F32),
                pltpu.VMEM((HD, LEN), F32),
                pltpu.VMEM((LEN, 2 * HD), F32),
                pltpu.VMEM((LEN, 2 * HD), F32),
            ],
        ),
        out_shape=jax.ShapeDtypeStruct((16, ROWS + BLK, 2 * HD), BF16),
        compiler_params=pltpu.CompilerParams(vmem_limit_bytes=VMEM_BYTES),
        name="attend_back",
    )(pair, recv, q_s, k_s, v_s, o_t, inv)


def project_back_kernel(blocks, recv, raw, h, w, cos_t, sin_t, g_q, g_k, gh, dw, gains, low):
    m = low_half((ROWS, 2 * HD))
    mh = low_half((BLK, 2 * HD))
    gq_sum = jnp.zeros((1, 2 * HD), F32)
    gk_sum = jnp.zeros((1, 2 * HD), F32)
    for s in range(NX):
        at = slice(s * ROWS, (s + 1) * ROWS)
        cos_r, sin_r = rope_rows(blocks, cos_t, s), rope_rows(blocks, sin_t, s)
        part = [recv[s * 4 + hh, :ROWS, :].astype(F32) for hh in range(4)]
        vals = [recv[s * 4 + hh, ROWS:, :].astype(F32) for hh in range(4)]
        grads = [
            jnp.where(m, part[0], swap(part[1])),
            jnp.where(m, part[2], swap(part[3])),
            jnp.where(m, swap(part[0] + part[1]), part[2] + part[3]),
        ]
        for p in range(3):
            turned = grads[p] * cos_r + swap_halves(grads[p] * sin_r)
            v = raw[at, p * 128 : (p + 1) * 128]
            gain = g_q[...] if p < 2 else g_k[...]
            r = lax.rsqrt(head_mean(v * v) + EPSILON)
            weighted = turned * gain
            grad = r * weighted - v * (r * r * r) * head_mean(weighted * v)
            low[at, p * 128 : (p + 1) * 128] = grad.astype(BF16)
            term = jnp.sum(turned * v * r, axis=0, keepdims=True)
            if p < 2:
                gq_sum = gq_sum + term
            else:
                gk_sum = gk_sum + term
        a, b = vals[0] + vals[1], vals[2] + vals[3]
        grad_v = jnp.concatenate([jnp.where(mh, a, swap(b)), jnp.where(mh, swap(a), b)], 0)
        low[at, 3 * 128 :] = grad_v.astype(BF16)
    gains[...] = jnp.concatenate([gq_sum, gk_sum, jnp.zeros((6, 2 * HD), F32)], 0)
    gh[...] = nt(low[...], w[...]).astype(BF16)
    dw[...] = tn(h[...], low[...]).astype(BF16)


def project_back(blocks, recv, raw, h, w, cos_t, sin_t, g_q, g_k):
    return pl.pallas_call(
        project_back_kernel,
        grid_spec=pltpu.PrefetchScalarGridSpec(
            num_scalar_prefetch=1,
            in_specs=[pl.BlockSpec(memory_space=pltpu.VMEM)] * 8,
            out_specs=[pl.BlockSpec(memory_space=pltpu.VMEM)] * 3,
            scratch_shapes=[pltpu.VMEM((NX * ROWS, QX + 2 * KX), BF16)],
        ),
        out_shape=[
            jax.ShapeDtypeStruct((NX * ROWS, D), BF16),
            jax.ShapeDtypeStruct((D, QX + 2 * KX), BF16),
            jax.ShapeDtypeStruct((8, 2 * HD), F32),
        ],
        compiler_params=pltpu.CompilerParams(vmem_limit_bytes=VMEM_BYTES),
        name="project_back",
    )(blocks, recv, raw, h, w, cos_t, sin_t, g_q, g_k)


def angle_constants():
    frequencies = ROPE_BASE ** (-np.arange(0, HD // 2, dtype=np.float64) * 2.0 / HD)
    phases = np.arange(LEN, dtype=np.float64)[:, None] * frequencies[None, :]
    cos, sin = np.cos(phases).astype(np.float32), np.sin(phases).astype(np.float32)
    return np.concatenate([cos] * 4, 1), np.concatenate([-sin, sin, -sin, sin], 1)


def rms_rows(values_in, gain):
    inv_rms = lax.rsqrt(jnp.mean(values_in * values_in, axis=-1, keepdims=True) + EPSILON)
    return (values_in * inv_rms * gain, inv_rms)


def rms_rows_back(values_in, gain, inv_rms, grad_in):
    weighted = grad_in * gain
    inner = jnp.mean(weighted * values_in, axis=-1, keepdims=True)
    grad_values = inv_rms * weighted - values_in * (inv_rms * inv_rms * inv_rms) * inner
    gain_terms = grad_in * values_in * inv_rms
    return (grad_values, gain_terms)


def columns_of(w, x, width):
    return lax.dynamic_slice_in_dim(w, x * width, width, axis=1)


def body(
    tokens,
    pairs,
    w_query,
    w_key,
    w_value,
    w_out,
    w_gate,
    w_up,
    w_down,
    g_attn,
    g_query,
    g_key,
    g_ffn,
    cotangent,
):
    x, z, y, c = coords()
    ctx = z * 4 + y
    cos_np, sin_np = angle_constants()
    cos_t, sin_t = jnp.asarray(cos_np), jnp.asarray(sin_np)
    gq2 = jnp.concatenate([g_query, g_query])[None]
    gk2 = jnp.concatenate([g_key, g_key])[None]

    mine = jnp.concatenate([columns_of(w_gate, x, FX), columns_of(w_up, x, FX), w_out], axis=1)
    wide = lax.all_gather(mine, CTX_FSDP, axis=0, tiled=True)
    w_gu, full_out = wide[:, : 2 * FX], wide[:, 2 * FX :]
    swap_xz = [(a * 4 + b, b * 4 + a) for a in range(4) for b in range(4)]
    down_part = lax.ppermute(columns_of(w_down, x, D // 4), ("seq", "ctx_0"), swap_xz)
    w_dn = lax.all_gather(down_part, CTX_FSDP, axis=0, tiled=True).reshape(4, FX, D // 4)

    inputs = tokens[0].astype(F32)
    normed_attn, inv_attn = rms_rows(inputs, g_attn)
    h_attn = normed_attn.astype(BF16)
    w_x = jnp.concatenate(
        [columns_of(w_query, x, QX), columns_of(w_key, x, KX), columns_of(w_value, x, KX)], axis=1
    )
    pairs_pad = jnp.pad(pairs, ((0, 7), (0, 112)))
    h_all, w_qkv, pairs_all = exchange(
        1, "gather_in", ("x", "ag", h_attn), ("p", "ag", w_x), ("x", "ag", pairs_pad)
    )
    h_all = h_all.reshape(NX * ROWS, D)
    w_qkv = w_qkv.reshape(D, QX + 2 * KX)
    pairs_all = pairs_all[:, 0, :16]
    first = lax.dynamic_slice_in_dim(pairs_all, ctx, 1, axis=1)[:, 0]
    blocks = jnp.stack([first, 31 - first], axis=1).reshape(8)
    pair = lax.dynamic_slice_in_dim(pairs_all, z, 1, axis=0)[0]

    send, raw = project(blocks, h_all, w_qkv, cos_t, sin_t, gq2, gk2)
    recv, cot_all = exchange(2, "to_heads", ("c", "a2a", send), ("x", "ag", cotangent[0]))
    heads_out, q_s, k_s, v_s, o_t, inv = attend(pair, recv)
    (mixed_parts,) = exchange(3, "to_tokens", ("t", "a2a", heads_out))
    mixed = mixed_parts.reshape(16, BLK, 2, HD).transpose(2, 1, 0, 3).reshape(ROWS, D)
    branch = jnp.dot(mixed, full_out, preferred_element_type=F32)
    middle = inputs + branch
    normed_ffn, inv_ffn = rms_rows(middle, g_ffn)
    (h4,) = exchange(4, "gather_ffn", ("x", "ag", normed_ffn.astype(BF16)))
    h4 = h4.reshape(NX * ROWS, D)
    cot4 = cot_all.reshape(NX * ROWS, D)

    gate_up = jnp.dot(h4, w_gu, preferred_element_type=F32)
    gate_act, up_act = gate_up[:, :FX], gate_up[:, FX:]
    sigmoid_gate = jax.nn.sigmoid(gate_act)
    silu_gate = gate_act * sigmoid_gate
    hidden = (silu_gate * up_act).astype(BF16)
    grad_hidden = sum(
        jnp.einsum(
            "rd,fd->rf", cot4[:, q * 256 : (q + 1) * 256], w_dn[q], preferred_element_type=F32
        )
        for q in range(4)
    )
    grad_gate = (
        grad_hidden * up_act * (sigmoid_gate * (1.0 + gate_act * (1.0 - sigmoid_gate)))
    ).astype(BF16)
    grad_up = (grad_hidden * silu_gate).astype(BF16)
    grad_gu = jnp.concatenate([grad_gate, grad_up], axis=1)
    grad_h4 = jnp.einsum("rf,df->rd", grad_gu, w_gu, preferred_element_type=F32).astype(BF16)
    (grad_h_parts,) = exchange(5, "sum_ffn", ("x", "a2a", grad_h4.reshape(NX, ROWS, D)))
    result4 = jnp.concatenate(
        [jnp.dot(hidden, w_dn[q], preferred_element_type=F32) for q in range(4)], axis=1
    ).astype(BF16)

    grad_h_ffn = jnp.sum(grad_h_parts.astype(F32), axis=0)
    grad_out = cotangent[0].astype(F32)
    grad_middle_norm, ffn_gain_terms = rms_rows_back(middle, g_ffn, inv_ffn, grad_h_ffn)
    grad_middle = grad_out + grad_middle_norm
    grad_branch = grad_middle.astype(BF16)
    grad_mixed = jnp.einsum("rd,hd->rh", grad_branch, full_out, preferred_element_type=F32).astype(BF16)
    back_parts = grad_mixed.reshape(2, BLK, 16, HD).transpose(2, 1, 0, 3).reshape(16, BLK, 2 * HD)
    recv_g, result_parts = exchange(
        6, "to_heads_back", ("r", "a2a", back_parts), ("x", "a2a", result4.reshape(NX, ROWS, D))
    )
    output = (middle + jnp.sum(result_parts.astype(F32), axis=0)).astype(BF16)[None]

    grad_w_gu = jnp.einsum("rd,rf->df", h4, grad_gu, preferred_element_type=F32).astype(BF16)
    grad_w_o = jnp.einsum("rh,rd->hd", mixed, grad_branch, preferred_element_type=F32).astype(BF16)
    grad_w_d = jnp.stack(
        [
            jnp.einsum(
                "rf,rd->fd", hidden, cot4[:, q * 256 : (q + 1) * 256], preferred_element_type=F32
            )
            for q in range(4)
        ]
    ).astype(BF16)
    sum_go = lax.psum_scatter(
        jnp.concatenate([grad_w_gu, grad_w_o], axis=1), CTX_FSDP, scatter_dimension=0, tiled=True
    )
    sum_d = lax.psum_scatter(
        grad_w_d.reshape(4 * FX, D // 4), CTX_FSDP, scatter_dimension=0, tiled=True
    )

    sends_back = attend_back(pair, recv_g, q_s, k_s, v_s, o_t, inv)
    (recv_back,) = exchange(7, "to_tokens_back", ("c", "a2a", sends_back))
    grad_h_qkv, grad_w_qkv, gains_qk = project_back(
        blocks, recv_back, raw, h_all, w_qkv, cos_t, sin_t, gq2, gk2
    )
    grad_h_parts, grad_w_parts = exchange(
        8,
        "sum_qkv",
        ("x", "a2a", grad_h_qkv.reshape(NX, ROWS, D)),
        ("p", "a2a", grad_w_qkv.reshape(32, 32, QX + 2 * KX)),
    )
    grad_h_attn = jnp.sum(grad_h_parts.astype(F32), axis=0)
    grad_inputs_norm, attn_gain_terms = rms_rows_back(inputs, g_attn, inv_attn, grad_h_attn)
    grad_tokens = (grad_middle + grad_inputs_norm).astype(BF16)[None]
    sum_qkv = jnp.sum(grad_w_parts.astype(F32), axis=0).astype(BF16)
    gains = jnp.concatenate(
        [
            jnp.sum(attn_gain_terms, axis=0).reshape(8, 128),
            jnp.sum(ffn_gain_terms, axis=0).reshape(8, 128),
            gains_qk,
        ]
    )
    last, gains_x, down_x = exchange(
        9,
        "gather_out",
        ("x", "ag", jnp.concatenate([sum_qkv, sum_go], axis=1)),
        ("x", "ag", gains),
        ("d", "ag", sum_d),
    )
    (gains_p,) = exchange(10, "gather_gains", ("p", "ag", jnp.sum(gains_x, axis=0)))
    gains = jnp.sum(gains_p, axis=0)
    last = last.astype(F32)
    grad_w_query = last[:, :, :QX].transpose(1, 0, 2).reshape(32, H * HD)
    grad_w_key = last[:, :, QX : QX + KX].transpose(1, 0, 2).reshape(32, KV * HD)
    grad_w_value = last[:, :, QX + KX : QX + 2 * KX].transpose(1, 0, 2).reshape(32, KV * HD)
    rest = last[:, :, QX + 2 * KX :]
    grad_w_gate = rest[:, :, :FX].transpose(1, 0, 2).reshape(32, FF)
    grad_w_up = rest[:, :, FX : 2 * FX].transpose(1, 0, 2).reshape(32, FF)
    grad_w_out = jnp.sum(rest[:, :, 2 * FX :], axis=0)
    grad_w_down = down_x.astype(F32).transpose(1, 0, 2).reshape(FF // 32, D)
    g_q = gains[16, :HD] + gains[16, HD:]
    g_k = gains[17, :HD] + gains[17, HD:]
    return (
        output,
        grad_tokens,
        grad_w_query,
        grad_w_key,
        grad_w_value,
        grad_w_out,
        grad_w_gate,
        grad_w_up,
        grad_w_down,
        gains[:8].reshape(D),
        g_q,
        g_k,
        gains[8:16].reshape(D),
    )


def solution(mesh):
    finer = Mesh(
        mesh.devices.reshape(mesh.shape["seq"], 4, 4, mesh.shape["fsdp"]),
        ("seq", "ctx_0", "ctx_1", "fsdp"),
    )
    tokens_spec = P(("seq", "fsdp"), CTX, None)
    rows_spec = P(CTX_FSDP, None)
    return jax.shard_map(
        body,
        mesh=finer,
        in_specs=(tokens_spec, P(("seq", "fsdp"), None))
        + (rows_spec,) * 7
        + (P(),) * 4
        + (tokens_spec,),
        out_specs=(tokens_spec, tokens_spec) + (rows_spec,) * 7 + (P(),) * 4,
        check_vma=False,
    )
```

time: 967 us -> 445 us (0.46)
  the two profiles are of different devices: /device:TPU:4 before, /device:TPU:1 now
where the time goes in v1:
time: 445 us; the launch traced here: 436 us
  Pallas kernels  256 us (58%)
  waiting for transfers between devices  72.3 us (16%)
  matrix products  43.6 us (10%)
  other arithmetic  30.2 us (7%)
  local copies, waits for them, and re-layouts  18.1 us (4%)
  between operations  14.8 us (3%)
    pallas_call x10, Pallas kernels, exchange(): pl.pallas_call(functools.partial(exchange_kernel, items), out_shape=outs,...  211 us
    reduce_scatter x1, waiting for transfers between devices, body(): lax.psum_scatter(grad_w_d.reshape(4 * FX, D // 4), CTX_FSDP, scatter_dime...  53.5 us
    all_gather x1, waiting for transfers between devices, body(): wide = lax.all_gather(mine, CTX_FSDP, axis=0, tiled=True)  18.7 us
    pallas_call x1, Pallas kernels, attend_back(): pl.pallas_call(attend_back_kernel, grid_spec=pltpu.PrefetchScalarGridSpec...  17.8 us
    dot_general x4, matrix products, body(): jnp.einsum('rd,fd->rf', cot4[:, q * 256:(q + 1) * 256], w_dn[q], preferre...  12.5 us
    pallas_call x1, Pallas kernels, attend(): pl.pallas_call(attend_kernel, grid_spec=pltpu.PrefetchScalarGridSpec(num_...  10.4 us
    pallas_call x1, Pallas kernels, project_back(): pl.pallas_call(project_back_kernel, grid_spec=pltpu.PrefetchScalarGridSpe...  9.91 us
  transfers between devices with their start and end apart: 5, of which 2 were waited for; matrix products, arithmetic and copies ran while one was open for 11% of the time, Pallas kernels for 43%

profile of v1, /device:TPU:1, one launch (start us, length us, event | category | flops | bytes accessed | tf_op | source)
XLA Modules:
  0.0 436.5 jit_solution(7202609337289285970)
XLA Ops:
  7.3 0.9 copy-done
  8.2 0.7 collective-permute-start
  9.6 0.9 constant_dynamic-slice_fusion.1
  10.5 1.5 pad_maximum_fusion.9
  12.1 1.3 pad.4.refs_2_
  13.4 0.7 constant_dynamic-slice_fusion.6
  14.1 0.7 constant_dynamic-slice_fusion.4
  15.4 1.1 fusion.23
  16.6 1.9 fusion.25.refs_0_
  18.4 34.8 %gather_in.1 = (bf16[4,160,1024]{2,1,0:T(8,128)(2,1)}, bf16[32,32,512]{2,1,0:T(8,128)(2,1)}, s32[4,8,128]{2,1,0:T(8,128)}) custom-call(bf16[160,1024]{1,0:T(8,128)(2,1)} %fusion.25.refs_0_, bf16[32,512]{1,0:T(8,128)(2,1)} %pad_maximum_fusion.10.refs_1_, s32[8,128]{1,0:T(8,128)} %pad.4.refs_2_), custom_call_target="tpu_custom_call" | custom-call | tf_op jit(solution)/shard_map/gather_in/pallas_call | solution.py:171
  53.2 0.7 slice.91
  55.5 6.9 %project.1 = (bf16[16,240,128]{2,1,0:T(8,128)(2,1)}, f32[640,384]{1,0:T(8,128)}) custom-call(s32[8]{0:T(128)} %reshape.172.blocks, bf16[640,1024]{1,0:T(8,128)(2,1)} %bitcast.100, bf16[1024,512]{1,0:T(8,128)(2,1)} %bitcast.102, f32[2560,128]{1,0:T(8,128)} %constant.53.clone.cos_t, f32[2560,128]{1,0:T(8,128)} %constant.54.clone.sin_t, ...), custom_call_target="tpu_custom_call" | custom-call | tf_op jit(solution)/shard_map/project/pallas_call | solution.py:254
  62.4 20.2 %to_heads.1 = (bf16[16,240,128]{2,1,0:T(8,128)(2,1)}, bf16[4,160,1024]{2,1,0:T(8,128)(2,1)}) custom-call(bf16[16,240,128]{2,1,0:T(8,128)(2,1)} %get-tuple-element.39.refs_0_, bf16[160,1024]{1,0:T(8,128)(2,1)} %bitcast.107), custom_call_target="tpu_custom_call" | custom-call | tf_op jit(solution)/shard_map/to_heads/pallas_call | solution.py:171
  83.1 10.4 %attend.1 = (bf16[16,80,128]{2,1,0:T(8,128)(2,1)}, bf16[2560,128]{1,0:T(8,128)(2,1)}, bf16[2560,128]{1,0:T(8,128)(2,1)}, bf16[2560,128]{1,0:T(8,128)(2,1)}, f32[64,2560]{1,0:T(8,128)}, /*index=5*/f32[8,2560]{1,0:T(8,128)}) custom-call(s32[16]{0:T(128)} %fusion.56.pair, bf16[16,240,128]{2,1,0:T(8,128)(2,1)} %get-tuple-element.40.recv), custom_call_target="tpu_custom_call" | custom-call | tf_op jit(solution)/shard_map/attend/pallas_call | solution.py:314
  93.5 22.0 %to_tokens.1 = bf16[16,80,128]{2,1,0:T(8,128)(2,1)} custom-call(bf16[16,80,128]{2,1,0:T(8,128)(2,1)} %get-tuple-element.41.refs_0_), custom_call_target="tpu_custom_call" | custom-call | tf_op jit(solution)/shard_map/to_tokens/pallas_call | solution.py:171
  115.5 1.2 copy.33
  117.8 3.6 fusion.34
  121.4 2.2 fusion.37
  123.6 2.2 fusion.40
  125.8 18.7 %all-gather.3.cloned.1.call-done = bf16[1024,3328]{1,0:T(8,128)(2,1)} async-done(((bf16[32,3328]{1,0:T(8,128)(2,1)}), bf16[1024,3328]{1,0:T(8,128)(2,1)}) %all-gather.3.cloned.1.call-update) | async-done | bytes 6815760 | tf_op jit(solution)/shard_map/all_gather | solution.py:508
  144.5 2.2 multiply_reduce_fusion.2
  146.8 0.9 multiply_convert_fusion.3.refs_0_
  147.6 18.7 %gather_ffn.1 = bf16[4,160,1024]{2,1,0:T(8,128)(2,1)} custom-call(bf16[160,1024]{1,0:T(8,128)(2,1)} %multiply_convert_fusion.3.refs_0_), custom_call_target="tpu_custom_call" | custom-call | tf_op jit(solution)/shard_map/gather_ffn/pallas_call | solution.py:171
  166.4 6.1 %fusion.2 = f32[640,2304]{1,0:T(8,128)S(1)} fusion(bf16[640,1024]{1,0:T(8,128)(2,1)} %bitcast.109, bf16[1024,3328]{1,0:T(8,128)(2,1)} %all-gather.3.cloned.1.call-done), kind=kOutput, calls=%fused_computation.4 | convolution fusion | flops 3019898880 | bytes 11927552 | tf_op jit(solution)/shard_map/dot_general | solution.py:543
  172.6 4.5 %multiply_convert_fusion.2 = (bf16[640,1152]{1,0:T(8,128)(2,1)S(1)}, bf16[640,1152]{1,0:T(8,128)(2,1)S(1)}, bf16[640,1152]{1,0:T(8,128)(2,1)}) fusion(f32[640,2304]{1,0:T(8,128)S(1)} %fusion.2, f32[640,1152]{1,0:T(8,128)S(1)} %copy-done.3, f32[640,1152]{1,0:T(8,128)S(1)} %copy-done.4, f32[640,1152]{1,0:T(8,128)S(1)} %copy-done.5, ...), kind=kOutput, calls=%fused_computation.12 | convolution fusion | flops 390758400 | bytes 20086784 | tf_op jit(solution)/shard_map/rd,fd->rf/dot_general | solution.py:549
  177.1 5.6 %convolution_convert_fusion = bf16[1024,2304]{1,0:T(8,128)(2,1)} fusion(bf16[640,1024]{1,0:T(8,128)(2,1)S(1)} %bitcast.110, bf16[640,1152]{1,0:T(8,128)(2,1)S(1)} %get-tuple-element.64, bf16[640,1152]{1,0:T(8,128)(2,1)S(1)} %get-tuple-element.63), kind=kOutput, calls=%fused_computation.1 | convolution fusion | flops 3028156416 | bytes 8978432 | tf_op jit(solution)/shard_map/rd,rf->df/dot_general | solution.py:577
  182.7 4.3 fusion.15
  187.0 18.4 %sum_ffn.1 = bf16[4,160,1024]{2,1,0:T(8,128)(2,1)} custom-call(bf16[4,160,1024]{2,1,0:T(8,128)(2,1)} %bitcast.111), custom_call_target="tpu_custom_call" | custom-call | tf_op jit(solution)/shard_map/sum_ffn/pallas_call | solution.py:171
  205.4 1.6 convert_reduce_fusion.2
  207.5 0.7 convolution_convert_fusion.5
  208.3 5.7 %pad_maximum_fusion = bf16[1024,3328]{1,0:T(8,128)(2,1)} fusion(bf16[1024,1024]{1,0:T(8,128)(2,1)S(1)} %convolution_convert_fusion.5, bf16[1024,2304]{1,0:T(8,128)(2,1)} %convolution_convert_fusion), kind=kLoop, calls=%fused_computation | loop fusion | flops 13631488 | bytes 13631488 | tf_op jit(solution)/shard_map/concatenate | solution.py:588
  214.3 1.0 copy-done.12
  215.3 2.0 fusion.10
  217.3 0.7 fusion.9
  218.0 0.7 fusion.8
  218.7 0.7 fusion.7
  219.4 1.7 pad_maximum_fusion.2
  221.1 2.4 fusion.20
  224.6 0.9 copy.36.refs_0_
  225.5 2.3 convolution_convert_fusion.6
  228.0 2.0 convolution_convert_fusion.7
  231.2 1.3 pad_maximum_fusion.7.refs_1_
  232.5 24.0 %to_heads_back.1 = (bf16[16,80,128]{2,1,0:T(8,128)(2,1)}, bf16[4,160,1024]{2,1,0:T(8,128)(2,1)}) custom-call(bf16[16,80,128]{2,1,0:T(8,128)(2,1)} %copy.36.refs_0_, bf16[4,160,1024]{2,1,0:T(8,128)(2,1)} %pad_maximum_fusion.7.refs_1_), custom_call_target="tpu_custom_call" | custom-call | tf_op jit(solution)/shard_map/to_heads_back/pallas_call | solution.py:171
  256.4 17.8 %attend_back.1.refs_0_ = bf16[16,240,128]{2,1,0:T(8,128)(2,1)} custom-call(s32[16]{0:T(128)} %fusion.56.pair, bf16[16,80,128]{2,1,0:T(8,128)(2,1)} %get-tuple-element.44.recv, bf16[2560,128]{1,0:T(8,128)(2,1)} %get-tuple-element.45.q_s, bf16[2560,128]{1,0:T(8,128)(2,1)} %get-tuple-element.46.k_s, bf16[2560,128]{1,0:T(8,128)(2,1)} %get-tuple-element.47.v_s, ...), custom_call_target="tpu_custom_call" | custom-call | tf_op jit(solution)/shard_map/attend_back/pallas_call | solution.py:384
  274.3 16.1 %to_tokens_back.1.recv = bf16[16,240,128]{2,1,0:T(8,128)(2,1)} custom-call(bf16[16,240,128]{2,1,0:T(8,128)(2,1)} %attend_back.1.refs_0_), custom_call_target="tpu_custom_call" | custom-call | tf_op jit(solution)/shard_map/to_tokens_back/pallas_call | solution.py:171
  290.4 9.9 %project_back.1 = (bf16[640,1024]{1,0:T(8,128)(2,1)}, bf16[1024,512]{1,0:T(8,128)(2,1)}, f32[8,128]{1,0:T(8,128)}) custom-call(s32[8]{0:T(128)} %reshape.172.blocks, bf16[16,240,128]{2,1,0:T(8,128)(2,1)} %to_tokens_back.1.recv, f32[640,384]{1,0:T(8,128)} %get-tuple-element.50.raw, bf16[640,1024]{1,0:T(8,128)(2,1)} %bitcast.101, bf16[1024,512]{1,0:T(8,128)(2,1)} %bitcast.103, ...), custom_call_target="tpu_custom_call" | custom-call | tf_op jit(solution)/shard_map/project_back/pallas_call | solution.py:442
  300.3 23.9 %sum_qkv.1 = (bf16[4,160,1024]{2,1,0:T(8,128)(2,1)}, bf16[32,32,512]{2,1,0:T(8,128)(2,1)}) custom-call(bf16[4,160,1024]{2,1,0:T(8,128)(2,1)} %bitcast.108, bf16[32,32,512]{2,1,0:T(8,128)(2,1)} %bitcast.112), custom_call_target="tpu_custom_call" | custom-call | tf_op jit(solution)/shard_map/sum_qkv/pallas_call | solution.py:171
  324.2 1.5 reduce_sum.127
  325.7 1.7 convert_reduce_fusion
  328.5 0.8 fusion.44
  329.3 1.0 fusion.45
  330.4 1.6 pad_maximum_fusion.8.refs_0_
  332.0 53.5 %reduce-scatter.5.cloned.1.call-done.refs_2_ = bf16[144,256]{1,0:T(8,128)(2,1)} async-done(((bf16[4608,256]{1,0:T(8,128)(2,1)}), bf16[144,256]{1,0:T(8,128)(2,1)}) %reduce-scatter.5.cloned.1.call-update) | async-done | bytes 73744 | tf_op jit(solution)/shard_map/reduce_scatter | solution.py:590
  385.5 17.0 %gather_out.1 = (bf16[4,32,3840]{2,1,0:T(8,128)(2,1)}, f32[4,24,128]{2,1,0:T(8,128)}, bf16[4,144,256]{2,1,0:T(8,128)(2,1)}) custom-call(bf16[32,3840]{1,0:T(8,128)(2,1)} %pad_maximum_fusion.8.refs_0_, f32[24,128]{1,0:T(8,128)} %pad_maximum_fusion.11.refs_1_, bf16[144,256]{1,0:T(8,128)(2,1)} %reduce-scatter.5.cloned.1.call-done.refs_2_), custom_call_target="tpu_custom_call" | custom-call | tf_op jit(solution)/shard_map/gather_out/pallas_call | solution.py:171
  402.5 1.4 reduce_sum.131.refs_0_
  403.9 16.3 %gather_gains.1 = f32[32,24,128]{2,1,0:T(8,128)} custom-call(f32[24,128]{1,0:T(8,128)} %reduce_sum.131.refs_0_), custom_call_target="tpu_custom_call" | custom-call | tf_op jit(solution)/shard_map/gather_gains/pallas_call | solution.py:171
  420.3 1.0 reduce_sum.132
  422.5 1.4 convert_element_type.86
  423.9 0.7 slice_reduce_fusion
  424.9 0.9 copy.50
  425.8 0.7 copy.45
  426.4 0.9 copy.49
  427.3 0.6 copy.53
  428.6 0.9 copy.48
  (89 shorter events, 10.8 us)
Async XLA Ops:
  7.2 1.0 copy-start
  7.2 47.7 %copy-start.19 = (f32[64]{0:T(128)S(1)}, f32[64]{0:T(128)}, u32[]{:S(2)}) copy-start(f32[64]{0:T(128)} %param.27) | copy-start | bytes 772
  7.2 47.7 %copy-start.18 = (f32[64]{0:T(128)S(1)}, f32[64]{0:T(128)}, u32[]{:S(2)}) copy-start(f32[64]{0:T(128)} %param.26) | copy-start | bytes 772
  7.2 110.6 %all-gather.5.cloned.1.call-start = ((), (), s32[]{:S(2)}) async-start(), calls=%async_computation.3 | async-start | bytes 2433024 | tf_op jit(solution)/shard_map/all_gather | solution.py:512
  8.2 0.7 collective-permute-start
  8.8 0.6 copy-start.14
  9.5 135.0 %all-gather.3.cloned.1.call-start = ((), (), s32[]{:S(2)}) async-start(), calls=%async_computation.2 | async-start | bytes 7028736 | tf_op jit(solution)/shard_map/all_gather | solution.py:508
  12.1 318.3 %reduce-scatter.3.cloned.1.call-start = ((), (), s32[]{:S(2)}) async-start(), calls=%async_computation.4 | async-start | bytes 7028736 | tf_op jit(solution)/shard_map/reduce_scatter | solution.py:587
  117.7 3.6 copy-start.11
  117.8 3.6 copy-start.6
  123.6 20.9 %copy-start.2 = (bf16[1,160,1024]{2,1,0:T(8,128)(2,1)S(1)}, bf16[1,160,1024]{2,1,0:T(8,128)(2,1)}, u32[]{:S(2)}) copy-start(bf16[1,160,1024]{2,1,0:T(8,128)(2,1)} %param.16) | copy-start | bytes 983044
  125.8 20.9 %copy-start.15 = (f32[1024]{0:T(1024)S(1)}, f32[1024]{0:T(1024)}, u32[]{:S(2)}) copy-start(f32[1024]{0:T(1024)} %param.28) | copy-start | bytes 12292
  166.4 6.1 %copy-start.3 = (f32[640,1152]{1,0:T(8,128)S(1)}, f32[640,1152]{1,0:T(8,128)}, u32[]{:S(2)}) copy-start(f32[640,1152]{1,0:T(8,128)} %fusion.34) | copy-start | bytes 8847364
  166.4 6.1 %copy-start.4 = (f32[640,1152]{1,0:T(8,128)S(1)}, f32[640,1152]{1,0:T(8,128)}, u32[]{:S(2)}) copy-start(f32[640,1152]{1,0:T(8,128)} %fusion.37) | copy-start | bytes 8847364
  166.4 6.1 %copy-start.5 = (f32[640,1152]{1,0:T(8,128)S(1)}, f32[640,1152]{1,0:T(8,128)}, u32[]{:S(2)}) copy-start(f32[640,1152]{1,0:T(8,128)} %fusion.40) | copy-start | bytes 8847364
  166.4 16.3 %slice-start = ((s8[6815744]{0:T(1024)(128)(4,1)}), s8[4194304]{0:T(1024)(128)(4,1)S(1)}, s32[]{:S(2)}) async-start(s8[6815744]{0:T(1024)(128)(4,1)} %bitcast.134), calls=%async_computation.6 | async-start | bytes 8388608
  172.5 4.5 %copy-start.9 = (bf16[4,160,1024]{2,1,0:T(8,128)(2,1)S(1)}, bf16[4,160,1024]{2,1,0:T(8,128)(2,1)}, u32[]{:S(2)}) copy-start(bf16[4,160,1024]{2,1,0:T(8,128)(2,1)} %gather_ffn.1) | copy-start | bytes 3932164
  172.6 10.1 %slice-start.1 = ((s8[6815744]{0:T(1024)(128)(4,1)}), s8[2621440]{0:T(1024)(128)(4,1)S(1)}, s32[]{:S(2)}) async-start(s8[6815744]{0:T(1024)(128)(4,1)} %bitcast.134), calls=%async_computation.7 | async-start | bytes 5242880
  187.0 20.3 %copy-start.8 = (bf16[1,160,1024]{2,1,0:T(8,128)(2,1)S(1)}, bf16[1,160,1024]{2,1,0:T(8,128)(2,1)}, u32[]{:S(2)}) copy-start(bf16[1,160,1024]{2,1,0:T(8,128)(2,1)} %param.29) | copy-start | bytes 983044
  214.0 1.3 copy-start.12
  214.0 171.5 %reduce-scatter.5.cloned.1.call-start = ((), (), s32[]{:S(2)}) async-start(), calls=%async_computation.5 | async-start | bytes 2433024 | tf_op jit(solution)/shard_map/reduce_scatter | solution.py:590
  214.2 3.1 copy-start.20
  225.5 2.5 copy-start.7
  225.5 4.5 %copy-start.21 = (bf16[640,1152]{1,0:T(8,128)(2,1)S(1)}, bf16[640,1152]{1,0:T(8,128)(2,1)}, u32[]{:S(2)}) copy-start(bf16[640,1152]{1,0:T(8,128)(2,1)} %get-tuple-element.65) | copy-start | bytes 4423684
  300.3 27.1 %copy-start.16 = (f32[1024]{0:T(1024)S(1)}, f32[1024]{0:T(1024)}, u32[]{:S(2)}) copy-start(f32[1024]{0:T(1024)} %param.25) | copy-start | bytes 12292
  324.2 3.4 copy-start.17
  324.2 4.0 copy-start.10
  423.8 1.0 copy-start.13
  424.7 4.8 %copy-start.1 = (bf16[144,1024]{1,0:T(8,128)(2,1)S(1)}, bf16[144,1024]{1,0:T(8,128)(2,1)}, u32[]{:S(2)}) copy-start(bf16[144,1024]{1,0:T(8,128)(2,1)} %param.24) | copy-start | bytes 884740
Sparse Core Ops, SparseCore 0:
  10.9 69.5 all-gather.4
  83.3 61.1 all-gather.2
  214.1 88.7 reduce-scatter.2
  306.7 78.7 reduce-scatter.4

commit v2 on v1

--- a/solution.py
+++ b/solution.py
@@ -41,6 +41,18 @@
     return tuple(lax.axis_index(a) for a in SEQ_CTX_FSDP)
 
 
+def twisted(x, v):
+    return lax.rem(v + 2 * (1 - lax.rem(x, 2)) * (1 - lax.rem(v, 2)), 4)
+
+
+def sequence_at(x, z):
+    return lax.rem(x + twisted(x, z), 4)
+
+
+def place_of(x, s):
+    return twisted(x, lax.rem(s - x + 4, 4))
+
+
 def target(group, t):
     s, z, y, c = coords()
     if group == "x":
@@ -50,18 +62,18 @@
     if group == "p":
         return (s, t // 8, lax.rem(t // 2, 4), lax.rem(t, 2)), (z * 4 + y) * 2 + c
     if group == "t":
-        return (z, t // 4, lax.rem(t, 4), c), s * 4 + y
+        return (sequence_at(s, z), t // 4, lax.rem(t, 4), c), s * 4 + y
     if group == "d":
         return (t, s, y, c), z
-    return (t // 4, s, lax.rem(t, 4), c), z * 4 + y
+    return (t // 4, place_of(t // 4, s), lax.rem(t, 4), c), z * 4 + y
 
 
 def source(group, t):
     s, z, y, c = coords()
     if group == "t":
-        return (t // 4, s, lax.rem(t, 4), c)
+        return (t // 4, place_of(t // 4, s), lax.rem(t, 4), c)
     if group == "r":
-        return (z, t // 4, lax.rem(t, 4), c)
+        return (sequence_at(s, z), t // 4, lax.rem(t, 4), c)
     if group == "d":
         return (z, t, y, c)
     return target(group, t)[0]
@@ -70,9 +82,9 @@
 def own(group):
     s, z, y, c = coords()
     if group == "t":
-        return s == z, z * 4 + y, s * 4 + y
+        return sequence_at(s, z) == s, z * 4 + y, s * 4 + y
     if group == "r":
-        return s == z, s * 4 + y, z * 4 + y
+        return sequence_at(s, z) == s, s * 4 + y, z * 4 + y
     if group == "d":
         return s == z, s, z
     me = target(group, 0)[1]
@@ -246,8 +258,8 @@
             q = turned[hh // 2]
             q = q if hh % 2 == 0 else swap(q)
             k = swapped_keys if hh < 2 else keys
-            send[s * 4 + hh, :ROWS, :] = jnp.where(m, q, k).astype(BF16)
-            send[s * 4 + hh, ROWS:, :] = packed[hh // 2].astype(BF16)
+            send[blocks[8 + s] * 4 + hh, :ROWS, :] = jnp.where(m, q, k).astype(BF16)
+            send[blocks[8 + s] * 4 + hh, ROWS:, :] = packed[hh // 2].astype(BF16)
 
 
 def project(blocks, h, w, cos_t, sin_t, g_q, g_k):
@@ -402,7 +414,7 @@
     )(pair, recv, q_s, k_s, v_s, o_t, inv)
 
 
-def project_back_kernel(blocks, recv, raw, h, w, cos_t, sin_t, g_q, g_k, gh, dw, gains, low):
+def project_back_kernel(blocks, recv, raw, h, w, cos_t, sin_t, g_q, g_k, gh, dw, gains, attn, low):
     m = low_half((ROWS, 2 * HD))
     mh = low_half((BLK, 2 * HD))
     gq_sum = jnp.zeros((1, 2 * HD), F32)
@@ -410,8 +422,8 @@
     for s in range(NX):
         at = slice(s * ROWS, (s + 1) * ROWS)
         cos_r, sin_r = rope_rows(blocks, cos_t, s), rope_rows(blocks, sin_t, s)
-        part = [recv[s * 4 + hh, :ROWS, :].astype(F32) for hh in range(4)]
-        vals = [recv[s * 4 + hh, ROWS:, :].astype(F32) for hh in range(4)]
+        part = [recv[blocks[8 + s] * 4 + hh, :ROWS, :].astype(F32) for hh in range(4)]
+        vals = [recv[blocks[8 + s] * 4 + hh, ROWS:, :].astype(F32) for hh in range(4)]
         grads = [
             jnp.where(m, part[0], swap(part[1])),
             jnp.where(m, part[2], swap(part[3])),
@@ -434,7 +446,12 @@
         grad_v = jnp.concatenate([jnp.where(mh, a, swap(b)), jnp.where(mh, swap(a), b)], 0)
         low[at, 3 * 128 :] = grad_v.astype(BF16)
     gains[...] = jnp.concatenate([gq_sum, gk_sum, jnp.zeros((6, 2 * HD), F32)], 0)
-    gh[...] = nt(low[...], w[...]).astype(BF16)
+    for s in range(NX):
+        at = slice(s * ROWS, (s + 1) * ROWS)
+        grad_h = nt(low[at, :], w[...])
+        gh[at, :] = grad_h.astype(BF16)
+        term = jnp.sum(grad_h * h[at, :].astype(F32), axis=0, keepdims=True)
+        attn[...] = term if s == 0 else attn[...] + term
     dw[...] = tn(h[...], low[...]).astype(BF16)
 
 
@@ -444,13 +461,14 @@
         grid_spec=pltpu.PrefetchScalarGridSpec(
             num_scalar_prefetch=1,
             in_specs=[pl.BlockSpec(memory_space=pltpu.VMEM)] * 8,
-            out_specs=[pl.BlockSpec(memory_space=pltpu.VMEM)] * 3,
+            out_specs=[pl.BlockSpec(memory_space=pltpu.VMEM)] * 4,
             scratch_shapes=[pltpu.VMEM((NX * ROWS, QX + 2 * KX), BF16)],
         ),
         out_shape=[
             jax.ShapeDtypeStruct((NX * ROWS, D), BF16),
             jax.ShapeDtypeStruct((D, QX + 2 * KX), BF16),
             jax.ShapeDtypeStruct((8, 2 * HD), F32),
+            jax.ShapeDtypeStruct((1, D), F32),
         ],
         compiler_params=pltpu.CompilerParams(vmem_limit_bytes=VMEM_BYTES),
         name="project_back",
@@ -479,6 +497,14 @@
 
 def columns_of(w, x, width):
     return lax.dynamic_slice_in_dim(w, x * width, width, axis=1)
+
+
+def by_tiles(blocks):
+    return blocks.reshape(-1, 9, 16, 2, 128).transpose(0, 3, 2, 1, 4).reshape(-1, 32, FX)
+
+
+def from_tiles(blocks):
+    return blocks.reshape(-1, 2, 16, 9, 128).transpose(0, 3, 2, 1, 4).reshape(-1, FF // 32, D // 4)
 
 
 def body(
@@ -504,12 +530,12 @@
     gq2 = jnp.concatenate([g_query, g_query])[None]
     gk2 = jnp.concatenate([g_key, g_key])[None]
 
-    mine = jnp.concatenate([columns_of(w_gate, x, FX), columns_of(w_up, x, FX), w_out], axis=1)
-    wide = lax.all_gather(mine, CTX_FSDP, axis=0, tiled=True)
-    w_gu, full_out = wide[:, : 2 * FX], wide[:, 2 * FX :]
     swap_xz = [(a * 4 + b, b * 4 + a) for a in range(4) for b in range(4)]
     down_part = lax.ppermute(columns_of(w_down, x, D // 4), ("seq", "ctx_0"), swap_xz)
-    w_dn = lax.all_gather(down_part, CTX_FSDP, axis=0, tiled=True).reshape(4, FX, D // 4)
+    mine = jnp.concatenate(
+        [columns_of(w_gate, x, FX), columns_of(w_up, x, FX), w_out, by_tiles(down_part[None])[0]],
+        axis=1,
+    )
 
     inputs = tokens[0].astype(F32)
     normed_attn, inv_attn = rms_rows(inputs, g_attn)
@@ -521,12 +547,17 @@
     h_all, w_qkv, pairs_all = exchange(
         1, "gather_in", ("x", "ag", h_attn), ("p", "ag", w_x), ("x", "ag", pairs_pad)
     )
+    h_all, mine = lax.optimization_barrier((h_all, mine))
+    wide = lax.all_gather(mine, CTX_FSDP, axis=0, tiled=True)
+    w_gu, full_out = wide[:, : 2 * FX], wide[:, 2 * FX : 2 * FX + D]
+    w_dn = from_tiles(wide[:, 2 * FX + D :].reshape(32, 32, FX)).reshape(4, FX, D // 4)
     h_all = h_all.reshape(NX * ROWS, D)
     w_qkv = w_qkv.reshape(D, QX + 2 * KX)
     pairs_all = pairs_all[:, 0, :16]
     first = lax.dynamic_slice_in_dim(pairs_all, ctx, 1, axis=1)[:, 0]
-    blocks = jnp.stack([first, 31 - first], axis=1).reshape(8)
-    pair = lax.dynamic_slice_in_dim(pairs_all, z, 1, axis=0)[0]
+    places = jnp.stack([place_of(x, s) for s in range(4)])
+    blocks = jnp.concatenate([jnp.stack([first, 31 - first], axis=1).reshape(8), places])
+    pair = lax.dynamic_slice_in_dim(pairs_all, sequence_at(x, z), 1, axis=0)[0]
 
     send, raw = project(blocks, h_all, w_qkv, cos_t, sin_t, gq2, gk2)
     recv, cot_all = exchange(2, "to_heads", ("c", "a2a", send), ("x", "ag", cotangent[0]))
@@ -557,6 +588,20 @@
     grad_up = (grad_hidden * silu_gate).astype(BF16)
     grad_gu = jnp.concatenate([grad_gate, grad_up], axis=1)
     grad_h4 = jnp.einsum("rf,df->rd", grad_gu, w_gu, preferred_element_type=F32).astype(BF16)
+    grad_w_gu = jnp.einsum("rd,rf->df", h4, grad_gu, preferred_element_type=F32).astype(BF16)
+    grad_w_d = jnp.stack(
+        [
+            jnp.einsum(
+                "rf,rd->fd", hidden, cot4[:, q * 256 : (q + 1) * 256], preferred_element_type=F32
+            )
+            for q in range(4)
+        ]
+    ).astype(BF16)
+    grad_w_d = by_tiles(grad_w_d.reshape(32, FF // 32, D // 4)).reshape(D, FX)
+    sums = lax.psum_scatter(
+        jnp.concatenate([grad_w_gu, grad_w_d], axis=1), CTX_FSDP, scatter_dimension=0, tiled=True
+    )
+    sum_gu, sum_d = sums[:, : 2 * FX], from_tiles(sums[:, 2 * FX :][None])[0]
     (grad_h_parts,) = exchange(5, "sum_ffn", ("x", "a2a", grad_h4.reshape(NX, ROWS, D)))
     result4 = jnp.concatenate(
         [jnp.dot(hidden, w_dn[q], preferred_element_type=F32) for q in range(4)], axis=1
@@ -574,54 +619,48 @@
     )
     output = (middle + jnp.sum(result_parts.astype(F32), axis=0)).astype(BF16)[None]
 
-    grad_w_gu = jnp.einsum("rd,rf->df", h4, grad_gu, preferred_element_type=F32).astype(BF16)
-    grad_w_o = jnp.einsum("rh,rd->hd", mixed, grad_branch, preferred_element_type=F32).astype(BF16)
-    grad_w_d = jnp.stack(
-        [
-            jnp.einsum(
-                "rf,rd->fd", hidden, cot4[:, q * 256 : (q + 1) * 256], preferred_element_type=F32
-            )
-            for q in range(4)
-        ]
+    sends_back = attend_back(pair, recv_g, q_s, k_s, v_s, o_t, inv)
+    recv_back, branch_x, mixed_x, gains_ffn = exchange(
+        7,
+        "to_tokens_back",
+        ("c", "a2a", sends_back),
+        ("x", "ag", grad_branch),
+        ("x", "a2a", mixed.reshape(ROWS, NX, QX).transpose(1, 0, 2)),
+        ("p", "ag", jnp.sum(ffn_gain_terms, axis=0).reshape(8, 128)),
+    )
+    grad_h_qkv, grad_w_qkv, gains_qk, gains_attn = project_back(
+        blocks, recv_back, raw, h_all, w_qkv, cos_t, sin_t, gq2, gk2
+    )
+    gains = jnp.concatenate([(gains_attn / g_attn).reshape(8, 128), gains_qk])
+    grad_w_o = jnp.einsum(
+        "rh,rd->hd",
+        mixed_x.reshape(NX * ROWS, QX),
+        branch_x.reshape(NX * ROWS, D),
+        preferred_element_type=F32,
     ).astype(BF16)
-    sum_go = lax.psum_scatter(
-        jnp.concatenate([grad_w_gu, grad_w_o], axis=1), CTX_FSDP, scatter_dimension=0, tiled=True
-    )
-    sum_d = lax.psum_scatter(
-        grad_w_d.reshape(4 * FX, D // 4), CTX_FSDP, scatter_dimension=0, tiled=True
-    )
-
-    sends_back = attend_back(pair, recv_g, q_s, k_s, v_s, o_t, inv)
-    (recv_back,) = exchange(7, "to_tokens_back", ("c", "a2a", sends_back))
-    grad_h_qkv, grad_w_qkv, gains_qk = project_back(
-        blocks, recv_back, raw, h_all, w_qkv, cos_t, sin_t, gq2, gk2
-    )
-    grad_h_parts, grad_w_parts = exchange(
+    grad_w_o = grad_w_o.reshape(8, 32, 4, D // 4).transpose(2, 0, 1, 3).reshape(32, 32, D // 4)
+    grad_h_parts, grad_w_parts, grad_o_parts, gains_p = exchange(
         8,
         "sum_qkv",
         ("x", "a2a", grad_h_qkv.reshape(NX, ROWS, D)),
         ("p", "a2a", grad_w_qkv.reshape(32, 32, QX + 2 * KX)),
+        ("p", "a2a", grad_w_o),
+        ("p", "ag", gains),
     )
     grad_h_attn = jnp.sum(grad_h_parts.astype(F32), axis=0)
-    grad_inputs_norm, attn_gain_terms = rms_rows_back(inputs, g_attn, inv_attn, grad_h_attn)
+    grad_inputs_norm, _ = rms_rows_back(inputs, g_attn, inv_attn, grad_h_attn)
     grad_tokens = (grad_middle + grad_inputs_norm).astype(BF16)[None]
     sum_qkv = jnp.sum(grad_w_parts.astype(F32), axis=0).astype(BF16)
-    gains = jnp.concatenate(
-        [
-            jnp.sum(attn_gain_terms, axis=0).reshape(8, 128),
-            jnp.sum(ffn_gain_terms, axis=0).reshape(8, 128),
-            gains_qk,
-        ]
-    )
-    last, gains_x, down_x = exchange(
+    sum_o = jnp.sum(grad_o_parts.astype(F32), axis=0).astype(BF16)
+    gains = jnp.concatenate([jnp.sum(gains_p, axis=0), jnp.sum(gains_ffn, axis=0)])
+    last, gains_x, quarters = exchange(
         9,
         "gather_out",
-        ("x", "ag", jnp.concatenate([sum_qkv, sum_go], axis=1)),
+        ("x", "ag", jnp.concatenate([sum_qkv, sum_gu], axis=1)),
         ("x", "ag", gains),
-        ("d", "ag", sum_d),
-    )
-    (gains_p,) = exchange(10, "gather_gains", ("p", "ag", jnp.sum(gains_x, axis=0)))
-    gains = jnp.sum(gains_p, axis=0)
+        ("d", "ag", jnp.concatenate([sum_o, sum_d], axis=0)),
+    )
+    gains = jnp.sum(gains_x, axis=0)
     last = last.astype(F32)
     grad_w_query = last[:, :, :QX].transpose(1, 0, 2).reshape(32, H * HD)
     grad_w_key = last[:, :, QX : QX + KX].transpose(1, 0, 2).reshape(32, KV * HD)
@@ -629,10 +668,11 @@
     rest = last[:, :, QX + 2 * KX :]
     grad_w_gate = rest[:, :, :FX].transpose(1, 0, 2).reshape(32, FF)
     grad_w_up = rest[:, :, FX : 2 * FX].transpose(1, 0, 2).reshape(32, FF)
-    grad_w_out = jnp.sum(rest[:, :, 2 * FX :], axis=0)
-    grad_w_down = down_x.astype(F32).transpose(1, 0, 2).reshape(FF // 32, D)
-    g_q = gains[16, :HD] + gains[16, HD:]
-    g_k = gains[17, :HD] + gains[17, HD:]
+    quarters = quarters.astype(F32)
+    grad_w_out = quarters[:, :32].transpose(1, 0, 2).reshape(32, D)
+    grad_w_down = quarters[:, 32:].transpose(1, 0, 2).reshape(FF // 32, D)
+    g_q = gains[8, :HD] + gains[8, HD:]
+    g_k = gains[9, :HD] + gains[9, HD:]
     return (
         output,
         grad_tokens,
@@ -646,7 +686,7 @@
         gains[:8].reshape(D),
         g_q,
         g_k,
-        gains[8:16].reshape(D),
+        gains[16:].reshape(D),
     )
 
 

time: 445 us -> 400 us (0.90)
  the two profiles are of different devices: /device:TPU:1 before, /device:TPU:4 now
where the time goes in v2:
time: 400 us; the launch traced here: 392 us
  Pallas kernels  244 us (61%)
  local copies, waits for them, and re-layouts  52.4 us (13%)
  matrix products  36.4 us (9%)
  other arithmetic  31.8 us (8%)
  between operations  15.4 us (4%)
  waiting for transfers between devices  6.95 us (2%)
  starting transfers between devices  5.81 us (1%)
    pallas_call x9, Pallas kernels, exchange(): pl.pallas_call(functools.partial(exchange_kernel, items), out_shape=outs,...  198 us
    pallas_call x1, Pallas kernels, attend_back(): pl.pallas_call(attend_back_kernel, grid_spec=pltpu.PrefetchScalarGridSpec...  17.9 us
    pallas_call x1, Pallas kernels, attend(): pl.pallas_call(attend_kernel, grid_spec=pltpu.PrefetchScalarGridSpec(num_...  10.5 us
    pallas_call x1, Pallas kernels, project_back(): pl.pallas_call(project_back_kernel, grid_spec=pltpu.PrefetchScalarGridSpe...  9.98 us
  transfers between devices with their start and end apart: 3, of which 1 were waited for; matrix products, arithmetic and copies ran while one was open for 15% of the time, Pallas kernels for 52%

profile of v2, /device:TPU:4, one launch (start us, length us, event | category | flops | bytes accessed | tf_op | source)
XLA Modules:
  0.0 392.3 jit_solution(17927520126281741569)
XLA Ops:
  7.3 0.9 copy-done
  8.2 5.7 %collective-permute-start = (bf16[144,256]{1,0:T(8,128)(2,1)S(1)}, bf16[144,256]{1,0:T(8,128)(2,1)S(1)}, u32[]{:S(2)}, u32[]{:S(2)}) collective-permute-start(bf16[144,256]{1,0:T(8,128)(2,1)S(1)} %constant_dynamic-slice_fusion), channel_id=1, source_target_pairs={{0,0},{8,32},{16,64},{24,96},{32,8},{40,40},{48,72},{56,104},{64,1... | collective-permute-start | bytes 221192 | tf_op jit(solution)/shard_map/ppermute | solution.py:534
  13.9 1.1 fusion.22
  15.8 1.3 pad.4.refs_2_
  17.0 1.8 fusion.24.refs_0_
  19.6 0.9 constant_dynamic-slice_fusion.1
  21.1 22.6 %gather_in.1 = (bf16[4,160,1024]{2,1,0:T(8,128)(2,1)}, bf16[32,32,512]{2,1,0:T(8,128)(2,1)}, s32[4,8,128]{2,1,0:T(8,128)}) custom-call(bf16[160,1024]{1,0:T(8,128)(2,1)} %fusion.24.refs_0_, bf16[32,512]{1,0:T(8,128)(2,1)} %pad_maximum_fusion.11.refs_1_, s32[8,128]{1,0:T(8,128)} %pad.4.refs_2_), custom_call_target="tpu_custom_call" | custom-call | tf_op jit(solution)/shard_map/gather_in/pallas_call | solution.py:183
  47.6 6.9 %project.1 = (bf16[16,240,128]{2,1,0:T(8,128)(2,1)}, f32[640,384]{1,0:T(8,128)}) custom-call(s32[12]{0:T(128)} %concatenate.39.blocks, bf16[640,1024]{1,0:T(8,128)(2,1)} %bitcast.171, bf16[1024,512]{1,0:T(8,128)(2,1)} %bitcast.173, f32[2560,128]{1,0:T(8,128)} %constant.98.clone.cos_t, f32[2560,128]{1,0:T(8,128)} %constant.99.clone.sin_t, ...), custom_call_target="tpu_custom_call" | custom-call | tf_op jit(solution)/shard_map/project/pallas_call | solution.py:266
  54.5 20.2 %to_heads.1 = (bf16[16,240,128]{2,1,0:T(8,128)(2,1)}, bf16[4,160,1024]{2,1,0:T(8,128)(2,1)}) custom-call(bf16[16,240,128]{2,1,0:T(8,128)(2,1)} %get-tuple-element.49.refs_0_, bf16[160,1024]{1,0:T(8,128)(2,1)} %bitcast.185), custom_call_target="tpu_custom_call" | custom-call | tf_op jit(solution)/shard_map/to_heads/pallas_call | solution.py:183
  74.7 10.5 %attend.1 = (bf16[16,80,128]{2,1,0:T(8,128)(2,1)}, bf16[2560,128]{1,0:T(8,128)(2,1)}, bf16[2560,128]{1,0:T(8,128)(2,1)}, bf16[2560,128]{1,0:T(8,128)(2,1)}, f32[64,2560]{1,0:T(8,128)}, /*index=5*/f32[8,2560]{1,0:T(8,128)}) custom-call(s32[16]{0:T(128)} %fusion.49.pair, bf16[16,240,128]{2,1,0:T(8,128)(2,1)} %get-tuple-element.50.recv), custom_call_target="tpu_custom_call" | custom-call | tf_op jit(solution)/shard_map/attend/pallas_call | solution.py:326
  85.2 15.6 %to_tokens.1 = bf16[16,80,128]{2,1,0:T(8,128)(2,1)} custom-call(bf16[16,80,128]{2,1,0:T(8,128)(2,1)} %get-tuple-element.51.refs_0_), custom_call_target="tpu_custom_call" | custom-call | tf_op jit(solution)/shard_map/to_tokens/pallas_call | solution.py:183
  100.9 1.2 copy.38
  103.5 6.9 %all-gather.2.cloned.1.call-done = bf16[1024,4480]{1,0:T(8,128)(2,1)} async-done(((bf16[32,4480]{1,0:T(8,128)(2,1)}), bf16[1024,4480]{1,0:T(8,128)(2,1)}) %all-gather.2.cloned.1.call-update) | async-done | bytes 9175056 | tf_op jit(solution)/shard_map/all_gather | solution.py:551
  110.4 2.2 multiply_reduce_fusion.2
  112.7 0.9 multiply_convert_fusion.3.refs_0_
  113.5 18.8 %gather_ffn.1 = bf16[4,160,1024]{2,1,0:T(8,128)(2,1)} custom-call(bf16[160,1024]{1,0:T(8,128)(2,1)} %multiply_convert_fusion.3.refs_0_), custom_call_target="tpu_custom_call" | custom-call | tf_op jit(solution)/shard_map/gather_ffn/pallas_call | solution.py:183
  132.3 1.7 slice-done.3
  134.0 3.5 reshape_reshape.11
  137.5 3.2 fusion.55
  145.4 0.9 slice-done.1
  146.8 3.2 fusion.2
  150.0 3.2 multiply_convert_fusion.2
  156.0 1.7 pad_maximum_fusion.2
  157.7 4.8 %convert_element_type.89 = bf16[32,9,16,2,128]{4,3,2,1,0:T(2,128)(2,1)S(1)} reshape(bf16[4,1152,256]{2,1,0:T(8,128)(2,1)} %pad_maximum_fusion.2) | data formatting | bytes 4718592 | tf_op jit(solution)/shard_map/convert_element_type | solution.py:599
  162.5 1.6 copy.49
  164.1 1.2 copy.96
  166.2 5.5 %convolution_convert_fusion = bf16[1024,2304]{1,0:T(8,128)(2,1)} fusion(bf16[640,1024]{1,0:T(8,128)(2,1)S(1)} %bitcast.181, bf16[640,1152]{1,0:T(8,128)(2,1)S(1)} %copy-done.31, bf16[640,1152]{1,0:T(8,128)(2,1)S(1)} %copy-done.30), kind=kOutput, calls=%fused_computation.1 | convolution fusion | flops 3028156416 | bytes 8978432 | tf_op jit(solution)/shard_map/rd,rf->df/dot_general | solution.py:591
  171.8 5.6 %pad_maximum_fusion = bf16[1024,3456]{1,0:T(8,128)(2,1)} fusion(bf16[1024,1152]{1,0:T(8,128)(2,1)S(1)} %bitcast.165, bf16[1024,2304]{1,0:T(8,128)(2,1)} %convolution_convert_fusion), kind=kLoop, calls=%fused_computation | loop fusion | flops 14155776 | bytes 14155776 | tf_op jit(solution)/shard_map/concatenate | solution.py:602
  177.4 1.1 copy-done.3
  178.5 1.2 reshape_reshape.12
  179.7 1.7 copy.97
  181.4 2.7 reshape.207
  184.1 1.2 reshape.206
  185.3 1.2 reshape.205
  186.5 1.2 reshape.204
  187.8 7.9 %fusion.13 = bf16[640,1024]{1,0:T(8,128)(2,1)} fusion(bf16[1024,4480]{1,0:T(8,128)(2,1)} %all-gather.2.cloned.1.call-done, bf16[640,1152]{1,0:T(8,128)(2,1)} %get-tuple-element.82, bf16[640,1152]{1,0:T(8,128)(2,1)} %get-tuple-element.81), kind=kOutput, calls=%fused_computation.32 | convolution fusion | flops 3026452480 | bytes 8978432 | tf_op jit(solution)/shard_map/rf,df->rd/dot_general | solution.py:590
  195.6 18.5 %sum_ffn.1 = bf16[4,160,1024]{2,1,0:T(8,128)(2,1)} custom-call(bf16[4,160,1024]{2,1,0:T(8,128)(2,1)} %bitcast.183), custom_call_target="tpu_custom_call" | custom-call | tf_op jit(solution)/shard_map/sum_ffn/pallas_call | solution.py:183
  214.2 1.7 convert_reduce_fusion.2
  216.9 2.5 fusion.19
  220.5 0.9 copy.45.refs_0_
  221.4 2.2 convolution_convert_fusion.5
  223.7 1.7 convolution_convert_fusion.6
  226.6 1.3 pad_maximum_fusion.7.refs_1_
  227.9 24.5 %to_heads_back.1 = (bf16[16,80,128]{2,1,0:T(8,128)(2,1)}, bf16[4,160,1024]{2,1,0:T(8,128)(2,1)}) custom-call(bf16[16,80,128]{2,1,0:T(8,128)(2,1)} %copy.45.refs_0_, bf16[4,160,1024]{2,1,0:T(8,128)(2,1)} %pad_maximum_fusion.7.refs_1_), custom_call_target="tpu_custom_call" | custom-call | tf_op jit(solution)/shard_map/to_heads_back/pallas_call | solution.py:183
  252.4 17.9 %attend_back.1.refs_0_ = bf16[16,240,128]{2,1,0:T(8,128)(2,1)} custom-call(s32[16]{0:T(128)} %fusion.49.pair, bf16[16,80,128]{2,1,0:T(8,128)(2,1)} %get-tuple-element.55.recv, bf16[2560,128]{1,0:T(8,128)(2,1)} %get-tuple-element.56.q_s, bf16[2560,128]{1,0:T(8,128)(2,1)} %get-tuple-element.57.k_s, bf16[2560,128]{1,0:T(8,128)(2,1)} %get-tuple-element.58.v_s, ...), custom_call_target="tpu_custom_call" | custom-call | tf_op jit(solution)/shard_map/attend_back/pallas_call | solution.py:396
  270.2 25.4 %to_tokens_back.1 = (bf16[16,240,128]{2,1,0:T(8,128)(2,1)}, bf16[4,160,1024]{2,1,0:T(8,128)(2,1)}, bf16[4,160,256]{2,1,0:T(8,128)(2,1)}, f32[32,8,128]{2,1,0:T(8,128)}) custom-call(bf16[16,240,128]{2,1,0:T(8,128)(2,1)} %attend_back.1.refs_0_, bf16[160,1024]{1,0:T(8,128)(2,1)} %copy-done.16, bf16[4,160,256]{2,1,0:T(8,128)(2,1)} %bitcast.184, f32[8,128]{1,0:T(8,128)} %bitcast.208), custom_call_target="tpu_custom_call" | custom-call | tf_op jit(solution)/shard_map/to_tokens_back/pallas_call | solution.py:183
  295.7 2.0 fusion.16
  298.1 0.9 copy.48
  299.0 10.0 %project_back.1 = (bf16[640,1024]{1,0:T(8,128)(2,1)}, bf16[1024,512]{1,0:T(8,128)(2,1)}, f32[8,128]{1,0:T(8,128)}, f32[1,1024]{1,0:T(1,128)}) custom-call(s32[12]{0:T(128)} %concatenate.39.blocks, bf16[16,240,128]{2,1,0:T(8,128)(2,1)} %get-tuple-element.61.recv, f32[640,384]{1,0:T(8,128)} %get-tuple-element.62.raw, bf16[640,1024]{1,0:T(8,128)(2,1)} %bitcast.172, ...), custom_call_target="tpu_custom_call" | custom-call | tf_op jit(solution)/shard_map/project_back/pallas_call | solution.py:459
  309.7 1.3 pad_maximum_fusion.13.refs_3_
  311.0 32.3 %sum_qkv.1 = (bf16[4,160,1024]{2,1,0:T(8,128)(2,1)}, bf16[32,32,512]{2,1,0:T(8,128)(2,1)}, bf16[32,32,256]{2,1,0:T(8,128)(2,1)}, f32[32,16,128]{2,1,0:T(8,128)}) custom-call(bf16[4,160,1024]{2,1,0:T(8,128)(2,1)} %bitcast.182, bf16[32,32,512]{2,1,0:T(8,128)(2,1)} %bitcast.186, bf16[32,32,256]{2,1,0:T(8,128)(2,1)} %bitcast.179, ...), custom_call_target="tpu_custom_call" | custom-call | tf_op jit(solution)/shard_map/sum_qkv/pallas_call | solution.py:183
  343.3 1.0 reduce_sum.132
  344.3 1.4 reduce_sum.131
  345.7 1.1 reduce_sum.134
  347.4 1.6 convert_reduce_fusion
  349.3 1.6 convert_reduce_fusion.1
  351.7 1.0 fusion.40
  352.7 0.9 slice.145
  353.8 0.9 slice.144
  356.0 20.4 %gather_out.1 = (bf16[4,32,2816]{2,1,0:T(8,128)(2,1)}, f32[4,24,128]{2,1,0:T(8,128)}, bf16[4,176,256]{2,1,0:T(8,128)(2,1)}) custom-call(bf16[32,2816]{1,0:T(8,128)(2,1)} %pad_maximum_fusion.9.refs_0_, f32[24,128]{1,0:T(8,128)} %pad_maximum_fusion.12.refs_1_, bf16[176,256]{1,0:T(8,128)(2,1)} %pad_maximum_fusion.10.refs_2_), custom_call_target="tpu_custom_call" | custom-call | tf_op jit(solution)/shard_map/gather_out/pallas_call | solution.py:183
  376.5 1.3 convert_element_type.90
  382.4 0.9 copy.62
  383.3 0.9 copy.63
  384.1 0.9 copy.64
  (139 shorter events, 28.1 us)
Async XLA Ops:
  7.2 1.0 copy-start
  7.2 36.6 %copy-start.23 = (bf16[32,1024]{1,0:T(8,128)(2,1)S(1)}, bf16[32,1024]{1,0:T(8,128)(2,1)}, u32[]{:S(2)}) copy-start(bf16[32,1024]{1,0:T(8,128)(2,1)} %param.21) | copy-start | bytes 196612
  7.2 39.8 %copy-start.26 = (f32[64]{0:T(128)S(1)}, f32[64]{0:T(128)}, u32[]{:S(2)}) copy-start(f32[64]{0:T(128)} %param.26) | copy-start | bytes 772
  7.2 39.8 %copy-start.27 = (f32[64]{0:T(128)S(1)}, f32[64]{0:T(128)}, u32[]{:S(2)}) copy-start(f32[64]{0:T(128)} %param.27) | copy-start | bytes 772
  7.2 103.2 %all-gather.2.cloned.1.call-start = ((), (), s32[]{:S(2)}) async-start(), calls=%async_computation.1 | async-start | bytes 9461760 | tf_op jit(solution)/shard_map/all_gather | solution.py:551
  8.2 35.6 %collective-permute-start = (bf16[144,256]{1,0:T(8,128)(2,1)S(1)}, bf16[144,256]{1,0:T(8,128)(2,1)S(1)}, u32[]{:S(2)}, u32[]{:S(2)}) collective-permute-start(bf16[144,256]{1,0:T(8,128)(2,1)S(1)} %constant_dynamic-slice_fusion), channel_id=1, source_target_pairs={{0,0},{8,32},{16,64},{24,96},{32,8},{40,40},{48,72},{56,104},{64,1... | collective-permute-start | bytes 221192 | tf_op jit(solution)/shard_map/ppermute | solution.py:534
  44.6 308.1 %reduce-scatter.2.cloned.1.call-start = ((), (), s32[]{:S(2)}) async-start(), calls=%async_computation.2 | async-start | bytes 7299072 | tf_op jit(solution)/shard_map/reduce_scatter | solution.py:601
  74.7 35.7 %copy-start.10 = (bf16[1,160,1024]{2,1,0:T(8,128)(2,1)S(1)}, bf16[1,160,1024]{2,1,0:T(8,128)(2,1)}, u32[]{:S(2)}) copy-start(bf16[1,160,1024]{2,1,0:T(8,128)(2,1)} %param.16) | copy-start | bytes 983044
  102.7 0.8 copy-start.2
  102.7 10.0 %copy-start.25 = (f32[1024]{0:T(1024)S(1)}, f32[1024]{0:T(1024)}, u32[]{:S(2)}) copy-start(f32[1024]{0:T(1024)} %param.28) | copy-start | bytes 12292
  132.3 1.7 slice-start.3
  141.3 2.0 copy-start.8
  141.3 2.0 copy-start.17
  142.0 2.0 copy-start.4
  142.0 3.3 slice-start
  142.7 2.0 copy-start.6
  143.3 6.7 %copy-start.12 = (bf16[8,9,16,2,128]{4,3,2,1,0:T(2,128)(2,1)}, bf16[8,9,16,2,128]{4,3,2,1,0:T(2,128)(2,1)S(1)}, u32[]{:S(2)}) copy-start(bf16[8,9,16,2,128]{4,3,2,1,0:T(2,128)(2,1)S(1)} %copy.43) | copy-start | bytes 1769476
  143.4 2.9 slice-start.1
  144.0 2.4 slice-start.2
  144.7 2.1 copy-start.13
  153.3 2.0 copy-start.28
  164.0 1.3 copy-start.14
  164.0 1.8 copy-start.30
  164.0 2.2 copy-start.31
  177.4 1.1 copy-start.3
  178.5 5.6 %copy-start.7 = (bf16[8,9,16,2,128]{4,3,2,1,0:T(2,128)(2,1)S(1)}, bf16[8,9,16,2,128]{4,3,2,1,0:T(2,128)(2,1)}, u32[]{:S(2)}) copy-start(bf16[8,9,16,2,128]{4,3,2,1,0:T(2,128)(2,1)} %copy-done.6) | copy-start | bytes 1769476
  178.5 6.8 %copy-start.5 = (bf16[8,9,16,2,128]{4,3,2,1,0:T(2,128)(2,1)S(1)}, bf16[8,9,16,2,128]{4,3,2,1,0:T(2,128)(2,1)}, u32[]{:S(2)}) copy-start(bf16[8,9,16,2,128]{4,3,2,1,0:T(2,128)(2,1)} %copy-done.4) | copy-start | bytes 1769476
  178.5 8.0 %copy-start.9 = (bf16[8,9,16,2,128]{4,3,2,1,0:T(2,128)(2,1)S(1)}, bf16[8,9,16,2,128]{4,3,2,1,0:T(2,128)(2,1)}, u32[]{:S(2)}) copy-start(bf16[8,9,16,2,128]{4,3,2,1,0:T(2,128)(2,1)} %copy-done.8) | copy-start | bytes 1769476
  195.6 21.0 %copy-start.15 = (bf16[1,160,1024]{2,1,0:T(8,128)(2,1)S(1)}, bf16[1,160,1024]{2,1,0:T(8,128)(2,1)}, u32[]{:S(2)}) copy-start(bf16[1,160,1024]{2,1,0:T(8,128)(2,1)} %param.29) | copy-start | bytes 983044
  216.9 3.6 copy-start.16
  221.4 2.3 copy-start.29
  221.4 4.0 %copy-start.19 = (bf16[1152,256,1]{1,0,2:T(8,128)(2,1)S(1)}, bf16[1152,256,1]{1,0,2:T(8,128)(2,1)}, u32[]{:S(2)}) copy-start(bf16[1152,256,1]{1,0,2:T(8,128)(2,1)} %reshape.205) | copy-start | bytes 1769476
  223.7 2.3 copy-start.18
  299.0 10.0 %copy-start.22 = (f32[1024]{0:T(1024)S(1)}, f32[1024]{0:T(1024)}, u32[]{:S(2)}) copy-start(f32[1024]{0:T(1024)} %param.25) | copy-start | bytes 12292
  299.0 10.7 %copy-start.21 = (f32[32,8,128]{2,1,0:T(8,128)S(1)}, f32[32,8,128]{2,1,0:T(8,128)}, u32[]{:S(2)}) copy-start(f32[32,8,128]{2,1,0:T(8,128)} %get-tuple-element.72) | copy-start | bytes 393220
  343.3 5.8 %copy-start.11 = (bf16[1,160,1024]{2,1,0:T(8,128)(2,1)S(1)}, bf16[1,160,1024]{2,1,0:T(8,128)(2,1)}, u32[]{:S(2)}) copy-start(bf16[1,160,1024]{2,1,0:T(8,128)(2,1)} %param.16) | copy-start | bytes 983044
  376.5 1.4 copy-start.20
  377.8 0.8 copy-start.24
  378.0 7.0 %copy-start.1 = (bf16[144,1024]{1,0:T(8,128)(2,1)S(1)}, bf16[144,1024]{1,0:T(8,128)(2,1)}, u32[]{:S(2)}) copy-start(bf16[144,1024]{1,0:T(8,128)(2,1)} %param.24) | copy-start | bytes 884740
Sparse Core Ops, SparseCore 0:
  44.7 65.6 all-gather.1
  177.6 90.9 reduce-scatter.1

commit v3 on v2

--- a/solution.py
+++ b/solution.py
@@ -412,6 +412,224 @@
         compiler_params=pltpu.CompilerParams(vmem_limit_bytes=VMEM_BYTES),
         name="attend_back",
     )(pair, recv, q_s, k_s, v_s, o_t, inv)
+
+
+def middle_kernel(
+    parts,
+    tokens,
+    cot,
+    g_ffn,
+    wide,
+    mid_o,
+    result_o,
+    dw_o,
+    gmid_o,
+    branch_o,
+    mixed_o,
+    back_o,
+    gain_o,
+    w_o,
+    w_gu,
+    dnp,
+    w_dn,
+    h_all,
+    part,
+    gparts,
+    gu_s,
+    dh_s,
+    ggu,
+    hid,
+    h_t,
+    hid_t,
+    wsem,
+    ss1,
+    rs1,
+    ss2,
+    rs2,
+):
+    me, z, y, c = coords()
+    barrier = pltpu.get_barrier_semaphore()
+    for k in range(1, NX):
+        pl.semaphore_signal(
+            barrier, inc=1, device_id=(lax.rem(me + k, NX), z, y, c), device_id_type=MESH
+        )
+    loads = [
+        pltpu.make_async_copy(wide.at[:, pl.ds(at, width)], there, wsem.at[i])
+        for i, (at, width, there) in enumerate(
+            ((0, D, w_o), (D, 2 * FX, w_gu), (D + 2 * FX, FX, dnp))
+        )
+    ]
+    for load in loads:
+        load.start()
+    m = low_half((BLK, 2 * HD))
+    for p in range(8):
+        a, b = parts[2 * p, :, :].astype(F32), parts[2 * p + 1, :, :].astype(F32)
+        at = slice((p % 2) * 128, (p % 2) * 128 + 128)
+        mixed_o[p // 2, :BLK, at] = jnp.where(m, a, swap(b)).astype(BF16)
+        mixed_o[p // 2, BLK:, at] = jnp.where(m, swap(a), b).astype(BF16)
+    loads[0].wait()
+    middle = tokens[...].astype(F32)
+    for q in range(NX):
+        middle = middle + nn(mixed_o[q, :, :], w_o[q * QX : (q + 1) * QX, :])
+    mid_o[...] = middle
+    r = lax.rsqrt(jnp.mean(middle * middle, axis=-1, keepdims=True) + EPSILON)
+    h_all[me] = (middle * r * g_ffn[...]).astype(BF16)
+    pl.semaphore_wait(barrier, NX - 1)
+
+    def send_h(t, place):
+        return pltpu.make_async_remote_copy(
+            src_ref=h_all.at[me],
+            dst_ref=h_all.at[place],
+            send_sem=ss1.at[t],
+            recv_sem=rs1.at[place],
+            device_id=(t, z, y, c),
+            device_id_type=MESH,
+        )
+
+    def send_grad(t, place):
+        return pltpu.make_async_remote_copy(
+            src_ref=part.at[t],
+            dst_ref=gparts.at[place],
+            send_sem=ss2.at[t],
+            recv_sem=rs2.at[place],
+            device_id=(t, z, y, c),
+            device_id_type=MESH,
+        )
+
+    for k in (1, 3, 2):
+        send_h(lax.rem(me + k, NX), me).start()
+    loads[1].wait()
+    loads[2].wait()
+    for o in range(32):
+        for rg in range(9):
+            for l in range(2):
+                row = (o % 8) * 144 + rg * 16
+                w_dn[o // 8, row : row + 16, l * 128 : l * 128 + 128] = dnp[
+                    o * 32 + l * 16 : o * 32 + l * 16 + 16, rg * 128 : rg * 128 + 128
+                ]
+
+    def block(k, carry):
+        t = lax.rem(me + k + k // 2 - 2 * (k // 2) * lax.rem(k, 2), NX)
+
+        @pl.when(k > 0)
+        def _():
+            send_h(t, t).wait_recv()
+
+        rows = pl.ds(pl.multiple_of(t * ROWS, ROWS), ROWS)
+        gu_s[...] = nn(h_all[t], w_gu[...])
+        cot_t = cot[t]
+        grad_hidden = nt(cot_t[:, :256], w_dn[0])
+        for q in range(1, NX):
+            grad_hidden = grad_hidden + nt(cot_t[:, q * 256 : (q + 1) * 256], w_dn[q])
+        dh_s[...] = grad_hidden
+        for j in range(FX // 128):
+            at, above = slice(j * 128, j * 128 + 128), slice(FX + j * 128, FX + j * 128 + 128)
+            gate, up, dh = gu_s[:, at], gu_s[:, above], dh_s[:, at]
+            sig = jax.nn.sigmoid(gate)
+            silu = gate * sig
+            hid[rows, at] = (silu * up).astype(BF16)
+            ggu[rows, at] = (dh * up * (sig * (1.0 + gate * (1.0 - sig)))).astype(BF16)
+            ggu[rows, above] = (dh * silu).astype(BF16)
+        part[t] = nt(ggu[rows, :], w_gu[...]).astype(BF16)
+
+        @pl.when(k > 0)
+        def _():
+            send_grad(t, me).start()
+
+        hidden = hid[rows, :]
+        for q in range(NX):
+            result_o[t, :, q * 256 : (q + 1) * 256] = nn(hidden, w_dn[q]).astype(BF16)
+        return carry
+
+    lax.fori_loop(0, NX, block, 0)
+
+    h_t[...] = h_all[...].reshape(NX * ROWS, D).T
+
+    def columns(j, carry):
+        at = pl.ds(pl.multiple_of(j * 256, 256), 256)
+        dw_o[:, at] = nn(h_t[...], ggu[:, at]).astype(BF16)
+        return carry
+
+    lax.fori_loop(0, 2 * FX // 256, columns, 0)
+    hid_t[...] = hid[...].T
+    for q in range(NX):
+        cot_q = cot[:, :, q * 256 : (q + 1) * 256].reshape(NX * ROWS, 256)
+        grad = nn(hid_t[...], cot_q).astype(BF16)
+        for o in range(8):
+            for rg in range(9):
+                for l in range(2):
+                    row, there = o * 144 + rg * 16, (q * 8 + o) * 32 + l * 16
+                    dw_o[there : there + 16, 2 * FX + rg * 128 : 2 * FX + rg * 128 + 128] = grad[
+                        row : row + 16, l * 128 : l * 128 + 128
+                    ]
+
+    grad_h = part[me].astype(F32)
+    for k in (1, 3, 2):
+        t = lax.rem(me + k, NX)
+        send_grad(t, t).wait_recv()
+        grad_h = grad_h + gparts[t].astype(F32)
+    for k in (1, 3, 2):
+        t = lax.rem(me + k, NX)
+        send_h(t, me).wait_send()
+        send_grad(t, me).wait_send()
+    middle = mid_o[...]
+    r = lax.rsqrt(jnp.mean(middle * middle, axis=-1, keepdims=True) + EPSILON)
+    weighted = grad_h * g_ffn[...]
+    inner = jnp.mean(weighted * middle, axis=-1, keepdims=True)
+    gain_o[...] = jnp.sum(grad_h * middle * r, axis=0, keepdims=True)
+    grad_middle = cot[me].astype(F32) + r * weighted - middle * (r * r * r) * inner
+    gmid_o[...] = grad_middle
+    branch_o[...] = grad_middle.astype(BF16)
+    for q in range(NX):
+        grad = nt(branch_o[...], w_o[q * QX : (q + 1) * QX, :]).astype(BF16).astype(F32)
+        for p in range(2):
+            top, bottom = grad[:BLK, p * 128 : p * 128 + 128], grad[BLK:, p * 128 : p * 128 + 128]
+            back_o[4 * q + 2 * p, :, :] = jnp.where(m, top, swap(bottom)).astype(BF16)
+            back_o[4 * q + 2 * p + 1, :, :] = jnp.where(m, swap(top), bottom).astype(BF16)
+
+
+def middle_part(number, parts, tokens, cot, g_ffn, wide):
+    vmem = pl.BlockSpec(memory_space=pltpu.VMEM)
+    blocks = (NX, ROWS, D)
+    return pl.pallas_call(
+        middle_kernel,
+        in_specs=[vmem] * 4 + [pl.BlockSpec(memory_space=pl.ANY)],
+        out_specs=[vmem] * 8,
+        out_shape=[
+            jax.ShapeDtypeStruct((ROWS, D), F32),
+            jax.ShapeDtypeStruct(blocks, BF16),
+            jax.ShapeDtypeStruct((D, 3 * FX), BF16),
+            jax.ShapeDtypeStruct((ROWS, D), F32),
+            jax.ShapeDtypeStruct((ROWS, D), BF16),
+            jax.ShapeDtypeStruct((NX, ROWS, QX), BF16),
+            jax.ShapeDtypeStruct((16, BLK, 2 * HD), BF16),
+            jax.ShapeDtypeStruct((1, D), F32),
+        ],
+        scratch_shapes=[
+            pltpu.VMEM((D, D), BF16),
+            pltpu.VMEM((D, 2 * FX), BF16),
+            pltpu.VMEM((D, FX), BF16),
+            pltpu.VMEM((4, FX, D // 4), BF16),
+            pltpu.VMEM(blocks, BF16),
+            pltpu.VMEM(blocks, BF16),
+            pltpu.VMEM(blocks, BF16),
+            pltpu.VMEM((ROWS, 2 * FX), F32),
+            pltpu.VMEM((ROWS, FX), F32),
+            pltpu.VMEM((NX * ROWS, 2 * FX), BF16),
+            pltpu.VMEM((NX * ROWS, FX), BF16),
+            pltpu.VMEM((D, NX * ROWS), BF16),
+            pltpu.VMEM((FX, NX * ROWS), BF16),
+            pltpu.SemaphoreType.DMA((3,)),
+            pltpu.SemaphoreType.DMA((NX,)),
+            pltpu.SemaphoreType.DMA((NX,)),
+            pltpu.SemaphoreType.DMA((NX,)),
+            pltpu.SemaphoreType.DMA((NX,)),
+        ],
+        compiler_params=pltpu.CompilerParams(
+            collective_id=number, has_side_effects=True, vmem_limit_bytes=VMEM_BYTES
+        ),
+        name="middle_part",
+    )(parts, tokens, cot, g_ffn, wide)
 
 
 def project_back_kernel(blocks, recv, raw, h, w, cos_t, sin_t, g_q, g_k, gh, dw, gains, attn, low):
@@ -533,7 +751,7 @@
     swap_xz = [(a * 4 + b, b * 4 + a) for a in range(4) for b in range(4)]
     down_part = lax.ppermute(columns_of(w_down, x, D // 4), ("seq", "ctx_0"), swap_xz)
     mine = jnp.concatenate(
-        [columns_of(w_gate, x, FX), columns_of(w_up, x, FX), w_out, by_tiles(down_part[None])[0]],
+        [w_out, columns_of(w_gate, x, FX), columns_of(w_up, x, FX), by_tiles(down_part[None])[0]],
         axis=1,
     )
 
@@ -549,8 +767,6 @@
     )
     h_all, mine = lax.optimization_barrier((h_all, mine))
     wide = lax.all_gather(mine, CTX_FSDP, axis=0, tiled=True)
-    w_gu, full_out = wide[:, : 2 * FX], wide[:, 2 * FX : 2 * FX + D]
-    w_dn = from_tiles(wide[:, 2 * FX + D :].reshape(32, 32, FX)).reshape(4, FX, D // 4)
     h_all = h_all.reshape(NX * ROWS, D)
     w_qkv = w_qkv.reshape(D, QX + 2 * KX)
     pairs_all = pairs_all[:, 0, :16]
@@ -563,59 +779,13 @@
     recv, cot_all = exchange(2, "to_heads", ("c", "a2a", send), ("x", "ag", cotangent[0]))
     heads_out, q_s, k_s, v_s, o_t, inv = attend(pair, recv)
     (mixed_parts,) = exchange(3, "to_tokens", ("t", "a2a", heads_out))
-    mixed = mixed_parts.reshape(16, BLK, 2, HD).transpose(2, 1, 0, 3).reshape(ROWS, D)
-    branch = jnp.dot(mixed, full_out, preferred_element_type=F32)
-    middle = inputs + branch
-    normed_ffn, inv_ffn = rms_rows(middle, g_ffn)
-    (h4,) = exchange(4, "gather_ffn", ("x", "ag", normed_ffn.astype(BF16)))
-    h4 = h4.reshape(NX * ROWS, D)
-    cot4 = cot_all.reshape(NX * ROWS, D)
-
-    gate_up = jnp.dot(h4, w_gu, preferred_element_type=F32)
-    gate_act, up_act = gate_up[:, :FX], gate_up[:, FX:]
-    sigmoid_gate = jax.nn.sigmoid(gate_act)
-    silu_gate = gate_act * sigmoid_gate
-    hidden = (silu_gate * up_act).astype(BF16)
-    grad_hidden = sum(
-        jnp.einsum(
-            "rd,fd->rf", cot4[:, q * 256 : (q + 1) * 256], w_dn[q], preferred_element_type=F32
-        )
-        for q in range(4)
-    )
-    grad_gate = (
-        grad_hidden * up_act * (sigmoid_gate * (1.0 + gate_act * (1.0 - sigmoid_gate)))
-    ).astype(BF16)
-    grad_up = (grad_hidden * silu_gate).astype(BF16)
-    grad_gu = jnp.concatenate([grad_gate, grad_up], axis=1)
-    grad_h4 = jnp.einsum("rf,df->rd", grad_gu, w_gu, preferred_element_type=F32).astype(BF16)
-    grad_w_gu = jnp.einsum("rd,rf->df", h4, grad_gu, preferred_element_type=F32).astype(BF16)
-    grad_w_d = jnp.stack(
-        [
-            jnp.einsum(
-                "rf,rd->fd", hidden, cot4[:, q * 256 : (q + 1) * 256], preferred_element_type=F32
-            )
-            for q in range(4)
-        ]
-    ).astype(BF16)
-    grad_w_d = by_tiles(grad_w_d.reshape(32, FF // 32, D // 4)).reshape(D, FX)
-    sums = lax.psum_scatter(
-        jnp.concatenate([grad_w_gu, grad_w_d], axis=1), CTX_FSDP, scatter_dimension=0, tiled=True
-    )
+    middle, result4, grad_w_ffn, grad_middle, grad_branch, mixed, back_parts, gain_ffn = middle_part(
+        4, mixed_parts, tokens[0], cot_all, g_ffn[None], wide
+    )
+    sums = lax.psum_scatter(grad_w_ffn, CTX_FSDP, scatter_dimension=0, tiled=True)
     sum_gu, sum_d = sums[:, : 2 * FX], from_tiles(sums[:, 2 * FX :][None])[0]
-    (grad_h_parts,) = exchange(5, "sum_ffn", ("x", "a2a", grad_h4.reshape(NX, ROWS, D)))
-    result4 = jnp.concatenate(
-        [jnp.dot(hidden, w_dn[q], preferred_element_type=F32) for q in range(4)], axis=1
-    ).astype(BF16)
-
-    grad_h_ffn = jnp.sum(grad_h_parts.astype(F32), axis=0)
-    grad_out = cotangent[0].astype(F32)
-    grad_middle_norm, ffn_gain_terms = rms_rows_back(middle, g_ffn, inv_ffn, grad_h_ffn)
-    grad_middle = grad_out + grad_middle_norm
-    grad_branch = grad_middle.astype(BF16)
-    grad_mixed = jnp.einsum("rd,hd->rh", grad_branch, full_out, preferred_element_type=F32).astype(BF16)
-    back_parts = grad_mixed.reshape(2, BLK, 16, HD).transpose(2, 1, 0, 3).reshape(16, BLK, 2 * HD)
     recv_g, result_parts = exchange(
-        6, "to_heads_back", ("r", "a2a", back_parts), ("x", "a2a", result4.reshape(NX, ROWS, D))
+        6, "to_heads_back", ("r", "a2a", back_parts), ("x", "a2a", result4)
     )
     output = (middle + jnp.sum(result_parts.astype(F32), axis=0)).astype(BF16)[None]
 
@@ -625,8 +795,8 @@
         "to_tokens_back",
         ("c", "a2a", sends_back),
         ("x", "ag", grad_branch),
-        ("x", "a2a", mixed.reshape(ROWS, NX, QX).transpose(1, 0, 2)),
-        ("p", "ag", jnp.sum(ffn_gain_terms, axis=0).reshape(8, 128)),
+        ("x", "a2a", mixed),
+        ("p", "ag", gain_ffn.reshape(8, 128)),
     )
     grad_h_qkv, grad_w_qkv, gains_qk, gains_attn = project_back(
         blocks, recv_back, raw, h_all, w_qkv, cos_t, sin_t, gq2, gk2

time: 400 us -> 321 us (0.80); the launches traced: 392 us -> 320 us
  matrix products: 36.4 us -> 2.03 us
  local copies, waits for them, and re-layouts: 52.4 us -> 18.2 us
  other arithmetic: 31.8 us -> 17.7 us
  Pallas kernels: 244 us -> 252 us
    pallas_call x0 -> x1, Pallas kernels: none -> 38.2 us  [middle_part(): pl.pallas_call(middle_kernel, in_specs=[vmem] * 4 + [pl.BlockSpec(memory_...]
    dot_general x17 -> x0, matrix products: 34.3 us -> none  [the longest x1 7.87 us: body(): jnp.einsum('rf,df->rd', grad_gu, w_gu, preferred_element_type=F32)]
    pallas_call x9 -> x7, Pallas kernels: 198 us -> 168 us  [exchange(): pl.pallas_call(functools.partial(exchange_kernel, items), out_shape=outs,...]
    slice x7 -> x0, local copies, waits for them, and re-layouts: 7.43 us -> none  [the longest x5 5.77 us: body(): w_dn[q]]
    concatenate x3 -> x1, other arithmetic: 7.65 us -> 0.73 us  [body(): jnp.concatenate([w_out, columns_of(w_gate, x, FX), columns_of(w_up, x, FX...]
    squeeze x4 -> x0, local copies, waits for them, and re-layouts: 6.36 us -> none  [body(): w_dn[q]]
    convert_element_type x2 -> x0, local copies, waits for them, and re-layouts: 6.33 us -> none  [body(): grad_w_d = jnp.stack([jnp.einsum('rf,rd->fd', hidden, cot4[:, q * 256:(q...]
  transfers between devices with their start and end apart: 3 -> 3, of which waited for: 1 -> 1; matrix products, arithmetic and copies ran while one was open for 15% -> 7% of each run, Pallas kernels for 52% -> 60%
where the time goes in v3:
time: 321 us; the launch traced here: 320 us
  Pallas kernels  252 us (79%)
  local copies, waits for them, and re-layouts  18.2 us (6%)
  other arithmetic  17.7 us (6%)
  between operations  14.5 us (5%)
  waiting for transfers between devices  9.77 us (3%)
  starting transfers between devices  5.81 us (2%)
    pallas_call x7, Pallas kernels, exchange(): pl.pallas_call(functools.partial(exchange_kernel, items), out_shape=outs,...  168 us
    pallas_call x1, Pallas kernels, middle_part(): pl.pallas_call(middle_kernel, in_specs=[vmem] * 4 + [pl.BlockSpec(memory_...  38.2 us
    pallas_call x1, Pallas kernels, attend_back(): pl.pallas_call(attend_back_kernel, grid_spec=pltpu.PrefetchScalarGridSpec...  18 us
    pallas_call x1, Pallas kernels, attend(): pl.pallas_call(attend_kernel, grid_spec=pltpu.PrefetchScalarGridSpec(num_...  10.4 us
    pallas_call x1, Pallas kernels, project_back(): pl.pallas_call(project_back_kernel, grid_spec=pltpu.PrefetchScalarGridSpe...  10.1 us
    all_gather x1, waiting for transfers between devices, body(): wide = lax.all_gather(mine, CTX_FSDP, axis=0, tiled=True)  9.73 us
    pallas_call x1, Pallas kernels, project(): pl.pallas_call(project_kernel, grid_spec=pltpu.PrefetchScalarGridSpec(num...  6.93 us
  transfers between devices with their start and end apart: 3, of which 1 were waited for; matrix products, arithmetic and copies ran while one was open for 7% of the time, Pallas kernels for 60%

profile of v3, /device:TPU:4, one launch (start us, length us, event | category | flops | bytes accessed | tf_op | source)
XLA Modules:
  0.0 319.9 jit_solution(11605961682788894141)
XLA Ops:
  7.3 0.9 copy-done
  8.2 5.7 %collective-permute-start = (bf16[144,256]{1,0:T(8,128)(2,1)S(1)}, bf16[144,256]{1,0:T(8,128)(2,1)S(1)}, u32[]{:S(2)}, u32[]{:S(2)}) collective-permute-start(bf16[144,256]{1,0:T(8,128)(2,1)S(1)} %constant_dynamic-slice_fusion), channel_id=1, source_target_pairs={{0,0},{8,32},{16,64},{24,96},{32,8},{40,40},{48,72},{56,104},{64,1... | collective-permute-start | bytes 221192 | tf_op jit(solution)/shard_map/ppermute | solution.py:752
  13.9 1.1 fusion.1
  15.0 1.3 pad.4.refs_2_
  16.3 0.7 constant_dynamic-slice_fusion.6
  17.0 1.9 fusion.3.refs_0_
  18.9 0.7 constant_dynamic-slice_fusion.4
  19.6 0.9 constant_dynamic-slice_fusion.1
  20.5 0.6 pad_maximum_fusion.3.refs_1_
  21.2 22.6 %gather_in.1 = (bf16[4,160,1024]{2,1,0:T(8,128)(2,1)}, bf16[32,32,512]{2,1,0:T(8,128)(2,1)}, s32[4,8,128]{2,1,0:T(8,128)}) custom-call(bf16[160,1024]{1,0:T(8,128)(2,1)} %fusion.3.refs_0_, bf16[32,512]{1,0:T(8,128)(2,1)} %pad_maximum_fusion.3.refs_1_, s32[8,128]{1,0:T(8,128)} %pad.4.refs_2_), custom_call_target="tpu_custom_call" | custom-call | tf_op jit(solution)/shard_map/gather_in/pallas_call | solution.py:183
  43.9 0.7 pad_maximum_fusion
  44.8 0.7 slice.51
  45.5 0.2 dynamic-slice_reduce_fusion
  45.8 0.1 copy.33
  45.9 0.1 reshape.117
  46.0 0.6 concatenate.28.blocks
  46.6 0.5 fusion.11.pair
  47.1 0.6 maximum_bitcast_fusion
  47.7 6.9 %project.1 = (bf16[16,240,128]{2,1,0:T(8,128)(2,1)}, f32[640,384]{1,0:T(8,128)}) custom-call(s32[12]{0:T(128)} %concatenate.28.blocks, bf16[640,1024]{1,0:T(8,128)(2,1)} %bitcast.92, bf16[1024,512]{1,0:T(8,128)(2,1)} %bitcast.94, f32[2560,128]{1,0:T(8,128)} %constant.94.clone.cos_t, f32[2560,128]{1,0:T(8,128)} %constant.95.clone.sin_t, ...), custom_call_target="tpu_custom_call" | custom-call | tf_op jit(solution)/shard_map/project/pallas_call | solution.py:266
  54.6 20.1 %to_heads.1 = (bf16[16,240,128]{2,1,0:T(8,128)(2,1)}, bf16[4,160,1024]{2,1,0:T(8,128)(2,1)}) custom-call(bf16[16,240,128]{2,1,0:T(8,128)(2,1)} %get-tuple-element.57.refs_0_, bf16[160,1024]{1,0:T(8,128)(2,1)} %bitcast.104), custom_call_target="tpu_custom_call" | custom-call | tf_op jit(solution)/shard_map/to_heads/pallas_call | solution.py:183
  74.8 10.4 %attend.1 = (bf16[16,80,128]{2,1,0:T(8,128)(2,1)}, bf16[2560,128]{1,0:T(8,128)(2,1)}, bf16[2560,128]{1,0:T(8,128)(2,1)}, bf16[2560,128]{1,0:T(8,128)(2,1)}, f32[64,2560]{1,0:T(8,128)}, /*index=5*/f32[8,2560]{1,0:T(8,128)}) custom-call(s32[16]{0:T(128)} %fusion.11.pair, bf16[16,240,128]{2,1,0:T(8,128)(2,1)} %get-tuple-element.58.recv), custom_call_target="tpu_custom_call" | custom-call | tf_op jit(solution)/shard_map/attend/pallas_call | solution.py:326
  85.1 15.5 %to_tokens.1.parts = bf16[16,80,128]{2,1,0:T(8,128)(2,1)} custom-call(bf16[16,80,128]{2,1,0:T(8,128)(2,1)} %get-tuple-element.59.refs_0_), custom_call_target="tpu_custom_call" | custom-call | tf_op jit(solution)/shard_map/to_tokens/pallas_call | solution.py:183
  100.6 9.7 %all-gather.2.cloned.1.call-done.wide = bf16[1024,4480]{1,0:T(8,128)(2,1)} async-done(((bf16[32,4480]{1,0:T(8,128)(2,1)}), bf16[1024,4480]{1,0:T(8,128)(2,1)}) %all-gather.2.cloned.1.call-update) | async-done | bytes 9175056 | tf_op jit(solution)/shard_map/all_gather | solution.py:769
  110.4 38.2 %middle_part.1 = (f32[160,1024]{1,0:T(8,128)}, bf16[4,160,1024]{2,1,0:T(8,128)(2,1)}, bf16[1024,3456]{1,0:T(8,128)(2,1)}, f32[160,1024]{1,0:T(8,128)}, bf16[160,...) custom-call(bf16[16,80,128]{2,1,0:T(8,128)(2,1)} %to_tokens.1.parts, ...), custom_call_target="tpu_custom_call" | custom-call | tf_op jit(solution)/shard_map/middle_part/pallas_call | solution.py:594
  148.5 27.0 %to_heads_back.1 = (bf16[16,80,128]{2,1,0:T(8,128)(2,1)}, bf16[4,160,1024]{2,1,0:T(8,128)(2,1)}) custom-call(bf16[16,80,128]{2,1,0:T(8,128)(2,1)} %get-tuple-element.63.refs_0_, bf16[4,160,1024]{2,1,0:T(8,128)(2,1)} %get-tuple-element.64.refs_1_), custom_call_target="tpu_custom_call" | custom-call | tf_op jit(solution)/shard_map/to_heads_back/pallas_call | solution.py:183
  175.5 18.0 %attend_back.1.refs_0_ = bf16[16,240,128]{2,1,0:T(8,128)(2,1)} custom-call(s32[16]{0:T(128)} %fusion.11.pair, bf16[16,80,128]{2,1,0:T(8,128)(2,1)} %get-tuple-element.67.recv, bf16[2560,128]{1,0:T(8,128)(2,1)} %get-tuple-element.68.q_s, bf16[2560,128]{1,0:T(8,128)(2,1)} %get-tuple-element.69.k_s, bf16[2560,128]{1,0:T(8,128)(2,1)} %get-tuple-element.70.v_s, ...), custom_call_target="tpu_custom_call" | custom-call | tf_op jit(solution)/shard_map/attend_back/pallas_call | solution.py:396
  193.6 29.2 %to_tokens_back.1 = (bf16[16,240,128]{2,1,0:T(8,128)(2,1)}, bf16[4,160,1024]{2,1,0:T(8,128)(2,1)}, bf16[4,160,256]{2,1,0:T(8,128)(2,1)}, f32[32,8,128]{2,1,0:T(8,128)}) custom-call(bf16[16,240,128]{2,1,0:T(8,128)(2,1)} %attend_back.1.refs_0_, bf16[160,1024]{1,0:T(8,128)(2,1)} %get-tuple-element.73.refs_1_, bf16[4,160,256]{2,1,0:T(8,128)(2,1)} %get-tuple-element.74.refs_2_, ...), custom_call_target="tpu_custom_call" | custom-call | tf_op jit(solution)/shard_map/to_tokens_back/pallas_call | solution.py:183
  222.8 2.0 fusion
  224.8 0.4 reshape.123
  225.2 0.9 copy.35
  226.1 10.1 %project_back.1 = (bf16[640,1024]{1,0:T(8,128)(2,1)}, bf16[1024,512]{1,0:T(8,128)(2,1)}, f32[8,128]{1,0:T(8,128)}, f32[1,1024]{1,0:T(1,128)}) custom-call(s32[12]{0:T(128)} %concatenate.28.blocks, bf16[16,240,128]{2,1,0:T(8,128)(2,1)} %get-tuple-element.76.recv, f32[640,384]{1,0:T(8,128)} %get-tuple-element.77.raw, bf16[640,1024]{1,0:T(8,128)(2,1)} %bitcast.93, ...), custom_call_target="tpu_custom_call" | custom-call | tf_op jit(solution)/shard_map/project_back/pallas_call | solution.py:677
  236.2 0.7 div.10
  236.9 1.3 pad_maximum_fusion.5.refs_3_
  238.2 33.5 %sum_qkv.1 = (bf16[4,160,1024]{2,1,0:T(8,128)(2,1)}, bf16[32,32,512]{2,1,0:T(8,128)(2,1)}, bf16[32,32,256]{2,1,0:T(8,128)(2,1)}, f32[32,16,128]{2,1,0:T(8,128)}) custom-call(bf16[4,160,1024]{2,1,0:T(8,128)(2,1)} %bitcast.97, bf16[32,32,512]{2,1,0:T(8,128)(2,1)} %bitcast.98, bf16[32,32,256]{2,1,0:T(8,128)(2,1)} %bitcast.96, f32[16,128]{1,0:T(8,128)} %pad_maximum_fusion.5.refs_3_), custom_call_target="tpu_custom_call" | custom-call | tf_op jit(solution)/shard_map/sum_qkv/pallas_call | solution.py:183
  271.7 1.1 reduce_sum.92
  272.8 1.1 reduce_sum.94
  273.9 1.4 reduce_sum.91
  275.3 0.6 pad_maximum_fusion.4.refs_1_
  275.9 0.2 convert_reduce_fusion
  276.2 0.2 fusion.8
  276.4 0.9 copy-done.2
  277.3 0.2 convert_reduce_fusion.1
  277.5 0.8 fusion.9
  278.3 0.4 copy-done.5
  278.7 1.0 fusion.10
  279.7 0.9 slice.68
  280.7 0.1 copy.36
  280.8 0.9 slice.67
  281.7 0.7 pad_maximum_fusion.1.refs_0_
  282.4 0.6 pad_maximum_fusion.2.refs_2_
  283.0 20.5 %gather_out.1 = (bf16[4,32,2816]{2,1,0:T(8,128)(2,1)}, f32[4,24,128]{2,1,0:T(8,128)}, bf16[4,176,256]{2,1,0:T(8,128)(2,1)}) custom-call(bf16[32,2816]{1,0:T(8,128)(2,1)} %pad_maximum_fusion.1.refs_0_, f32[24,128]{1,0:T(8,128)} %pad_maximum_fusion.4.refs_1_, bf16[176,256]{1,0:T(8,128)(2,1)} %pad_maximum_fusion.2.refs_2_), custom_call_target="tpu_custom_call" | custom-call | tf_op jit(solution)/shard_map/gather_out/pallas_call | solution.py:183
  303.5 0.8 reduce_sum.95
  304.4 0.6 fusion.12
  304.9 0.6 slice_bitcast_fusion.7
  305.5 1.2 convert_element_type.38
  306.8 0.1 slice_bitcast_fusion.1
  306.9 0.9 copy-done.6
  307.9 0.7 copy.44
  308.6 0.9 copy.49
  309.4 0.6 copy.59
  310.1 0.6 copy.60
  310.7 0.9 copy.48
  311.5 0.9 copy.50
  312.4 0.7 copy.47
  (42 shorter events, 0.5 us)
Async XLA Ops:
  7.2 1.0 copy-start
  7.2 36.7 %copy-start.9 = (bf16[32,1024]{1,0:T(8,128)(2,1)S(1)}, bf16[32,1024]{1,0:T(8,128)(2,1)}, u32[]{:S(2)}) copy-start(bf16[32,1024]{1,0:T(8,128)(2,1)} %param.21) | copy-start | bytes 196612
  7.2 103.1 %all-gather.2.cloned.1.call-start = ((), (), s32[]{:S(2)}) async-start(), calls=%async_computation.1 | async-start | bytes 9461760 | tf_op jit(solution)/shard_map/all_gather | solution.py:769
  8.2 35.6 %collective-permute-start = (bf16[144,256]{1,0:T(8,128)(2,1)S(1)}, bf16[144,256]{1,0:T(8,128)(2,1)S(1)}, u32[]{:S(2)}, u32[]{:S(2)}) collective-permute-start(bf16[144,256]{1,0:T(8,128)(2,1)S(1)} %constant_dynamic-slice_fusion), channel_id=1, source_target_pairs={{0,0},{8,32},{16,64},{24,96},{32,8},{40,40},{48,72},{56,104},{64,1... | collective-permute-start | bytes 221192 | tf_op jit(solution)/shard_map/ppermute | solution.py:752
  18.9 28.2 %copy-start.10 = (f32[64]{0:T(128)S(1)}, f32[64]{0:T(128)}, u32[]{:S(2)}) copy-start(f32[64]{0:T(128)} %param.26) | copy-start | bytes 772
  18.9 28.2 %copy-start.11 = (f32[64]{0:T(128)S(1)}, f32[64]{0:T(128)}, u32[]{:S(2)}) copy-start(f32[64]{0:T(128)} %param.27) | copy-start | bytes 772
  44.6 235.1 %reduce-scatter.2.cloned.1.call-start = ((), (), s32[]{:S(2)}) async-start(), calls=%async_computation.2 | async-start | bytes 7299072 | tf_op jit(solution)/shard_map/reduce_scatter | solution.py:785
  226.1 10.1 %copy-start.8 = (f32[1024]{0:T(1024)S(1)}, f32[1024]{0:T(1024)}, u32[]{:S(2)}) copy-start(f32[1024]{0:T(1024)} %param.25) | copy-start | bytes 12292
  226.1 10.8 %copy-start.7 = (f32[32,8,128]{2,1,0:T(8,128)S(1)}, f32[32,8,128]{2,1,0:T(8,128)}, u32[]{:S(2)}) copy-start(f32[32,8,128]{2,1,0:T(8,128)} %get-tuple-element.88) | copy-start | bytes 393220
  271.7 4.3 %copy-start.3 = (bf16[4,160,1024]{2,1,0:T(8,128)(2,1)S(1)}, bf16[4,160,1024]{2,1,0:T(8,128)(2,1)}, u32[]{:S(2)}) copy-start(bf16[4,160,1024]{2,1,0:T(8,128)(2,1)} %get-tuple-element.84) | copy-start | bytes 3932164
  273.9 2.3 copy-start.1
  275.9 1.3 copy-start.2
  276.2 1.3 copy-start.4
  277.5 1.2 copy-start.5
  306.8 1.0 copy-start.6
Sparse Core Ops, SparseCore 0:
  44.8 65.5 all-gather.1
  148.7 109.2 reduce-scatter.1

commit v4 on v3

--- a/solution.py
+++ b/solution.py
@@ -97,7 +97,7 @@
     barrier = pltpu.get_barrier_semaphore()
     expected = 0
     starts = []
-    for i, (g, _) in enumerate(items):
+    for i, (g, _, _) in enumerate(items):
         has_own, sent, _ = own(g)
         size = SIZE[g]
         if has_own is None:
@@ -116,13 +116,19 @@
 
         lax.fori_loop(first, size, greet, 0)
 
+    def block_of(i, t):
+        _, mode, cols = items[i]
+        if cols is not None:
+            return srcs[i].at[:, pl.ds(*cols)]
+        return srcs[i] if mode == "ag" else srcs[i].at[t]
+
     def own_copy(i):
-        g, mode = items[i]
+        g = items[i][0]
         _, sent, place = own(g)
-        src = srcs[i] if mode == "ag" else srcs[i].at[sent]
+        src = block_of(i, sent)
         return pltpu.make_async_copy(src, outs[i].at[place], sems[3 * i + 2])
 
-    for i, (g, _) in enumerate(items):
+    for i, (g, _, _) in enumerate(items):
         if own(g)[0] is None:
             own_copy(i).start()
         else:
@@ -130,9 +136,9 @@
     pl.semaphore_wait(barrier, expected)
 
     def remote(i, t, place):
-        g, mode = items[i]
+        g = items[i][0]
         dev, there = target(g, t)
-        src = srcs[i] if mode == "ag" else srcs[i].at[t]
+        src = block_of(i, t)
         return pltpu.make_async_remote_copy(
             src_ref=src,
             dst_ref=outs[i].at[there if place is None else place],
@@ -142,7 +148,7 @@
             device_id_type=MESH,
         )
 
-    for i, (g, _) in enumerate(items):
+    for i, (g, _, _) in enumerate(items):
         first, sent = starts[i]
 
         def send(k, carry, i=i, g=g, sent=sent):
@@ -150,7 +156,7 @@
             return carry
 
         lax.fori_loop(first, SIZE[g], send, 0)
-    for i, (g, _) in enumerate(items):
+    for i, (g, _, _) in enumerate(items):
         first, sent = starts[i]
         place = own(g)[2]
 
@@ -167,14 +173,15 @@
 
 
 def exchange(number, name, *parts):
-    items = tuple((g, m) for g, m, _ in parts)
-    arrays = [a for _, _, a in parts]
-    outs = [
-        jax.ShapeDtypeStruct((SIZE[g],) + (a.shape if m == "ag" else a.shape[1:]), a.dtype)
-        for g, m, a in parts
-    ]
+    items = tuple((part[0], part[1], part[3] if len(part) > 3 else None) for part in parts)
+    arrays = [part[2] for part in parts]
+    outs = []
+    for (g, m, cols), a in zip(items, arrays):
+        shape = a.shape if m == "ag" else a.shape[1:]
+        shape = shape if cols is None else shape[:-1] + (cols[1],)
+        outs.append(jax.ShapeDtypeStruct((SIZE[g],) + shape, a.dtype))
     scratch = []
-    for g, _ in items:
+    for g, _, _ in items:
         scratch += [
             pltpu.SemaphoreType.DMA((SIZE[g],)),
             pltpu.SemaphoreType.DMA((SIZE[g],)),
@@ -235,13 +242,14 @@
     return jnp.concatenate([table[rows_of(blocks[2 * s]), :], table[rows_of(blocks[2 * s + 1]), :]], 0)
 
 
-def project_kernel(blocks, h, w, cos_t, sin_t, g_q, g_k, send, raw, acc):
+def project_kernel(blocks, h, w, cos_t, sin_t, g_q, g_k, send, raw, cos_o, sin_o, acc):
     acc[...] = nn(h[...], w[...])
     m = low_half((ROWS, 2 * HD))
     mh = low_half((BLK, 2 * HD))
     for s in range(NX):
         at = slice(s * ROWS, (s + 1) * ROWS)
         cos_r, sin_r = rope_rows(blocks, cos_t, s), rope_rows(blocks, sin_t, s)
+        cos_o[at, :], sin_o[at, :] = cos_r, sin_r
         raw[at, :] = acc[at, : QX + KX]
         turned = []
         for p in range(3):
@@ -268,12 +276,14 @@
         grid_spec=pltpu.PrefetchScalarGridSpec(
             num_scalar_prefetch=1,
             in_specs=[pl.BlockSpec(memory_space=pltpu.VMEM)] * 6,
-            out_specs=[pl.BlockSpec(memory_space=pltpu.VMEM)] * 2,
+            out_specs=[pl.BlockSpec(memory_space=pltpu.VMEM)] * 4,
             scratch_shapes=[pltpu.VMEM((NX * ROWS, QX + 2 * KX), F32)],
         ),
         out_shape=[
             jax.ShapeDtypeStruct((16, ROWS + BLK, 2 * HD), BF16),
             jax.ShapeDtypeStruct((NX * ROWS, QX + KX), F32),
+            jax.ShapeDtypeStruct((NX * ROWS, 2 * HD), F32),
+            jax.ShapeDtypeStruct((NX * ROWS, 2 * HD), F32),
         ],
         compiler_params=pltpu.CompilerParams(vmem_limit_bytes=VMEM_BYTES),
         name="project",
@@ -632,23 +642,122 @@
     )(parts, tokens, cot, g_ffn, wide)
 
 
-def project_back_kernel(blocks, recv, raw, h, w, cos_t, sin_t, g_q, g_k, gh, dw, gains, attn, low):
+def project_back_kernel(
+    recv,
+    raw,
+    h,
+    w,
+    cos_r,
+    sin_r,
+    g_q,
+    g_k,
+    g_attn,
+    mixed_x,
+    branch_x,
+    result,
+    gain_ffn,
+    tokens,
+    grad_middle,
+    middle,
+    out_o,
+    tokens_o,
+    qkv_o,
+    wo_o,
+    gains_o,
+    low,
+    attn,
+    gh,
+    gh_parts,
+    result_parts,
+    dw,
+    sibling_dw,
+    reduced,
+    dw_parts,
+    gains,
+    sibling_gains,
+    gains_all,
+    ss_r,
+    rs_r,
+    ss_h,
+    rs_h,
+    ss_s,
+    rs_s,
+    ss_w,
+    rs_w,
+    ss_g,
+    rs_g,
+):
+    x, z, y, c = coords()
+    ctx = z * 4 + y
+    barrier = pltpu.get_barrier_semaphore()
+    for k in range(1, NX):
+        pl.semaphore_signal(
+            barrier, inc=1, device_id=(lax.rem(x + k, NX), z, y, c), device_id_type=MESH
+        )
+    pl.semaphore_signal(barrier, inc=1, device_id=(x, z, y, 1 - c), device_id_type=MESH)
+
+    def greet(k, carry):
+        t = lax.rem(ctx + k, 16)
+        dev = (x, t // 4, lax.rem(t, 4), c)
+        pl.semaphore_signal(barrier, inc=1, device_id=dev, device_id_type=MESH)
+        return carry
+
+    lax.fori_loop(1, 16, greet, 0)
+    pl.semaphore_wait(barrier, NX + 15)
+
+    def along_x(src, dst, ss, rs, t, place):
+        return pltpu.make_async_remote_copy(
+            src_ref=src.at[t],
+            dst_ref=dst.at[place],
+            send_sem=ss.at[t],
+            recv_sem=rs.at[place],
+            device_id=(t, z, y, c),
+            device_id_type=MESH,
+        )
+
+    def to_sibling(i):
+        src, dst = ((dw.at[1 - c], sibling_dw), (gains, sibling_gains))[i]
+        return pltpu.make_async_remote_copy(
+            src_ref=src,
+            dst_ref=dst,
+            send_sem=ss_s.at[i],
+            recv_sem=rs_s.at[i],
+            device_id=(x, z, y, 1 - c),
+            device_id_type=MESH,
+        )
+
+    def over_ctx(i, t, place):
+        src, dst, ss, rs = (
+            (reduced.at[t], dw_parts, ss_w, rs_w),
+            (gains, gains_all, ss_g, rs_g),
+        )[i]
+        return pltpu.make_async_remote_copy(
+            src_ref=src,
+            dst_ref=dst.at[place],
+            send_sem=ss.at[t],
+            recv_sem=rs.at[place],
+            device_id=(x, t // 4, lax.rem(t, 4), c),
+            device_id_type=MESH,
+        )
+
     m = low_half((ROWS, 2 * HD))
     mh = low_half((BLK, 2 * HD))
     gq_sum = jnp.zeros((1, 2 * HD), F32)
     gk_sum = jnp.zeros((1, 2 * HD), F32)
-    for s in range(NX):
-        at = slice(s * ROWS, (s + 1) * ROWS)
-        cos_r, sin_r = rope_rows(blocks, cos_t, s), rope_rows(blocks, sin_t, s)
-        part = [recv[blocks[8 + s] * 4 + hh, :ROWS, :].astype(F32) for hh in range(4)]
-        vals = [recv[blocks[8 + s] * 4 + hh, ROWS:, :].astype(F32) for hh in range(4)]
+    for n, k in enumerate((1, 3, 2, 0)):
+        s = lax.rem(x + k, NX)
+        at = pl.ds(pl.multiple_of(s * ROWS, ROWS), ROWS)
+        place = place_of(x, s) * 4
+        cos_s, sin_s = cos_r[at, :], sin_r[at, :]
+        part = [recv[place + hh, :ROWS, :].astype(F32) for hh in range(4)]
+        vals = [recv[place + hh, ROWS:, :].astype(F32) for hh in range(4)]
         grads = [
             jnp.where(m, part[0], swap(part[1])),
             jnp.where(m, part[2], swap(part[3])),
             jnp.where(m, swap(part[0] + part[1]), part[2] + part[3]),
         ]
         for p in range(3):
-            turned = grads[p] * cos_r + swap_halves(grads[p] * sin_r)
+            turned = grads[p] * cos_s + swap_halves(grads[p] * sin_s)
             v = raw[at, p * 128 : (p + 1) * 128]
             gain = g_q[...] if p < 2 else g_k[...]
             r = lax.rsqrt(head_mean(v * v) + EPSILON)
@@ -663,34 +772,160 @@
         a, b = vals[0] + vals[1], vals[2] + vals[3]
         grad_v = jnp.concatenate([jnp.where(mh, a, swap(b)), jnp.where(mh, swap(a), b)], 0)
         low[at, 3 * 128 :] = grad_v.astype(BF16)
-    gains[...] = jnp.concatenate([gq_sum, gk_sum, jnp.zeros((6, 2 * HD), F32)], 0)
-    for s in range(NX):
-        at = slice(s * ROWS, (s + 1) * ROWS)
         grad_h = nt(low[at, :], w[...])
-        gh[at, :] = grad_h.astype(BF16)
+        gh[s] = grad_h.astype(BF16)
+        if k:
+            along_x(gh, gh_parts, ss_h, rs_h, s, x).start()
         term = jnp.sum(grad_h * h[at, :].astype(F32), axis=0, keepdims=True)
-        attn[...] = term if s == 0 else attn[...] + term
-    dw[...] = tn(h[...], low[...]).astype(BF16)
-
-
-def project_back(blocks, recv, raw, h, w, cos_t, sin_t, g_q, g_k):
+        attn[...] = term if n == 0 else attn[...] + term
+    for i in range(8):
+        cols = slice(i * 128, i * 128 + 128)
+        gains[i : i + 1, :] = attn[:, cols] / g_attn[:, cols]
+        gains[8 + i : 9 + i, :] = gain_ffn[:, cols]
+    gains[16:, :] = jnp.concatenate([gq_sum, gk_sum, jnp.zeros((6, 2 * HD), F32)], 0)
+    grad_w = tn(h[...], low[...]).astype(BF16)
+    for i in range(32):
+        dw[i % 2, i // 2, :, : QX + 2 * KX] = grad_w[i * 32 : (i + 1) * 32, :]
+    grad_w = tn(
+        mixed_x[...].reshape(NX * ROWS, QX), branch_x[...].reshape(NX * ROWS, D)
+    ).astype(BF16)
+    for q in range(4):
+        for i in range(8):
+            dw[i % 2, q * 4 + i // 2, :, QX + 2 * KX :] = grad_w[
+                i * 32 : (i + 1) * 32, q * 256 : (q + 1) * 256
+            ]
+    to_sibling(0).start()
+    to_sibling(1).start()
+    for k in (1, 3, 2):
+        along_x(result, result_parts, ss_r, rs_r, lax.rem(x + k, NX), x).start()
+    to_sibling(1).wait()
+    gains[...] = gains[...] + sibling_gains[...]
+    to_sibling(0).wait()
+
+    def send(k, carry):
+        t = lax.rem(ctx + k, 16)
+        reduced[t] = (dw[c, t].astype(F32) + sibling_dw[t].astype(F32)).astype(BF16)
+        over_ctx(0, t, ctx).start()
+        over_ctx(1, t, ctx).start()
+        return carry
+
+    lax.fori_loop(1, 16, send, 0)
+    total = dw[c, ctx].astype(F32) + sibling_dw[ctx].astype(F32)
+    all_gains = gains[...]
+
+    grad_h = gh[x].astype(F32)
+    for k in (1, 3, 2):
+        t = lax.rem(x + k, NX)
+        along_x(gh, gh_parts, ss_h, rs_h, t, t).wait_recv()
+        grad_h = grad_h + gh_parts[t].astype(F32)
+    inputs = tokens[...].astype(F32)
+    r = lax.rsqrt(jnp.mean(inputs * inputs, axis=-1, keepdims=True) + EPSILON)
+    weighted = grad_h * g_attn[...]
+    inner = jnp.mean(weighted * inputs, axis=-1, keepdims=True)
+    tokens_o[...] = (
+        grad_middle[...] + r * weighted - inputs * (r * r * r) * inner
+    ).astype(BF16)
+    out = middle[...] + result[x].astype(F32)
+    for k in (1, 3, 2):
+        t = lax.rem(x + k, NX)
+        along_x(result, result_parts, ss_r, rs_r, t, t).wait_recv()
+        out = out + result_parts[t].astype(F32)
+    out_o[...] = out.astype(BF16)
+
+    def collect(k, carry):
+        t = lax.rem(ctx + k, 16)
+        over_ctx(0, t, t).wait_recv()
+        over_ctx(1, t, t).wait_recv()
+        return carry[0] + dw_parts[t].astype(F32), carry[1] + gains_all[t]
+
+    total, all_gains = lax.fori_loop(1, 16, collect, (total, all_gains))
+    qkv_o[...] = total[:, : QX + 2 * KX].astype(BF16)
+    wo_o[...] = total[:, QX + 2 * KX :].astype(BF16)
+    gains_o[...] = all_gains
+
+    def drain(k, carry):
+        t = lax.rem(ctx + k, 16)
+        over_ctx(0, t, ctx).wait_send()
+        over_ctx(1, t, ctx).wait_send()
+        return carry
+
+    lax.fori_loop(1, 16, drain, 0)
+    for k in (1, 3, 2):
+        t = lax.rem(x + k, NX)
+        along_x(gh, gh_parts, ss_h, rs_h, t, x).wait_send()
+        along_x(result, result_parts, ss_r, rs_r, t, x).wait_send()
+
+
+def project_back(number, *operands):
+    vmem = pl.BlockSpec(memory_space=pltpu.VMEM)
+    tokens = (NX, ROWS, D)
+    wide = QX + 2 * KX + QX
     return pl.pallas_call(
         project_back_kernel,
-        grid_spec=pltpu.PrefetchScalarGridSpec(
-            num_scalar_prefetch=1,
-            in_specs=[pl.BlockSpec(memory_space=pltpu.VMEM)] * 8,
-            out_specs=[pl.BlockSpec(memory_space=pltpu.VMEM)] * 4,
-            scratch_shapes=[pltpu.VMEM((NX * ROWS, QX + 2 * KX), BF16)],
+        in_specs=[vmem] * 16,
+        out_specs=[vmem] * 5,
+        out_shape=[
+            jax.ShapeDtypeStruct((ROWS, D), BF16),
+            jax.ShapeDtypeStruct((ROWS, D), BF16),
+            jax.ShapeDtypeStruct((32, QX + 2 * KX), BF16),
+            jax.ShapeDtypeStruct((32, QX), BF16),
+            jax.ShapeDtypeStruct((24, 2 * HD), F32),
+        ],
+        scratch_shapes=[
+            pltpu.VMEM((NX * ROWS, QX + 2 * KX), BF16),
+            pltpu.VMEM((1, D), F32),
+            pltpu.VMEM(tokens, BF16),
+            pltpu.VMEM(tokens, BF16),
+            pltpu.VMEM(tokens, BF16),
+            pltpu.VMEM((2, 16, 32, wide), BF16),
+            pltpu.VMEM((16, 32, wide), BF16),
+            pltpu.VMEM((16, 32, wide), BF16),
+            pltpu.VMEM((16, 32, wide), BF16),
+            pltpu.VMEM((24, 2 * HD), F32),
+            pltpu.VMEM((24, 2 * HD), F32),
+            pltpu.VMEM((16, 24, 2 * HD), F32),
+        ]
+        + [pltpu.SemaphoreType.DMA((n,)) for n in (NX, NX, NX, NX, 2, 2, 16, 16, 16, 16)],
+        compiler_params=pltpu.CompilerParams(
+            collective_id=number, has_side_effects=True, vmem_limit_bytes=VMEM_BYTES
         ),
-        out_shape=[
-            jax.ShapeDtypeStruct((NX * ROWS, D), BF16),
-            jax.ShapeDtypeStruct((D, QX + 2 * KX), BF16),
-            jax.ShapeDtypeStruct((8, 2 * HD), F32),
-            jax.ShapeDtypeStruct((1, D), F32),
-        ],
+        name="project_back",
+    )(*operands)
+
+
+def hand_out_kernel(qkv, gu, wo, wd, gains, q_o, k_o, v_o, o_o, g_o, u_o, d_o, ga_o, gf_o, gh_o):
+    for s in range(NX):
+        q_o[:, s * QX : (s + 1) * QX] = qkv[s, :, :QX].astype(F32)
+        k_o[:, s * KX : (s + 1) * KX] = qkv[s, :, QX : QX + KX].astype(F32)
+        v_o[:, s * KX : (s + 1) * KX] = qkv[s, :, QX + KX :].astype(F32)
+        g_o[:, s * FX : (s + 1) * FX] = gu[s, :, :FX].astype(F32)
+        u_o[:, s * FX : (s + 1) * FX] = gu[s, :, FX:].astype(F32)
+        o_o[:, s * 256 : (s + 1) * 256] = wo[s, :, :].astype(F32)
+        for rg in range(9):
+            for l in range(2):
+                at = slice(s * 256 + l * 128, s * 256 + l * 128 + 128)
+                d_o[rg * 16 : rg * 16 + 16, at] = wd[
+                    s, l * 16 : l * 16 + 16, rg * 128 : rg * 128 + 128
+                ].astype(F32)
+    total = gains[0] + gains[1] + gains[2] + gains[3]
+    for i in range(8):
+        ga_o[:, i * 128 : i * 128 + 128] = total[i : i + 1, :]
+        gf_o[:, i * 128 : i * 128 + 128] = total[8 + i : 9 + i, :]
+    gh_o[...] = total[16:, :] + swap(total[16:, :])
+
+
+def hand_out(*operands):
+    vmem = pl.BlockSpec(memory_space=pltpu.VMEM)
+    shapes = [(32, D), (32, KV * HD), (32, KV * HD), (32, D), (32, FF), (32, FF), (FF // 32, D)]
+    shapes += [(1, D), (1, D), (8, 2 * HD)]
+    return pl.pallas_call(
+        hand_out_kernel,
+        in_specs=[vmem] * 5,
+        out_specs=[vmem] * 10,
+        out_shape=[jax.ShapeDtypeStruct(s, F32) for s in shapes],
         compiler_params=pltpu.CompilerParams(vmem_limit_bytes=VMEM_BYTES),
-        name="project_back",
-    )(blocks, recv, raw, h, w, cos_t, sin_t, g_q, g_k)
+        name="hand_out",
+    )(*operands)
 
 
 def angle_constants():
@@ -703,14 +938,6 @@
 def rms_rows(values_in, gain):
     inv_rms = lax.rsqrt(jnp.mean(values_in * values_in, axis=-1, keepdims=True) + EPSILON)
     return (values_in * inv_rms * gain, inv_rms)
-
-
-def rms_rows_back(values_in, gain, inv_rms, grad_in):
-    weighted = grad_in * gain
-    inner = jnp.mean(weighted * values_in, axis=-1, keepdims=True)
-    grad_values = inv_rms * weighted - values_in * (inv_rms * inv_rms * inv_rms) * inner
-    gain_terms = grad_in * values_in * inv_rms
-    return (grad_values, gain_terms)
 
 
 def columns_of(w, x, width):
@@ -756,7 +983,7 @@
     )
 
     inputs = tokens[0].astype(F32)
-    normed_attn, inv_attn = rms_rows(inputs, g_attn)
+    normed_attn, _ = rms_rows(inputs, g_attn)
     h_attn = normed_attn.astype(BF16)
     w_x = jnp.concatenate(
         [columns_of(w_query, x, QX), columns_of(w_key, x, KX), columns_of(w_value, x, KX)], axis=1
@@ -775,7 +1002,7 @@
     blocks = jnp.concatenate([jnp.stack([first, 31 - first], axis=1).reshape(8), places])
     pair = lax.dynamic_slice_in_dim(pairs_all, sequence_at(x, z), 1, axis=0)[0]
 
-    send, raw = project(blocks, h_all, w_qkv, cos_t, sin_t, gq2, gk2)
+    send, raw, cos_r, sin_r = project(blocks, h_all, w_qkv, cos_t, sin_t, gq2, gk2)
     recv, cot_all = exchange(2, "to_heads", ("c", "a2a", send), ("x", "ag", cotangent[0]))
     heads_out, q_s, k_s, v_s, o_t, inv = attend(pair, recv)
     (mixed_parts,) = exchange(3, "to_tokens", ("t", "a2a", heads_out))
@@ -783,80 +1010,52 @@
         4, mixed_parts, tokens[0], cot_all, g_ffn[None], wide
     )
     sums = lax.psum_scatter(grad_w_ffn, CTX_FSDP, scatter_dimension=0, tiled=True)
-    sum_gu, sum_d = sums[:, : 2 * FX], from_tiles(sums[:, 2 * FX :][None])[0]
-    recv_g, result_parts = exchange(
-        6, "to_heads_back", ("r", "a2a", back_parts), ("x", "a2a", result4)
-    )
-    output = (middle + jnp.sum(result_parts.astype(F32), axis=0)).astype(BF16)[None]
-
+    (recv_g,) = exchange(6, "to_heads_back", ("r", "a2a", back_parts))
     sends_back = attend_back(pair, recv_g, q_s, k_s, v_s, o_t, inv)
-    recv_back, branch_x, mixed_x, gains_ffn = exchange(
+    recv_back, branch_x, mixed_x = exchange(
         7,
         "to_tokens_back",
         ("c", "a2a", sends_back),
         ("x", "ag", grad_branch),
         ("x", "a2a", mixed),
-        ("p", "ag", gain_ffn.reshape(8, 128)),
     )
-    grad_h_qkv, grad_w_qkv, gains_qk, gains_attn = project_back(
-        blocks, recv_back, raw, h_all, w_qkv, cos_t, sin_t, gq2, gk2
+    output, grad_tokens, sum_qkv, sum_o, gains = project_back(
+        8,
+        recv_back,
+        raw,
+        h_all,
+        w_qkv,
+        cos_r,
+        sin_r,
+        gq2,
+        gk2,
+        g_attn[None],
+        mixed_x,
+        branch_x,
+        result4,
+        gain_ffn,
+        tokens[0],
+        grad_middle,
+        middle,
     )
-    gains = jnp.concatenate([(gains_attn / g_attn).reshape(8, 128), gains_qk])
-    grad_w_o = jnp.einsum(
-        "rh,rd->hd",
-        mixed_x.reshape(NX * ROWS, QX),
-        branch_x.reshape(NX * ROWS, D),
-        preferred_element_type=F32,
-    ).astype(BF16)
-    grad_w_o = grad_w_o.reshape(8, 32, 4, D // 4).transpose(2, 0, 1, 3).reshape(32, 32, D // 4)
-    grad_h_parts, grad_w_parts, grad_o_parts, gains_p = exchange(
-        8,
-        "sum_qkv",
-        ("x", "a2a", grad_h_qkv.reshape(NX, ROWS, D)),
-        ("p", "a2a", grad_w_qkv.reshape(32, 32, QX + 2 * KX)),
-        ("p", "a2a", grad_w_o),
-        ("p", "ag", gains),
-    )
-    grad_h_attn = jnp.sum(grad_h_parts.astype(F32), axis=0)
-    grad_inputs_norm, _ = rms_rows_back(inputs, g_attn, inv_attn, grad_h_attn)
-    grad_tokens = (grad_middle + grad_inputs_norm).astype(BF16)[None]
-    sum_qkv = jnp.sum(grad_w_parts.astype(F32), axis=0).astype(BF16)
-    sum_o = jnp.sum(grad_o_parts.astype(F32), axis=0).astype(BF16)
-    gains = jnp.concatenate([jnp.sum(gains_p, axis=0), jnp.sum(gains_ffn, axis=0)])
-    last, gains_x, quarters = exchange(
+    qkv, gate_up, out_rows, down_rows, gains = exchange(
         9,
         "gather_out",
-        ("x", "ag", jnp.concatenate([sum_qkv, sum_gu], axis=1)),
+        ("x", "ag", sum_qkv),
+        ("x", "ag", sums, (0, 2 * FX)),
+        ("d", "ag", sum_o),
+        ("d", "ag", sums, (2 * FX, FX)),
         ("x", "ag", gains),
-        ("d", "ag", jnp.concatenate([sum_o, sum_d], axis=0)),
     )
-    gains = jnp.sum(gains_x, axis=0)
-    last = last.astype(F32)
-    grad_w_query = last[:, :, :QX].transpose(1, 0, 2).reshape(32, H * HD)
-    grad_w_key = last[:, :, QX : QX + KX].transpose(1, 0, 2).reshape(32, KV * HD)
-    grad_w_value = last[:, :, QX + KX : QX + 2 * KX].transpose(1, 0, 2).reshape(32, KV * HD)
-    rest = last[:, :, QX + 2 * KX :]
-    grad_w_gate = rest[:, :, :FX].transpose(1, 0, 2).reshape(32, FF)
-    grad_w_up = rest[:, :, FX : 2 * FX].transpose(1, 0, 2).reshape(32, FF)
-    quarters = quarters.astype(F32)
-    grad_w_out = quarters[:, :32].transpose(1, 0, 2).reshape(32, D)
-    grad_w_down = quarters[:, 32:].transpose(1, 0, 2).reshape(FF // 32, D)
-    g_q = gains[8, :HD] + gains[8, HD:]
-    g_k = gains[9, :HD] + gains[9, HD:]
+    *weights, gain_a, gain_f, gain_h = hand_out(qkv, gate_up, out_rows, down_rows, gains)
     return (
-        output,
-        grad_tokens,
-        grad_w_query,
-        grad_w_key,
-        grad_w_value,
-        grad_w_out,
-        grad_w_gate,
-        grad_w_up,
-        grad_w_down,
-        gains[:8].reshape(D),
-        g_q,
-        g_k,
-        gains[16:].reshape(D),
+        output[None],
+        grad_tokens[None],
+        *weights,
+        gain_a[0],
+        gain_h[0, :HD],
+        gain_h[1, :HD],
+        gain_f[0],
     )
 
 

time: 321 us -> 277 us (0.86)
  Pallas kernels: 252 us -> 230 us
  other arithmetic: 17.7 us -> 4.94 us
  local copies, waits for them, and re-layouts: 18.2 us -> 9.64 us
    pallas_call x7 -> x6, Pallas kernels: 168 us -> 114 us  [exchange(): pl.pallas_call(functools.partial(exchange_kernel, items), out_shape=outs,...]
    pallas_call x1 -> x2, Pallas kernels: 10.1 us -> 42.2 us  [the longest x1 39.6 us: project_back(): pl.pallas_call(project_back_kernel, in_specs=[vmem] * 16, out_specs=[vmem...]
    reshape x10 -> x0, local copies, waits for them, and re-layouts: 7.04 us -> none  [the longest x2 1.26 us: body(): grad_w_o.reshape(8, 32, 4, D // 4).transpose(2, 0, 1, 3)]
    reduce_sum x8 -> x0, other arithmetic: 5.15 us -> none  [the longest x1 1.43 us: body(): sum_qkv = jnp.sum(grad_w_parts.astype(F32), axis=0).astype(BF16)]
    concatenate x4 -> x0, other arithmetic: 3.22 us -> none  [the longest x1 1.29 us: body(): gains = jnp.concatenate([(gains_attn / g_attn).reshape(8, 128), gains_qk])]
  transfers between devices with their start and end apart: 3 -> 3, of which waited for: 1 -> 2; matrix products, arithmetic and copies ran while one was open for 7% -> 4% of each run, Pallas kernels for 60% -> 62%
where the time goes in v4:
time: 277 us
  Pallas kernels  230 us (83%)
  between operations  14.3 us (5%)
  waiting for transfers between devices  12 us (4%)
  local copies, waits for them, and re-layouts  9.64 us (3%)
  starting transfers between devices  5.81 us (2%)
  other arithmetic  4.94 us (2%)
    pallas_call x6, Pallas kernels, exchange(): pl.pallas_call(functools.partial(exchange_kernel, items), out_shape=outs,...  114 us
    pallas_call x1, Pallas kernels, project_back(): pl.pallas_call(project_back_kernel, in_specs=[vmem] * 16, out_specs=[vmem...  39.6 us
    pallas_call x1, Pallas kernels, middle_part(): pl.pallas_call(middle_kernel, in_specs=[vmem] * 4 + [pl.BlockSpec(memory_...  38.2 us
    pallas_call x1, Pallas kernels, attend_back(): pl.pallas_call(attend_back_kernel, grid_spec=pltpu.PrefetchScalarGridSpec...  18 us
    pallas_call x1, Pallas kernels, attend(): pl.pallas_call(attend_kernel, grid_spec=pltpu.PrefetchScalarGridSpec(num_...  10.4 us
    all_gather x1, waiting for transfers between devices, body(): wide = lax.all_gather(mine, CTX_FSDP, axis=0, tiled=True)  9.65 us
    pallas_call x1, Pallas kernels, project(): pl.pallas_call(project_kernel, grid_spec=pltpu.PrefetchScalarGridSpec(num...  7.17 us
    ppermute x1, starting transfers between devices, body(): lax.ppermute(columns_of(w_down, x, D // 4), ('seq', 'ctx_0'), swap_xz)  5.73 us
  transfers between devices with their start and end apart: 3, of which 2 were waited for; matrix products, arithmetic and copies ran while one was open for 4% of the time, Pallas kernels for 62%

profile of v4, /device:TPU:4, one launch (start us, length us, event | category | flops | bytes accessed | tf_op | source)
XLA Modules:
  0.0 276.7 jit_solution(7150483019760115221)
XLA Ops:
  7.2 0.0 copy-start
  7.2 0.0 copy-start.3
  7.2 0.0 all-gather.2.cloned.1.call-start
  7.3 0.9 copy-done
  8.2 5.7 %collective-permute-start = (bf16[144,256]{1,0:T(8,128)(2,1)S(1)}, bf16[144,256]{1,0:T(8,128)(2,1)S(1)}, u32[]{:S(2)}, u32[]{:S(2)}) collective-permute-start(bf16[144,256]{1,0:T(8,128)(2,1)S(1)} %constant_dynamic-slice_fusion), channel_id=1, source_target_pairs={{0,0},{8,32},{16,64},{24,96},{32,8},{40,40},{48,72},{56,104},{64,1... | collective-permute-start | bytes 221192 | tf_op jit(solution)/shard_map/ppermute | solution.py:979
  13.9 1.1 fusion
  15.0 1.3 pad.4.refs_2_
  16.3 0.7 constant_dynamic-slice_fusion.6
  17.0 1.9 fusion.2.refs_0_
  18.9 0.0 copy-start.4
  18.9 0.0 copy-start.5
  18.9 0.7 constant_dynamic-slice_fusion.4
  19.6 0.9 constant_dynamic-slice_fusion.1
  20.5 0.6 pad_maximum_fusion.1.refs_1_
  21.2 22.6 %gather_in.1 = (bf16[4,160,1024]{2,1,0:T(8,128)(2,1)}, bf16[32,32,512]{2,1,0:T(8,128)(2,1)}, s32[4,8,128]{2,1,0:T(8,128)}) custom-call(bf16[160,1024]{1,0:T(8,128)(2,1)} %fusion.2.refs_0_, bf16[32,512]{1,0:T(8,128)(2,1)} %pad_maximum_fusion.1.refs_1_, s32[8,128]{1,0:T(8,128)} %pad.4.refs_2_), custom_call_target="tpu_custom_call" | custom-call | tf_op jit(solution)/shard_map/gather_in/pallas_call | solution.py:190
  43.8 0.0 collective-permute-done
  43.9 0.0 copy-done.3
  43.9 0.7 pad_maximum_fusion
  44.6 0.0 all-gather.2.cloned.1.call-update
  44.6 0.0 reduce-scatter.2.cloned.1.call-start
  44.8 0.7 slice.9
  45.5 0.2 dynamic-slice_reduce_fusion
  45.8 0.1 copy.31
  45.9 0.1 reshape.58
  46.0 0.6 concatenate.16.blocks
  46.6 0.5 fusion.3.pair
  47.1 0.0 copy-done.4
  47.1 0.0 copy-done.5
  47.1 0.6 maximum_bitcast_fusion
  47.7 7.2 %project.1 = (bf16[16,240,128]{2,1,0:T(8,128)(2,1)}, f32[640,384]{1,0:T(8,128)}, f32[640,128]{1,0:T(8,128)}, f32[640,128]{1,0:T(8,128)}) custom-call(s32[12]{0:T(128)} %concatenate.16.blocks, bf16[640,1024]{1,0:T(8,128)(2,1)} %bitcast.36, bf16[1024,512]{1,0:T(8,128)(2,1)} %bitcast.38, f32[2560,128]{1,0:T(8,128)} %constant.90.clone.cos_t, ...), custom_call_target="tpu_custom_call" | custom-call | tf_op jit(solution)/shard_map/project/pallas_call | solution.py:274
  54.8 20.1 %to_heads.1 = (bf16[16,240,128]{2,1,0:T(8,128)(2,1)}, bf16[4,160,1024]{2,1,0:T(8,128)(2,1)}) custom-call(bf16[16,240,128]{2,1,0:T(8,128)(2,1)} %get-tuple-element.65.refs_0_, bf16[160,1024]{1,0:T(8,128)(2,1)} %bitcast.41), custom_call_target="tpu_custom_call" | custom-call | tf_op jit(solution)/shard_map/to_heads/pallas_call | solution.py:190
  75.0 10.4 %attend.1 = (bf16[16,80,128]{2,1,0:T(8,128)(2,1)}, bf16[2560,128]{1,0:T(8,128)(2,1)}, bf16[2560,128]{1,0:T(8,128)(2,1)}, bf16[2560,128]{1,0:T(8,128)(2,1)}, f32[64,2560]{1,0:T(8,128)}, /*index=5*/f32[8,2560]{1,0:T(8,128)}) custom-call(s32[16]{0:T(128)} %fusion.3.pair, bf16[16,240,128]{2,1,0:T(8,128)(2,1)} %get-tuple-element.66.recv), custom_call_target="tpu_custom_call" | custom-call | tf_op jit(solution)/shard_map/attend/pallas_call | solution.py:336
  85.4 15.4 %to_tokens.1.parts = bf16[16,80,128]{2,1,0:T(8,128)(2,1)} custom-call(bf16[16,80,128]{2,1,0:T(8,128)(2,1)} %get-tuple-element.67.refs_0_), custom_call_target="tpu_custom_call" | custom-call | tf_op jit(solution)/shard_map/to_tokens/pallas_call | solution.py:190
  100.8 9.7 %all-gather.2.cloned.1.call-done.wide = bf16[1024,4480]{1,0:T(8,128)(2,1)} async-done(((bf16[32,4480]{1,0:T(8,128)(2,1)}), bf16[1024,4480]{1,0:T(8,128)(2,1)}) %all-gather.2.cloned.1.call-update) | async-done | bytes 9175056 | tf_op jit(solution)/shard_map/all_gather | solution.py:996
  110.4 38.2 %middle_part.1 = (f32[160,1024]{1,0:T(8,128)}, bf16[4,160,1024]{2,1,0:T(8,128)(2,1)}, bf16[1024,3456]{1,0:T(8,128)(2,1)}, f32[160,1024]{1,0:T(8,128)}, bf16[160,...) custom-call(bf16[16,80,128]{2,1,0:T(8,128)(2,1)} %to_tokens.1.parts, ...), custom_call_target="tpu_custom_call" | custom-call | tf_op jit(solution)/shard_map/middle_part/pallas_call | solution.py:604
  148.6 0.0 reduce-scatter.2.cloned.1.call-update
  148.6 14.9 %to_heads_back.1.recv = bf16[16,80,128]{2,1,0:T(8,128)(2,1)} custom-call(bf16[16,80,128]{2,1,0:T(8,128)(2,1)} %get-tuple-element.70.refs_0_), custom_call_target="tpu_custom_call" | custom-call | tf_op jit(solution)/shard_map/to_heads_back/pallas_call | solution.py:190
  163.5 18.0 %attend_back.1.refs_0_ = bf16[16,240,128]{2,1,0:T(8,128)(2,1)} custom-call(s32[16]{0:T(128)} %fusion.3.pair, bf16[16,80,128]{2,1,0:T(8,128)(2,1)} %to_heads_back.1.recv, bf16[2560,128]{1,0:T(8,128)(2,1)} %get-tuple-element.71.q_s, bf16[2560,128]{1,0:T(8,128)(2,1)} %get-tuple-element.72.k_s, bf16[2560,128]{1,0:T(8,128)(2,1)} %get-tuple-element.73.v_s, ...), custom_call_target="tpu_custom_call" | custom-call | tf_op jit(solution)/shard_map/attend_back/pallas_call | solution.py:406
  181.5 22.3 %to_tokens_back.1 = (bf16[16,240,128]{2,1,0:T(8,128)(2,1)}, bf16[4,160,1024]{2,1,0:T(8,128)(2,1)}, bf16[4,160,256]{2,1,0:T(8,128)(2,1)}) custom-call(bf16[16,240,128]{2,1,0:T(8,128)(2,1)} %attend_back.1.refs_0_, bf16[160,1024]{1,0:T(8,128)(2,1)} %get-tuple-element.76.refs_1_, bf16[4,160,256]{2,1,0:T(8,128)(2,1)} %get-tuple-element.77.refs_2_), custom_call_target="tpu_custom_call" | custom-call | tf_op jit(solution)/shard_map/to_tokens_back/pallas_call | solution.py:190
  203.8 39.6 %project_back.1 = (bf16[160,1024]{1,0:T(8,128)(2,1)}, bf16[160,1024]{1,0:T(8,128)(2,1)}, bf16[32,512]{1,0:T(8,128)(2,1)}, bf16[32,256]{1,0:T(8,128)(2,1)}, f32[24,128]{1,0:T(8,128)}) custom-call(bf16[16,240,128]{2,1,0:T(8,128)(2,1)} %get-tuple-element.78.recv, f32[640,384]{1,0:T(8,128)} %get-tuple-element.79.raw, bf16[640,1024]{1,0:T(8,128)(2,1)} %bitcast.37, ...), custom_call_target="tpu_custom_call" | custom-call | tf_op jit(solution)/shard_map/project_back/pallas_call | solution.py:863
  243.4 0.0 copy-start.2
  243.4 0.0 copy-start.1
  243.4 2.3 reduce-scatter.2.cloned.1.call-done.refs_1_.refs_3_
  245.7 18.8 %gather_out.1 = (bf16[4,32,512]{2,1,0:T(8,128)(2,1)}, bf16[4,32,2304]{2,1,0:T(8,128)(2,1)}, bf16[4,32,256]{2,1,0:T(8,128)(2,1)}, bf16[4,32,1152]{2,1,0:T(8,128)(2,1)}, f32[4,24,128]{2,1,0:T(8,128)}) custom-call(bf16[32,512]{1,0:T(8,128)(2,1)} %get-tuple-element.90.refs_0_, bf16[32,3456]{1,0:T(8,128)(2,1)} %reduce-scatter.2.cloned.1.call-done.refs_1_.refs_3_, ...), custom_call_target="tpu_custom_call" | custom-call | tf_op jit(solution)/shard_map/gather_out/pallas_call | solution.py:190
  264.5 2.6 hand_out.1
  267.2 1.3 slice_bitcast_fusion
  268.4 0.0 copy-done.2
  268.4 0.7 copy.38
  269.2 0.0 copy-done.1
  269.2 0.7 copy.39
  (7 shorter events, 0.1 us)
Async XLA Ops:
  7.2 1.0 copy-start
  7.2 36.7 %copy-start.3 = (bf16[32,1024]{1,0:T(8,128)(2,1)S(1)}, bf16[32,1024]{1,0:T(8,128)(2,1)}, u32[]{:S(2)}) copy-start(bf16[32,1024]{1,0:T(8,128)(2,1)} %param.21) | copy-start | bytes 196612
  7.2 103.2 %all-gather.2.cloned.1.call-start = ((), (), s32[]{:S(2)}) async-start(), calls=%async_computation.1 | async-start | bytes 9461760 | tf_op jit(solution)/shard_map/all_gather | solution.py:996
  8.2 35.6 %collective-permute-start = (bf16[144,256]{1,0:T(8,128)(2,1)S(1)}, bf16[144,256]{1,0:T(8,128)(2,1)S(1)}, u32[]{:S(2)}, u32[]{:S(2)}) collective-permute-start(bf16[144,256]{1,0:T(8,128)(2,1)S(1)} %constant_dynamic-slice_fusion), channel_id=1, source_target_pairs={{0,0},{8,32},{16,64},{24,96},{32,8},{40,40},{48,72},{56,104},{64,1... | collective-permute-start | bytes 221192 | tf_op jit(solution)/shard_map/ppermute | solution.py:979
  18.9 28.2 %copy-start.4 = (f32[64]{0:T(128)S(1)}, f32[64]{0:T(128)}, u32[]{:S(2)}) copy-start(f32[64]{0:T(128)} %param.26) | copy-start | bytes 772
  18.9 28.2 %copy-start.5 = (f32[64]{0:T(128)S(1)}, f32[64]{0:T(128)}, u32[]{:S(2)}) copy-start(f32[64]{0:T(128)} %param.27) | copy-start | bytes 772
  44.6 201.0 %reduce-scatter.2.cloned.1.call-start = ((), (), s32[]{:S(2)}) async-start(), calls=%async_computation.2 | async-start | bytes 7299072 | tf_op jit(solution)/shard_map/reduce_scatter | solution.py:1012
  243.4 25.0 %copy-start.2 = (bf16[160,1024]{1,0:T(8,128)(2,1)S(1)}, bf16[160,1024]{1,0:T(8,128)(2,1)}, u32[]{:S(2)}) copy-start(bf16[160,1024]{1,0:T(8,128)(2,1)} %get-tuple-element.88) | copy-start | bytes 983044
  243.4 25.8 %copy-start.1 = (bf16[160,1024]{1,0:T(8,128)(2,1)S(1)}, bf16[160,1024]{1,0:T(8,128)(2,1)}, u32[]{:S(2)}) copy-start(bf16[160,1024]{1,0:T(8,128)(2,1)} %get-tuple-element.89) | copy-start | bytes 983044
Sparse Core Ops, SparseCore 0:
  44.8 65.6 all-gather.1
  148.8 96.8 reduce-scatter.1

commit v5 on v4

--- a/solution.py
+++ b/solution.py
@@ -234,21 +234,179 @@
     return lax.dot_general(a, b, (((0,), (0,)), ((), ())), preferred_element_type=F32)
 
 
+def my_pairs(pairs):
+    x, z, _, _ = coords()
+    line = sequence_at(x, z) * 8
+    return [pairs[line, j] for j in range(16)]
+
+
 def rows_of(block):
     return pl.ds(pl.multiple_of(block * BLK, 16), BLK)
 
 
-def rope_rows(blocks, table, s):
-    return jnp.concatenate([table[rows_of(blocks[2 * s]), :], table[rows_of(blocks[2 * s + 1]), :]], 0)
-
-
-def project_kernel(blocks, h, w, cos_t, sin_t, g_q, g_k, send, raw, cos_o, sin_o, acc):
+def rope_rows(block, table):
+    return jnp.concatenate([table[rows_of(block), :], table[rows_of(31 - block), :]], 0)
+
+
+def gather_in_kernel(
+    tokens,
+    g_attn,
+    w_q,
+    w_k,
+    w_v,
+    pairs,
+    h_o,
+    w_o,
+    pairs_o,
+    h,
+    w,
+    row,
+    ss_h,
+    rs_h,
+    ss_p,
+    rs_p,
+    ss_w,
+    rs_w,
+    ss_f,
+    rs_f,
+    own_sem,
+):
+    x, z, y, c = coords()
+    ctx = z * 4 + y
+    barrier = pltpu.get_barrier_semaphore()
+    for k in range(1, NX):
+        pl.semaphore_signal(
+            barrier, inc=1, device_id=(lax.rem(x + k, NX), z, y, c), device_id_type=MESH
+        )
+    pl.semaphore_signal(barrier, inc=1, device_id=(x, z, y, 1 - c), device_id_type=MESH)
+
+    def greet(k, carry):
+        t = lax.rem(ctx + k, 16)
+        dev = (x, t // 4, lax.rem(t, 4), c)
+        pl.semaphore_signal(barrier, inc=1, device_id=dev, device_id_type=MESH)
+        return carry
+
+    lax.fori_loop(1, 16, greet, 0)
+    w[:, :QX] = w_q[:, pl.ds(pl.multiple_of(x * QX, QX), QX)]
+    w[:, QX : QX + KX] = w_k[:, pl.ds(pl.multiple_of(x * KX, KX), KX)]
+    w[:, QX + KX :] = w_v[:, pl.ds(pl.multiple_of(x * KX, KX), KX)]
+    row[...] = jnp.zeros_like(row)
+    row[0:1, :16] = pairs[...]
+    inputs = tokens[...].astype(F32)
+    inv_rms = lax.rsqrt(jnp.mean(inputs * inputs, axis=-1, keepdims=True) + EPSILON)
+    h[...] = (inputs * inv_rms * g_attn[...]).astype(BF16)
+
+    def along_x(src, dst, ss, rs, t, place):
+        return pltpu.make_async_remote_copy(
+            src_ref=src,
+            dst_ref=dst.at[place],
+            send_sem=ss.at[t],
+            recv_sem=rs.at[place],
+            device_id=(t, z, y, c),
+            device_id_type=MESH,
+        )
+
+    def over_ctx(t, place):
+        return pltpu.make_async_remote_copy(
+            src_ref=w,
+            dst_ref=w_o.at[place * 2 + c],
+            send_sem=ss_w.at[t],
+            recv_sem=rs_w.at[place],
+            device_id=(x, t // 4, lax.rem(t, 4), c),
+            device_id_type=MESH,
+        )
+
+    def to_sibling(t, core, src):
+        return pltpu.make_async_remote_copy(
+            src_ref=src,
+            dst_ref=w_o.at[t * 2 + core],
+            send_sem=ss_f.at[t],
+            recv_sem=rs_f.at[t],
+            device_id=(x, z, y, 1 - c),
+            device_id_type=MESH,
+        )
+
+    mine = [
+        pltpu.make_async_copy(h, h_o.at[x], own_sem.at[0]),
+        pltpu.make_async_copy(row, pairs_o.at[x], own_sem.at[1]),
+        pltpu.make_async_copy(w, w_o.at[ctx * 2 + c], own_sem.at[2]),
+    ]
+    for copy in mine:
+        copy.start()
+    pl.semaphore_wait(barrier, NX + 15)
+    for k in (1, 3, 2):
+        t = lax.rem(x + k, NX)
+        along_x(h, h_o, ss_h, rs_h, t, x).start()
+        along_x(row, pairs_o, ss_p, rs_p, t, x).start()
+
+    def send(k, carry):
+        over_ctx(lax.rem(ctx + k, 16), ctx).start()
+        return carry
+
+    lax.fori_loop(1, 16, send, 0)
+    to_sibling(ctx, c, w).start()
+
+    def forward(k, carry):
+        t = lax.rem(ctx + k, 16)
+        over_ctx(t, t).wait_recv()
+        to_sibling(t, c, w_o.at[t * 2 + c]).start()
+        return carry
+
+    lax.fori_loop(1, 16, forward, 0)
+
+    def drain(k, carry):
+        t = lax.rem(ctx + k, 16)
+        to_sibling(t, 1 - c, w).wait_recv()
+        to_sibling(t, c, w).wait_send()
+        return carry
+
+    lax.fori_loop(0, 16, drain, 0)
+
+    def drain_ctx(k, carry):
+        over_ctx(lax.rem(ctx + k, 16), ctx).wait_send()
+        return carry
+
+    lax.fori_loop(1, 16, drain_ctx, 0)
+    for k in (1, 3, 2):
+        t = lax.rem(x + k, NX)
+        along_x(h, h_o, ss_h, rs_h, t, x).wait_send()
+        along_x(row, pairs_o, ss_p, rs_p, t, x).wait_send()
+        along_x(h, h_o, ss_h, rs_h, t, t).wait_recv()
+        along_x(row, pairs_o, ss_p, rs_p, t, t).wait_recv()
+    for copy in mine:
+        copy.wait()
+
+
+def gather_in(number, *operands):
+    wide = QX + 2 * KX
+    return pl.pallas_call(
+        gather_in_kernel,
+        in_specs=[pl.BlockSpec(memory_space=pltpu.VMEM)] * 6,
+        out_specs=[pl.BlockSpec(memory_space=pl.ANY)] * 3,
+        out_shape=[
+            jax.ShapeDtypeStruct((NX, ROWS, D), BF16),
+            jax.ShapeDtypeStruct((32, 32, wide), BF16),
+            jax.ShapeDtypeStruct((NX, 8, 128), jnp.int32),
+        ],
+        scratch_shapes=[
+            pltpu.VMEM((ROWS, D), BF16),
+            pltpu.VMEM((32, wide), BF16),
+            pltpu.VMEM((8, 128), jnp.int32),
+        ]
+        + [pltpu.SemaphoreType.DMA((n,)) for n in (NX, NX, NX, NX, 16, 16, 16, 16, 3)],
+        compiler_params=pltpu.CompilerParams(collective_id=number, has_side_effects=True),
+        name="gather_in",
+    )(*operands)
+
+
+def project_kernel(pairs, h, w, cos_t, sin_t, g_q, g_k, send, raw, cos_o, sin_o, acc):
+    x, z, y, _ = coords()
     acc[...] = nn(h[...], w[...])
     m = low_half((ROWS, 2 * HD))
     mh = low_half((BLK, 2 * HD))
     for s in range(NX):
         at = slice(s * ROWS, (s + 1) * ROWS)
-        cos_r, sin_r = rope_rows(blocks, cos_t, s), rope_rows(blocks, sin_t, s)
+        cos_r, sin_r = (rope_rows(pairs[s * 8, z * 4 + y], table) for table in (cos_t, sin_t))
         cos_o[at, :], sin_o[at, :] = cos_r, sin_r
         raw[at, :] = acc[at, : QX + KX]
         turned = []
@@ -266,11 +424,11 @@
             q = turned[hh // 2]
             q = q if hh % 2 == 0 else swap(q)
             k = swapped_keys if hh < 2 else keys
-            send[blocks[8 + s] * 4 + hh, :ROWS, :] = jnp.where(m, q, k).astype(BF16)
-            send[blocks[8 + s] * 4 + hh, ROWS:, :] = packed[hh // 2].astype(BF16)
-
-
-def project(blocks, h, w, cos_t, sin_t, g_q, g_k):
+            send[place_of(x, s) * 4 + hh, :ROWS, :] = jnp.where(m, q, k).astype(BF16)
+            send[place_of(x, s) * 4 + hh, ROWS:, :] = packed[hh // 2].astype(BF16)
+
+
+def project(pairs, h, w, cos_t, sin_t, g_q, g_k):
     return pl.pallas_call(
         project_kernel,
         grid_spec=pltpu.PrefetchScalarGridSpec(
@@ -287,11 +445,12 @@
         ],
         compiler_params=pltpu.CompilerParams(vmem_limit_bytes=VMEM_BYTES),
         name="project",
-    )(blocks, h, w, cos_t, sin_t, g_q, g_k)
-
-
-def attend_kernel(pair, recv, out, q_s, k_s, v_s, o_t, inv, o_s, v_t):
+    )(pairs, h, w, cos_t, sin_t, g_q, g_k)
+
+
+def attend_kernel(pairs, recv, out, q_s, k_s, v_s, o_t, inv, o_s, v_t):
     m = low_half((BLK, 2 * HD))
+    pair = my_pairs(pairs)
     for j in range(16):
         packed = recv[j, ROWS:, :].astype(F32)
         for half in range(2):
@@ -331,7 +490,7 @@
         out[j, :, :] = (low_rows + swap(high_rows)).astype(BF16)
 
 
-def attend(pair, recv):
+def attend(pairs, recv):
     wide = jax.ShapeDtypeStruct((LEN, 2 * HD), BF16)
     return pl.pallas_call(
         attend_kernel,
@@ -351,11 +510,12 @@
         ],
         compiler_params=pltpu.CompilerParams(vmem_limit_bytes=VMEM_BYTES),
         name="attend",
-    )(pair, recv)
-
-
-def attend_back_kernel(pair, recv, q_s, k_s, v_s, o_t, inv, out, g_s, k_t, delta, dq_t, dk_s, dv_s):
+    )(pairs, recv)
+
+
+def attend_back_kernel(pairs, recv, q_s, k_s, v_s, o_t, inv, out, g_s, k_t, delta, dq_t, dk_s, dv_s):
     m = low_half((BLK, 2 * HD))
+    pair = my_pairs(pairs)
     for j in range(16):
         packed = recv[j, :, :].astype(F32)
         g_s[rows_of(pair[j]), :] = jnp.where(m, packed, 0.0).astype(BF16)
@@ -402,7 +562,7 @@
         out[j, ROWS:, :] = (dv_s[rows_of(pair[j]), :] + swap(dv_s[rows_of(31 - pair[j]), :])).astype(BF16)
 
 
-def attend_back(pair, recv, q_s, k_s, v_s, o_t, inv):
+def attend_back(pairs, recv, q_s, k_s, v_s, o_t, inv):
     return pl.pallas_call(
         attend_back_kernel,
         grid_spec=pltpu.PrefetchScalarGridSpec(
@@ -421,7 +581,7 @@
         out_shape=jax.ShapeDtypeStruct((16, ROWS + BLK, 2 * HD), BF16),
         compiler_params=pltpu.CompilerParams(vmem_limit_bytes=VMEM_BYTES),
         name="attend_back",
-    )(pair, recv, q_s, k_s, v_s, o_t, inv)
+    )(pairs, recv, q_s, k_s, v_s, o_t, inv)
 
 
 def middle_kernel(
@@ -935,21 +1095,12 @@
     return np.concatenate([cos] * 4, 1), np.concatenate([-sin, sin, -sin, sin], 1)
 
 
-def rms_rows(values_in, gain):
-    inv_rms = lax.rsqrt(jnp.mean(values_in * values_in, axis=-1, keepdims=True) + EPSILON)
-    return (values_in * inv_rms * gain, inv_rms)
-
-
 def columns_of(w, x, width):
     return lax.dynamic_slice_in_dim(w, x * width, width, axis=1)
 
 
 def by_tiles(blocks):
     return blocks.reshape(-1, 9, 16, 2, 128).transpose(0, 3, 2, 1, 4).reshape(-1, 32, FX)
-
-
-def from_tiles(blocks):
-    return blocks.reshape(-1, 2, 16, 9, 128).transpose(0, 3, 2, 1, 4).reshape(-1, FF // 32, D // 4)
 
 
 def body(
@@ -968,8 +1119,7 @@
     g_ffn,
     cotangent,
 ):
-    x, z, y, c = coords()
-    ctx = z * 4 + y
+    x = lax.axis_index("seq")
     cos_np, sin_np = angle_constants()
     cos_t, sin_t = jnp.asarray(cos_np), jnp.asarray(sin_np)
     gq2 = jnp.concatenate([g_query, g_query])[None]
@@ -982,27 +1132,13 @@
         axis=1,
     )
 
-    inputs = tokens[0].astype(F32)
-    normed_attn, _ = rms_rows(inputs, g_attn)
-    h_attn = normed_attn.astype(BF16)
-    w_x = jnp.concatenate(
-        [columns_of(w_query, x, QX), columns_of(w_key, x, KX), columns_of(w_value, x, KX)], axis=1
-    )
-    pairs_pad = jnp.pad(pairs, ((0, 7), (0, 112)))
-    h_all, w_qkv, pairs_all = exchange(
-        1, "gather_in", ("x", "ag", h_attn), ("p", "ag", w_x), ("x", "ag", pairs_pad)
-    )
-    h_all, mine = lax.optimization_barrier((h_all, mine))
     wide = lax.all_gather(mine, CTX_FSDP, axis=0, tiled=True)
+    h_all, w_qkv, pair = gather_in(1, tokens[0], g_attn[None], w_query, w_key, w_value, pairs)
     h_all = h_all.reshape(NX * ROWS, D)
     w_qkv = w_qkv.reshape(D, QX + 2 * KX)
-    pairs_all = pairs_all[:, 0, :16]
-    first = lax.dynamic_slice_in_dim(pairs_all, ctx, 1, axis=1)[:, 0]
-    places = jnp.stack([place_of(x, s) for s in range(4)])
-    blocks = jnp.concatenate([jnp.stack([first, 31 - first], axis=1).reshape(8), places])
-    pair = lax.dynamic_slice_in_dim(pairs_all, sequence_at(x, z), 1, axis=0)[0]
-
-    send, raw, cos_r, sin_r = project(blocks, h_all, w_qkv, cos_t, sin_t, gq2, gk2)
+    pair = pair.reshape(NX * 8, 128)
+
+    send, raw, cos_r, sin_r = project(pair, h_all, w_qkv, cos_t, sin_t, gq2, gk2)
     recv, cot_all = exchange(2, "to_heads", ("c", "a2a", send), ("x", "ag", cotangent[0]))
     heads_out, q_s, k_s, v_s, o_t, inv = attend(pair, recv)
     (mixed_parts,) = exchange(3, "to_tokens", ("t", "a2a", heads_out))

time: 277 us -> 269 us (0.971)
  local copies, waits for them, and re-layouts: 9.64 us -> 4.67 us
  other arithmetic: 4.94 us -> 2.16 us
    pallas_call x6 -> x5, Pallas kernels: 114 us -> 90.6 us  [exchange(): pl.pallas_call(functools.partial(exchange_kernel, items), out_shape=outs,...]
    pallas_call x0 -> x1, Pallas kernels: none -> 23.5 us  [gather_in(): pl.pallas_call(gather_in_kernel, in_specs=[pl.BlockSpec(memory_space=pltp...]
    all_gather x1, waiting for transfers between devices: 9.65 us -> 0.02 us  [body(): wide = lax.all_gather(mine, CTX_FSDP, axis=0, tiled=True)]
    reduce_scatter x1, waiting for transfers between devices: 2.26 us -> 8.91 us  [body(): lax.psum_scatter(grad_w_ffn, CTX_FSDP, scatter_dimension=0, tiled=True)]
    ppermute x1, waiting for transfers between devices: 0.01 us -> 4.27 us  [body(): lax.ppermute(columns_of(w_down, x, D // 4), ('seq', 'ctx_0'), swap_xz)]
  transfers between devices with their start and end apart: 3 -> 3, of which waited for: 2 -> 2; matrix products, arithmetic and copies ran while one was open for 4% -> 1% of each run, Pallas kernels for 62% -> 64%
where the time goes in v5:
time: 269 us; the launch traced here: 268 us
  Pallas kernels  228 us (85%)
  between operations  14.2 us (5%)
  waiting for transfers between devices  13.2 us (5%)
  starting transfers between devices  5.81 us (2%)
  local copies, waits for them, and re-layouts  4.67 us (2%)
    pallas_call x5, Pallas kernels, exchange(): pl.pallas_call(functools.partial(exchange_kernel, items), out_shape=outs,...  90.6 us
    pallas_call x1, Pallas kernels, project_back(): pl.pallas_call(project_back_kernel, in_specs=[vmem] * 16, out_specs=[vmem...  38.3 us
    pallas_call x1, Pallas kernels, middle_part(): pl.pallas_call(middle_kernel, in_specs=[vmem] * 4 + [pl.BlockSpec(memory_...  36.8 us
    pallas_call x1, Pallas kernels, gather_in(): pl.pallas_call(gather_in_kernel, in_specs=[pl.BlockSpec(memory_space=pltp...  23.5 us
    pallas_call x1, Pallas kernels, attend_back(): pl.pallas_call(attend_back_kernel, grid_spec=pltpu.PrefetchScalarGridSpec...  18.2 us
    pallas_call x1, Pallas kernels, attend(): pl.pallas_call(attend_kernel, grid_spec=pltpu.PrefetchScalarGridSpec(num_...  10.7 us
    reduce_scatter x1, waiting for transfers between devices, body(): lax.psum_scatter(grad_w_ffn, CTX_FSDP, scatter_dimension=0, tiled=True)  8.91 us
    pallas_call x1, Pallas kernels, project(): pl.pallas_call(project_kernel, grid_spec=pltpu.PrefetchScalarGridSpec(num...  7.18 us
  transfers between devices with their start and end apart: 3, of which 2 were waited for; matrix products, arithmetic and copies ran while one was open for 1% of the time, Pallas kernels for 64%

profile of v5, /device:TPU:4, one launch (start us, length us, event | category | flops | bytes accessed | tf_op | source)
XLA Modules:
  0.0 268.1 jit_solution(5376200010219195006)
XLA Ops:
  7.2 0.0 copy-start
  7.2 0.0 copy-start.4
  7.2 0.0 copy-start.3
  7.2 0.0 all-gather.2.cloned.1.call-start
  7.3 0.9 copy-done
  8.2 5.7 %collective-permute-start = (bf16[144,256]{1,0:T(8,128)(2,1)S(1)}, bf16[144,256]{1,0:T(8,128)(2,1)S(1)}, u32[]{:S(2)}, u32[]{:S(2)}) collective-permute-start(bf16[144,256]{1,0:T(8,128)(2,1)S(1)} %constant_dynamic-slice_fusion), channel_id=1, source_target_pairs={{0,0},{8,32},{16,64},{24,96},{32,8},{40,40},{48,72},{56,104},{64,1... | collective-permute-start | bytes 221192 | tf_op jit(solution)/shard_map/ppermute | solution.py:1129
  13.9 0.9 constant_dynamic-slice_fusion.1
  14.8 4.3 %collective-permute-done = bf16[144,256]{1,0:T(8,128)(2,1)S(1)} collective-permute-done((bf16[144,256]{1,0:T(8,128)(2,1)S(1)}, bf16[144,256]{1,0:T(8,128)(2,1)S(1)}, u32[]{:S(2)}, u32[]{:S(2)}) %collective-permute-start) | collective-permute-done | bytes 73760 | tf_op jit(solution)/shard_map/ppermute | solution.py:1129
  19.2 1.6 pad_maximum_fusion
  20.8 0.0 all-gather.2.cloned.1.call-update
  20.8 0.0 reduce-scatter.2.cloned.1.call-start
  20.9 23.5 %gather_in.1 = (bf16[4,160,1024]{2,1,0:T(8,128)(2,1)}, bf16[32,32,512]{2,1,0:T(8,128)(2,1)}, s32[4,8,128]{2,1,0:T(8,128)}) custom-call(bf16[160,1024]{1,0:T(8,128)(2,1)} %bitcast.29, f32[1,1024]{1,0:T(1,128)} %bitcast.40, bf16[32,1024]{1,0:T(8,128)(2,1)} %w_q.1, bf16[32,512]{1,0:T(8,128)(2,1)} %w_k.1, bf16[32,512]{1,0:T(8,128)(2,1)} %w_v.1, s32[1,16]{1,0:T(1,128)} %pairs.1), custom_call_target="tpu_custom_call" | custom-call | tf_op jit(solution)/shard_map/gather_in/pallas_call | solution.py:382
  44.4 0.0 copy-done.4
  44.4 0.0 copy-done.3
  44.4 0.6 maximum_bitcast_fusion
  45.0 7.2 %project.1 = (bf16[16,240,128]{2,1,0:T(8,128)(2,1)}, f32[640,384]{1,0:T(8,128)}, f32[640,128]{1,0:T(8,128)}, f32[640,128]{1,0:T(8,128)}) custom-call(s32[32,128]{1,0:T(8,128)} %bitcast.37, bf16[640,1024]{1,0:T(8,128)(2,1)} %bitcast.25, bf16[1024,512]{1,0:T(8,128)(2,1)} %bitcast.27, f32[2560,128]{1,0:T(8,128)} %constant.20.clone.cos_t, ...), custom_call_target="tpu_custom_call" | custom-call | tf_op jit(solution)/shard_map/project/pallas_call | solution.py:432
  52.2 25.9 %to_heads.1 = (bf16[16,240,128]{2,1,0:T(8,128)(2,1)}, bf16[4,160,1024]{2,1,0:T(8,128)(2,1)}) custom-call(bf16[16,240,128]{2,1,0:T(8,128)(2,1)} %get-tuple-element.62.refs_0_, bf16[160,1024]{1,0:T(8,128)(2,1)} %bitcast.33), custom_call_target="tpu_custom_call" | custom-call | tf_op jit(solution)/shard_map/to_heads/pallas_call | solution.py:190
  78.1 10.7 %attend.1 = (bf16[16,80,128]{2,1,0:T(8,128)(2,1)}, bf16[2560,128]{1,0:T(8,128)(2,1)}, bf16[2560,128]{1,0:T(8,128)(2,1)}, bf16[2560,128]{1,0:T(8,128)(2,1)}, f32[64,2560]{1,0:T(8,128)}, /*index=5*/f32[8,2560]{1,0:T(8,128)}) custom-call(s32[32,128]{1,0:T(8,128)} %bitcast.38, bf16[16,240,128]{2,1,0:T(8,128)(2,1)} %get-tuple-element.63.recv), custom_call_target="tpu_custom_call" | custom-call | tf_op jit(solution)/shard_map/attend/pallas_call | solution.py:495
  88.8 14.3 %to_tokens.1.parts = bf16[16,80,128]{2,1,0:T(8,128)(2,1)} custom-call(bf16[16,80,128]{2,1,0:T(8,128)(2,1)} %get-tuple-element.64.refs_0_), custom_call_target="tpu_custom_call" | custom-call | tf_op jit(solution)/shard_map/to_tokens/pallas_call | solution.py:190
  103.2 0.0 all-gather.2.cloned.1.call-done.wide
  103.2 36.8 %middle_part.1 = (f32[160,1024]{1,0:T(8,128)}, bf16[4,160,1024]{2,1,0:T(8,128)(2,1)}, bf16[1024,3456]{1,0:T(8,128)(2,1)}, f32[160,1024]{1,0:T(8,128)}, bf16[160,...) custom-call(bf16[16,80,128]{2,1,0:T(8,128)(2,1)} %to_tokens.1.parts, ...), custom_call_target="tpu_custom_call" | custom-call | tf_op jit(solution)/shard_map/middle_part/pallas_call | solution.py:764
  140.0 0.0 reduce-scatter.2.cloned.1.call-update
  140.0 15.7 %to_heads_back.1.recv = bf16[16,80,128]{2,1,0:T(8,128)(2,1)} custom-call(bf16[16,80,128]{2,1,0:T(8,128)(2,1)} %get-tuple-element.66.refs_0_), custom_call_target="tpu_custom_call" | custom-call | tf_op jit(solution)/shard_map/to_heads_back/pallas_call | solution.py:190
  155.7 18.2 %attend_back.1.refs_0_ = bf16[16,240,128]{2,1,0:T(8,128)(2,1)} custom-call(s32[32,128]{1,0:T(8,128)} %bitcast.39, bf16[16,80,128]{2,1,0:T(8,128)(2,1)} %to_heads_back.1.recv, bf16[2560,128]{1,0:T(8,128)(2,1)} %get-tuple-element.67.q_s, bf16[2560,128]{1,0:T(8,128)(2,1)} %get-tuple-element.68.k_s, bf16[2560,128]{1,0:T(8,128)(2,1)} %get-tuple-element.69.v_s, ...), custom_call_target="tpu_custom_call" | custom-call | tf_op jit(solution)/shard_map/attend_back/pallas_call | solution.py:566
  174.0 16.9 %to_tokens_back.1 = (bf16[16,240,128]{2,1,0:T(8,128)(2,1)}, bf16[4,160,1024]{2,1,0:T(8,128)(2,1)}, bf16[4,160,256]{2,1,0:T(8,128)(2,1)}) custom-call(bf16[16,240,128]{2,1,0:T(8,128)(2,1)} %attend_back.1.refs_0_, bf16[160,1024]{1,0:T(8,128)(2,1)} %get-tuple-element.72.refs_1_, bf16[4,160,256]{2,1,0:T(8,128)(2,1)} %get-tuple-element.73.refs_2_), custom_call_target="tpu_custom_call" | custom-call | tf_op jit(solution)/shard_map/to_tokens_back/pallas_call | solution.py:190
  190.8 38.3 %project_back.1 = (bf16[160,1024]{1,0:T(8,128)(2,1)}, bf16[160,1024]{1,0:T(8,128)(2,1)}, bf16[32,512]{1,0:T(8,128)(2,1)}, bf16[32,256]{1,0:T(8,128)(2,1)}, f32[24,128]{1,0:T(8,128)}) custom-call(bf16[16,240,128]{2,1,0:T(8,128)(2,1)} %get-tuple-element.74.recv, f32[640,384]{1,0:T(8,128)} %get-tuple-element.75.raw, bf16[640,1024]{1,0:T(8,128)(2,1)} %bitcast.26, ...), custom_call_target="tpu_custom_call" | custom-call | tf_op jit(solution)/shard_map/project_back/pallas_call | solution.py:1023
  229.1 0.0 copy-start.2
  229.1 0.0 copy-start.1
  229.1 8.9 %reduce-scatter.2.cloned.1.call-done.refs_1_.refs_3_ = bf16[32,3456]{1,0:T(8,128)(2,1)} async-done(((bf16[1024,3456]{1,0:T(8,128)(2,1)}), bf16[32,3456]{1,0:T(8,128)(2,1)}) %reduce-scatter.2.cloned.1.call-update) | async-done | bytes 221200 | tf_op jit(solution)/shard_map/reduce_scatter | solution.py:1148
  238.0 17.8 %gather_out.1 = (bf16[4,32,512]{2,1,0:T(8,128)(2,1)}, bf16[4,32,2304]{2,1,0:T(8,128)(2,1)}, bf16[4,32,256]{2,1,0:T(8,128)(2,1)}, bf16[4,32,1152]{2,1,0:T(8,128)(2,1)}, f32[4,24,128]{2,1,0:T(8,128)}) custom-call(bf16[32,512]{1,0:T(8,128)(2,1)} %get-tuple-element.86.refs_0_, bf16[32,3456]{1,0:T(8,128)(2,1)} %reduce-scatter.2.cloned.1.call-done.refs_1_.refs_3_, ...), custom_call_target="tpu_custom_call" | custom-call | tf_op jit(solution)/shard_map/gather_out/pallas_call | solution.py:190
  255.9 2.6 hand_out.1
  258.5 1.3 slice_bitcast_fusion
  259.8 0.0 copy-done.2
  259.8 0.7 copy.36
  260.5 0.0 copy-done.1
  260.5 0.7 copy.37
  (4 shorter events, 0.1 us)
Async XLA Ops:
  7.2 1.0 copy-start
  7.2 37.2 %copy-start.4 = (f32[64]{0:T(128)S(1)}, f32[64]{0:T(128)}, u32[]{:S(2)}) copy-start(f32[64]{0:T(128)} %param.27) | copy-start | bytes 772
  7.2 37.2 %copy-start.3 = (f32[64]{0:T(128)S(1)}, f32[64]{0:T(128)}, u32[]{:S(2)}) copy-start(f32[64]{0:T(128)} %param.26) | copy-start | bytes 772
  7.2 96.0 %all-gather.2.cloned.1.call-start = ((), (), s32[]{:S(2)}) async-start(), calls=%async_computation.1 | async-start | bytes 9461760 | tf_op jit(solution)/shard_map/all_gather | solution.py:1135
  8.2 11.0 %collective-permute-start = (bf16[144,256]{1,0:T(8,128)(2,1)S(1)}, bf16[144,256]{1,0:T(8,128)(2,1)S(1)}, u32[]{:S(2)}, u32[]{:S(2)}) collective-permute-start(bf16[144,256]{1,0:T(8,128)(2,1)S(1)} %constant_dynamic-slice_fusion), channel_id=1, source_target_pairs={{0,0},{8,32},{16,64},{24,96},{32,8},{40,40},{48,72},{56,104},{64,1... | collective-permute-start | bytes 221192 | tf_op jit(solution)/shard_map/ppermute | solution.py:1129
  20.8 217.2 %reduce-scatter.2.cloned.1.call-start = ((), (), s32[]{:S(2)}) async-start(), calls=%async_computation.2 | async-start | bytes 7299072 | tf_op jit(solution)/shard_map/reduce_scatter | solution.py:1148
  229.1 30.7 %copy-start.2 = (bf16[160,1024]{1,0:T(8,128)(2,1)S(1)}, bf16[160,1024]{1,0:T(8,128)(2,1)}, u32[]{:S(2)}) copy-start(bf16[160,1024]{1,0:T(8,128)(2,1)} %get-tuple-element.84) | copy-start | bytes 983044
  229.1 31.4 %copy-start.1 = (bf16[160,1024]{1,0:T(8,128)(2,1)S(1)}, bf16[160,1024]{1,0:T(8,128)(2,1)}, u32[]{:S(2)}) copy-start(bf16[160,1024]{1,0:T(8,128)(2,1)} %get-tuple-element.85) | copy-start | bytes 983044
Sparse Core Ops, SparseCore 0:
  20.9 65.4 all-gather.1
  140.2 97.8 reduce-scatter.1

commit v6 on v5

--- a/solution.py
+++ b/solution.py
@@ -611,11 +611,15 @@
     hid,
     h_t,
     hid_t,
+    dw,
+    sibling_dw,
     wsem,
     ss1,
     rs1,
     ss2,
     rs2,
+    ss3,
+    rs3,
 ):
     me, z, y, c = coords()
     barrier = pltpu.get_barrier_semaphore()
@@ -623,6 +627,7 @@
         pl.semaphore_signal(
             barrier, inc=1, device_id=(lax.rem(me + k, NX), z, y, c), device_id_type=MESH
         )
+    pl.semaphore_signal(barrier, inc=1, device_id=(me, z, y, 1 - c), device_id_type=MESH)
     loads = [
         pltpu.make_async_copy(wide.at[:, pl.ds(at, width)], there, wsem.at[i])
         for i, (at, width, there) in enumerate(
@@ -644,7 +649,7 @@
     mid_o[...] = middle
     r = lax.rsqrt(jnp.mean(middle * middle, axis=-1, keepdims=True) + EPSILON)
     h_all[me] = (middle * r * g_ffn[...]).astype(BF16)
-    pl.semaphore_wait(barrier, NX - 1)
+    pl.semaphore_wait(barrier, NX)
 
     def send_h(t, place):
         return pltpu.make_async_remote_copy(
@@ -713,14 +718,17 @@
 
     lax.fori_loop(0, NX, block, 0)
 
-    h_t[...] = h_all[...].reshape(NX * ROWS, D).T
-
-    def columns(j, carry):
-        at = pl.ds(pl.multiple_of(j * 256, 256), 256)
-        dw_o[:, at] = nn(h_t[...], ggu[:, at]).astype(BF16)
-        return carry
-
-    lax.fori_loop(0, 2 * FX // 256, columns, 0)
+    def to_sibling(i, at):
+        return pltpu.make_async_remote_copy(
+            src_ref=dw.at[pl.ds(pl.multiple_of((1 - c) * 512, 512), 512), at],
+            dst_ref=sibling_dw.at[:, at],
+            send_sem=ss3.at[i],
+            recv_sem=rs3.at[i],
+            device_id=(me, z, y, 1 - c),
+            device_id_type=MESH,
+        )
+
+    down = pl.ds(2 * FX, FX)
     hid_t[...] = hid[...].T
     for q in range(NX):
         cot_q = cot[:, :, q * 256 : (q + 1) * 256].reshape(NX * ROWS, 256)
@@ -728,10 +736,26 @@
         for o in range(8):
             for rg in range(9):
                 for l in range(2):
-                    row, there = o * 144 + rg * 16, (q * 8 + o) * 32 + l * 16
-                    dw_o[there : there + 16, 2 * FX + rg * 128 : 2 * FX + rg * 128 + 128] = grad[
+                    row = o * 144 + rg * 16
+                    there = ((o % 2) * 16 + (o // 2) * 4 + q) * 32 + l * 16
+                    dw[there : there + 16, 2 * FX + rg * 128 : 2 * FX + rg * 128 + 128] = grad[
                         row : row + 16, l * 128 : l * 128 + 128
                     ]
+    to_sibling(9, down).start()
+    h_rows = h_all[...].reshape(NX * ROWS, D).T
+    for o in range(32):
+        there = ((o % 2) * 16 + (o // 2 % 4) * 4 + o // 8) * 32
+        h_t[there : there + 32, :] = h_rows[o * 32 : o * 32 + 32, :]
+
+    def chunk(j):
+        return pl.ds(pl.multiple_of(j * 256, 256), 256)
+
+    def columns(j, carry):
+        dw[:, chunk(j)] = nn(h_t[...], ggu[:, chunk(j)]).astype(BF16)
+        to_sibling(j, chunk(j)).start()
+        return carry
+
+    lax.fori_loop(0, 2 * FX // 256, columns, 0)
 
     grad_h = part[me].astype(F32)
     for k in (1, 3, 2):
@@ -756,6 +780,20 @@
             top, bottom = grad[:BLK, p * 128 : p * 128 + 128], grad[BLK:, p * 128 : p * 128 + 128]
             back_o[4 * q + 2 * p, :, :] = jnp.where(m, top, swap(bottom)).astype(BF16)
             back_o[4 * q + 2 * p + 1, :, :] = jnp.where(m, swap(top), bottom).astype(BF16)
+    half = pl.ds(pl.multiple_of(c * 512, 512), 512)
+
+    def both(at):
+        dw_o[:, at] = (dw[half, at].astype(F32) + sibling_dw[:, at].astype(F32)).astype(BF16)
+
+    to_sibling(9, down).wait()
+    both(down)
+
+    def add(j, carry):
+        to_sibling(j, chunk(j)).wait()
+        both(chunk(j))
+        return carry
+
+    lax.fori_loop(0, 2 * FX // 256, add, 0)
 
 
 def middle_part(number, parts, tokens, cot, g_ffn, wide):
@@ -768,7 +806,7 @@
         out_shape=[
             jax.ShapeDtypeStruct((ROWS, D), F32),
             jax.ShapeDtypeStruct(blocks, BF16),
-            jax.ShapeDtypeStruct((D, 3 * FX), BF16),
+            jax.ShapeDtypeStruct((D // 2, 3 * FX), BF16),
             jax.ShapeDtypeStruct((ROWS, D), F32),
             jax.ShapeDtypeStruct((ROWS, D), BF16),
             jax.ShapeDtypeStruct((NX, ROWS, QX), BF16),
@@ -789,11 +827,15 @@
             pltpu.VMEM((NX * ROWS, FX), BF16),
             pltpu.VMEM((D, NX * ROWS), BF16),
             pltpu.VMEM((FX, NX * ROWS), BF16),
+            pltpu.VMEM((D, 3 * FX), BF16),
+            pltpu.VMEM((D // 2, 3 * FX), BF16),
             pltpu.SemaphoreType.DMA((3,)),
             pltpu.SemaphoreType.DMA((NX,)),
             pltpu.SemaphoreType.DMA((NX,)),
             pltpu.SemaphoreType.DMA((NX,)),
             pltpu.SemaphoreType.DMA((NX,)),
+            pltpu.SemaphoreType.DMA((10,)),
+            pltpu.SemaphoreType.DMA((10,)),
         ],
         compiler_params=pltpu.CompilerParams(
             collective_id=number, has_side_effects=True, vmem_limit_bytes=VMEM_BYTES
@@ -1145,7 +1187,8 @@
     middle, result4, grad_w_ffn, grad_middle, grad_branch, mixed, back_parts, gain_ffn = middle_part(
         4, mixed_parts, tokens[0], cot_all, g_ffn[None], wide
     )
-    sums = lax.psum_scatter(grad_w_ffn, CTX_FSDP, scatter_dimension=0, tiled=True)
+    sums = lax.psum_scatter(grad_w_ffn, "ctx_1", scatter_dimension=0, tiled=True)
+    sums = lax.psum_scatter(sums, "ctx_0", scatter_dimension=0, tiled=True)
     (recv_g,) = exchange(6, "to_heads_back", ("r", "a2a", back_parts))
     sends_back = attend_back(pair, recv_g, q_s, k_s, v_s, o_t, inv)
     recv_back, branch_x, mixed_x = exchange(

time: 269 us -> 318 us (1.18)
  waiting for transfers between devices: 13.2 us -> 51.8 us
  Pallas kernels: 228 us -> 238 us
    reduce_scatter x1 -> x2, waiting for transfers between devices: 8.91 us -> 47.5 us  [the longest x1 47.4 us: body(): lax.psum_scatter(grad_w_ffn, 'ctx_1', scatter_dimension=0, tiled=True)]
    pallas_call x5, Pallas kernels: 90.6 us -> 96.2 us  [exchange(): pl.pallas_call(functools.partial(exchange_kernel, items), out_shape=outs,...]
  transfers between devices with their start and end apart: 3 -> 4, of which waited for: 2 -> 2; matrix products, arithmetic and copies ran while one was open for 1% -> 0% of each run, Pallas kernels for 64% -> 55%
where the time goes in v6:
time: 318 us; the launch traced here: 317 us
  Pallas kernels  238 us (75%)
  waiting for transfers between devices  51.8 us (16%)
  between operations  13.9 us (4%)
  starting transfers between devices  5.85 us (2%)
  local copies, waits for them, and re-layouts  4.67 us (1%)
    pallas_call x5, Pallas kernels, exchange(): pl.pallas_call(functools.partial(exchange_kernel, items), out_shape=outs,...  96.2 us
    reduce_scatter x1, waiting for transfers between devices, body(): lax.psum_scatter(grad_w_ffn, 'ctx_1', scatter_dimension=0, tiled=True)  47.4 us
    pallas_call x1, Pallas kernels, project_back(): pl.pallas_call(project_back_kernel, in_specs=[vmem] * 16, out_specs=[vmem...  40 us
    pallas_call x1, Pallas kernels, middle_part(): pl.pallas_call(middle_kernel, in_specs=[vmem] * 4 + [pl.BlockSpec(memory_...  39.8 us
    pallas_call x1, Pallas kernels, gather_in(): pl.pallas_call(gather_in_kernel, in_specs=[pl.BlockSpec(memory_space=pltp...  23.5 us
    pallas_call x1, Pallas kernels, attend_back(): pl.pallas_call(attend_back_kernel, grid_spec=pltpu.PrefetchScalarGridSpec...  18.1 us
    pallas_call x1, Pallas kernels, attend(): pl.pallas_call(attend_kernel, grid_spec=pltpu.PrefetchScalarGridSpec(num_...  10.7 us
    pallas_call x1, Pallas kernels, project(): pl.pallas_call(project_kernel, grid_spec=pltpu.PrefetchScalarGridSpec(num...  7.19 us
  transfers between devices with their start and end apart: 4, of which 2 were waited for; matrix products, arithmetic and copies ran while one was open for 0% of the time, Pallas kernels for 55%

profile of v6, /device:TPU:4, one launch (start us, length us, event | category | flops | bytes accessed | tf_op | source)
XLA Modules:
  0.0 316.7 jit_solution(200309402691860773)
XLA Ops:
  7.2 0.0 copy-start
  7.2 0.0 copy-start.4
  7.2 0.0 copy-start.3
  7.2 0.0 all-gather.2.cloned.1.call-start
  7.3 0.9 copy-done
  8.2 5.7 %collective-permute-start = (bf16[144,256]{1,0:T(8,128)(2,1)S(1)}, bf16[144,256]{1,0:T(8,128)(2,1)S(1)}, u32[]{:S(2)}, u32[]{:S(2)}) collective-permute-start(bf16[144,256]{1,0:T(8,128)(2,1)S(1)} %constant_dynamic-slice_fusion), channel_id=1, source_target_pairs={{0,0},{8,32},{16,64},{24,96},{32,8},{40,40},{48,72},{56,104},{64,1... | collective-permute-start | bytes 221192 | tf_op jit(solution)/shard_map/ppermute | solution.py:1171
  13.9 0.9 constant_dynamic-slice_fusion.1
  14.8 4.3 %collective-permute-done = bf16[144,256]{1,0:T(8,128)(2,1)S(1)} collective-permute-done((bf16[144,256]{1,0:T(8,128)(2,1)S(1)}, bf16[144,256]{1,0:T(8,128)(2,1)S(1)}, u32[]{:S(2)}, u32[]{:S(2)}) %collective-permute-start) | collective-permute-done | bytes 73760 | tf_op jit(solution)/shard_map/ppermute | solution.py:1171
  19.2 1.6 pad_maximum_fusion
  20.8 0.0 all-gather.2.cloned.1.call-update
  20.8 0.0 reduce-scatter.3.cloned.1.call-start
  20.9 23.5 %gather_in.1 = (bf16[4,160,1024]{2,1,0:T(8,128)(2,1)}, bf16[32,32,512]{2,1,0:T(8,128)(2,1)}, s32[4,8,128]{2,1,0:T(8,128)}) custom-call(bf16[160,1024]{1,0:T(8,128)(2,1)} %bitcast.29, f32[1,1024]{1,0:T(1,128)} %bitcast.40, bf16[32,1024]{1,0:T(8,128)(2,1)} %w_q.1, bf16[32,512]{1,0:T(8,128)(2,1)} %w_k.1, bf16[32,512]{1,0:T(8,128)(2,1)} %w_v.1, s32[1,16]{1,0:T(1,128)} %pairs.1), custom_call_target="tpu_custom_call" | custom-call | tf_op jit(solution)/shard_map/gather_in/pallas_call | solution.py:382
  44.4 0.0 copy-done.4
  44.4 0.0 copy-done.3
  44.4 0.6 maximum_bitcast_fusion
  45.0 7.2 %project.1 = (bf16[16,240,128]{2,1,0:T(8,128)(2,1)}, f32[640,384]{1,0:T(8,128)}, f32[640,128]{1,0:T(8,128)}, f32[640,128]{1,0:T(8,128)}) custom-call(s32[32,128]{1,0:T(8,128)} %bitcast.37, bf16[640,1024]{1,0:T(8,128)(2,1)} %bitcast.25, bf16[1024,512]{1,0:T(8,128)(2,1)} %bitcast.27, f32[2560,128]{1,0:T(8,128)} %constant.20.clone.cos_t, ...), custom_call_target="tpu_custom_call" | custom-call | tf_op jit(solution)/shard_map/project/pallas_call | solution.py:432
  52.2 25.9 %to_heads.1 = (bf16[16,240,128]{2,1,0:T(8,128)(2,1)}, bf16[4,160,1024]{2,1,0:T(8,128)(2,1)}) custom-call(bf16[16,240,128]{2,1,0:T(8,128)(2,1)} %get-tuple-element.62.refs_0_, bf16[160,1024]{1,0:T(8,128)(2,1)} %bitcast.33), custom_call_target="tpu_custom_call" | custom-call | tf_op jit(solution)/shard_map/to_heads/pallas_call | solution.py:190
  78.1 10.7 %attend.1 = (bf16[16,80,128]{2,1,0:T(8,128)(2,1)}, bf16[2560,128]{1,0:T(8,128)(2,1)}, bf16[2560,128]{1,0:T(8,128)(2,1)}, bf16[2560,128]{1,0:T(8,128)(2,1)}, f32[64,2560]{1,0:T(8,128)}, /*index=5*/f32[8,2560]{1,0:T(8,128)}) custom-call(s32[32,128]{1,0:T(8,128)} %bitcast.38, bf16[16,240,128]{2,1,0:T(8,128)(2,1)} %get-tuple-element.63.recv), custom_call_target="tpu_custom_call" | custom-call | tf_op jit(solution)/shard_map/attend/pallas_call | solution.py:495
  88.8 14.3 %to_tokens.1.parts = bf16[16,80,128]{2,1,0:T(8,128)(2,1)} custom-call(bf16[16,80,128]{2,1,0:T(8,128)(2,1)} %get-tuple-element.64.refs_0_), custom_call_target="tpu_custom_call" | custom-call | tf_op jit(solution)/shard_map/to_tokens/pallas_call | solution.py:190
  103.2 0.0 all-gather.2.cloned.1.call-done.wide
  103.2 39.8 %middle_part.1 = (f32[160,1024]{1,0:T(8,128)}, bf16[4,160,1024]{2,1,0:T(8,128)(2,1)}, bf16[512,3456]{1,0:T(8,128)(2,1)}, f32[160,1024]{1,0:T(8,128)}, bf16[160,1...) custom-call(bf16[16,80,128]{2,1,0:T(8,128)(2,1)} %to_tokens.1.parts, ...), custom_call_target="tpu_custom_call" | custom-call | tf_op jit(solution)/shard_map/middle_part/pallas_call | solution.py:802
  143.0 0.0 reduce-scatter.3.cloned.1.call-update
  143.0 0.0 reduce-scatter.5.cloned.1.call-start
  143.1 47.4 %reduce-scatter.3.cloned.1.call-done = bf16[128,3456]{1,0:T(8,128)(2,1)} async-done(((bf16[512,3456]{1,0:T(8,128)(2,1)}), bf16[128,3456]{1,0:T(8,128)(2,1)}) %reduce-scatter.3.cloned.1.call-update) | async-done | bytes 884752 | tf_op jit(solution)/shard_map/reduce_scatter | solution.py:1190
  190.5 0.0 reduce-scatter.5.cloned.1.call-update
  190.5 13.2 %to_heads_back.1.recv = bf16[16,80,128]{2,1,0:T(8,128)(2,1)} custom-call(bf16[16,80,128]{2,1,0:T(8,128)(2,1)} %get-tuple-element.66.refs_0_), custom_call_target="tpu_custom_call" | custom-call | tf_op jit(solution)/shard_map/to_heads_back/pallas_call | solution.py:190
  203.8 18.1 %attend_back.1.refs_0_ = bf16[16,240,128]{2,1,0:T(8,128)(2,1)} custom-call(s32[32,128]{1,0:T(8,128)} %bitcast.39, bf16[16,80,128]{2,1,0:T(8,128)(2,1)} %to_heads_back.1.recv, bf16[2560,128]{1,0:T(8,128)(2,1)} %get-tuple-element.67.q_s, bf16[2560,128]{1,0:T(8,128)(2,1)} %get-tuple-element.68.k_s, bf16[2560,128]{1,0:T(8,128)(2,1)} %get-tuple-element.69.v_s, ...), custom_call_target="tpu_custom_call" | custom-call | tf_op jit(solution)/shard_map/attend_back/pallas_call | solution.py:566
  221.9 22.1 %to_tokens_back.1 = (bf16[16,240,128]{2,1,0:T(8,128)(2,1)}, bf16[4,160,1024]{2,1,0:T(8,128)(2,1)}, bf16[4,160,256]{2,1,0:T(8,128)(2,1)}) custom-call(bf16[16,240,128]{2,1,0:T(8,128)(2,1)} %attend_back.1.refs_0_, bf16[160,1024]{1,0:T(8,128)(2,1)} %get-tuple-element.72.refs_1_, bf16[4,160,256]{2,1,0:T(8,128)(2,1)} %get-tuple-element.73.refs_2_), custom_call_target="tpu_custom_call" | custom-call | tf_op jit(solution)/shard_map/to_tokens_back/pallas_call | solution.py:190
  244.0 40.0 %project_back.1 = (bf16[160,1024]{1,0:T(8,128)(2,1)}, bf16[160,1024]{1,0:T(8,128)(2,1)}, bf16[32,512]{1,0:T(8,128)(2,1)}, bf16[32,256]{1,0:T(8,128)(2,1)}, f32[24,128]{1,0:T(8,128)}) custom-call(bf16[16,240,128]{2,1,0:T(8,128)(2,1)} %get-tuple-element.74.recv, f32[640,384]{1,0:T(8,128)} %get-tuple-element.75.raw, bf16[640,1024]{1,0:T(8,128)(2,1)} %bitcast.26, ...), custom_call_target="tpu_custom_call" | custom-call | tf_op jit(solution)/shard_map/project_back/pallas_call | solution.py:1065
  284.0 0.0 copy-start.2
  284.1 0.0 copy-start.1
  284.1 0.0 reduce-scatter.5.cloned.1.call-done.refs_1_.refs_3_
  284.1 20.7 %gather_out.1 = (bf16[4,32,512]{2,1,0:T(8,128)(2,1)}, bf16[4,32,2304]{2,1,0:T(8,128)(2,1)}, bf16[4,32,256]{2,1,0:T(8,128)(2,1)}, bf16[4,32,1152]{2,1,0:T(8,128)(2,1)}, f32[4,24,128]{2,1,0:T(8,128)}) custom-call(bf16[32,512]{1,0:T(8,128)(2,1)} %get-tuple-element.86.refs_0_, bf16[32,3456]{1,0:T(8,128)(2,1)} %reduce-scatter.5.cloned.1.call-done.refs_1_.refs_3_, ...), custom_call_target="tpu_custom_call" | custom-call | tf_op jit(solution)/shard_map/gather_out/pallas_call | solution.py:190
  304.8 2.6 hand_out.1
  307.4 1.3 slice_bitcast_fusion
  308.7 0.0 copy-done.2
  308.7 0.7 copy.36
  309.4 0.0 copy-done.1
  309.4 0.7 copy.37
  (4 shorter events, 0.1 us)
Async XLA Ops:
  7.2 1.0 copy-start
  7.2 37.2 %copy-start.4 = (f32[64]{0:T(128)S(1)}, f32[64]{0:T(128)}, u32[]{:S(2)}) copy-start(f32[64]{0:T(128)} %param.27) | copy-start | bytes 772
  7.2 37.2 %copy-start.3 = (f32[64]{0:T(128)S(1)}, f32[64]{0:T(128)}, u32[]{:S(2)}) copy-start(f32[64]{0:T(128)} %param.26) | copy-start | bytes 772
  7.2 96.0 %all-gather.2.cloned.1.call-start = ((), (), s32[]{:S(2)}) async-start(), calls=%async_computation.2 | async-start | bytes 9461760 | tf_op jit(solution)/shard_map/all_gather | solution.py:1177
  8.2 11.0 %collective-permute-start = (bf16[144,256]{1,0:T(8,128)(2,1)S(1)}, bf16[144,256]{1,0:T(8,128)(2,1)S(1)}, u32[]{:S(2)}, u32[]{:S(2)}) collective-permute-start(bf16[144,256]{1,0:T(8,128)(2,1)S(1)} %constant_dynamic-slice_fusion), channel_id=1, source_target_pairs={{0,0},{8,32},{16,64},{24,96},{32,8},{40,40},{48,72},{56,104},{64,1... | collective-permute-start | bytes 221192 | tf_op jit(solution)/shard_map/ppermute | solution.py:1171
  20.8 169.7 %reduce-scatter.3.cloned.1.call-start = ((), (), s32[]{:S(2)}) async-start(), calls=%async_computation.3 | async-start | bytes 4423680 | tf_op jit(solution)/shard_map/reduce_scatter | solution.py:1190
  143.0 141.1 %reduce-scatter.5.cloned.1.call-start = ((), (), s32[]{:S(2)}) async-start(), calls=%async_computation.4 | async-start | bytes 1105920 | tf_op jit(solution)/shard_map/reduce_scatter | solution.py:1191
  284.0 24.6 %copy-start.2 = (bf16[160,1024]{1,0:T(8,128)(2,1)S(1)}, bf16[160,1024]{1,0:T(8,128)(2,1)}, u32[]{:S(2)}) copy-start(bf16[160,1024]{1,0:T(8,128)(2,1)} %get-tuple-element.84) | copy-start | bytes 983044
  284.1 25.4 %copy-start.1 = (bf16[160,1024]{1,0:T(8,128)(2,1)S(1)}, bf16[160,1024]{1,0:T(8,128)(2,1)}, u32[]{:S(2)}) copy-start(bf16[160,1024]{1,0:T(8,128)(2,1)} %get-tuple-element.85) | copy-start | bytes 983044
Sparse Core Ops, SparseCore 0:
  20.9 65.4 all-gather.1
  143.2 47.3 reduce-scatter.2
  192.9 22.8 reduce-scatter.4

commit v7 on v6

--- a/solution.py
+++ b/solution.py
@@ -1188,7 +1188,6 @@
         4, mixed_parts, tokens[0], cot_all, g_ffn[None], wide
     )
     sums = lax.psum_scatter(grad_w_ffn, "ctx_1", scatter_dimension=0, tiled=True)
-    sums = lax.psum_scatter(sums, "ctx_0", scatter_dimension=0, tiled=True)
     (recv_g,) = exchange(6, "to_heads_back", ("r", "a2a", back_parts))
     sends_back = attend_back(pair, recv_g, q_s, k_s, v_s, o_t, inv)
     recv_back, branch_x, mixed_x = exchange(
@@ -1198,6 +1197,8 @@
         ("x", "ag", grad_branch),
         ("x", "a2a", mixed),
     )
+    sums, recv_back = lax.optimization_barrier((sums, recv_back))
+    sums = lax.psum_scatter(sums, "ctx_0", scatter_dimension=0, tiled=True)
     output, grad_tokens, sum_qkv, sum_o, gains = project_back(
         8,
         recv_back,

time: 318 us -> 273 us (0.86)
  waiting for transfers between devices: 51.8 us -> 4.39 us
  Pallas kernels: 238 us -> 242 us
    reduce_scatter x1, waiting for transfers between devices: 47.4 us -> 0.02 us  [body(): lax.psum_scatter(grad_w_ffn, 'ctx_1', scatter_dimension=0, tiled=True)]
    pallas_call x5, Pallas kernels: 96.2 us -> 99.8 us  [exchange(): pl.pallas_call(functools.partial(exchange_kernel, items), out_shape=outs,...]
  transfers between devices with their start and end apart: 4 -> 4, of which waited for: 2 -> 1; matrix products, arithmetic and copies ran while one was open for 0% -> 1% of each run, Pallas kernels for 55% -> 66%
where the time goes in v7:
time: 273 us
  Pallas kernels  242 us (89%)
  between operations  13.9 us (5%)
  starting transfers between devices  5.85 us (2%)
  local copies, waits for them, and re-layouts  4.67 us (2%)
  waiting for transfers between devices  4.39 us (2%)
    pallas_call x5, Pallas kernels, exchange(): pl.pallas_call(functools.partial(exchange_kernel, items), out_shape=outs,...  99.8 us
    pallas_call x1, Pallas kernels, middle_part(): pl.pallas_call(middle_kernel, in_specs=[vmem] * 4 + [pl.BlockSpec(memory_...  39.8 us
    pallas_call x1, Pallas kernels, project_back(): pl.pallas_call(project_back_kernel, in_specs=[vmem] * 16, out_specs=[vmem...  39.7 us
    pallas_call x1, Pallas kernels, gather_in(): pl.pallas_call(gather_in_kernel, in_specs=[pl.BlockSpec(memory_space=pltp...  23.5 us
    pallas_call x1, Pallas kernels, attend_back(): pl.pallas_call(attend_back_kernel, grid_spec=pltpu.PrefetchScalarGridSpec...  18.1 us
    pallas_call x1, Pallas kernels, attend(): pl.pallas_call(attend_kernel, grid_spec=pltpu.PrefetchScalarGridSpec(num_...  10.8 us
    pallas_call x1, Pallas kernels, project(): pl.pallas_call(project_kernel, grid_spec=pltpu.PrefetchScalarGridSpec(num...  7.18 us
    ppermute x1, starting transfers between devices, body(): lax.ppermute(columns_of(w_down, x, D // 4), ('seq', 'ctx_0'), swap_xz)  5.73 us
  transfers between devices with their start and end apart: 4, of which 1 were waited for; matrix products, arithmetic and copies ran while one was open for 1% of the time, Pallas kernels for 66%

profile of v7, /device:TPU:4, one launch (start us, length us, event | category | flops | bytes accessed | tf_op | source)
XLA Modules:
  0.0 272.5 jit_solution(10819246856073299985)
XLA Ops:
  7.2 0.0 copy-start
  7.2 0.0 copy-start.4
  7.2 0.0 copy-start.3
  7.2 0.0 all-gather.2.cloned.1.call-start
  7.3 0.9 copy-done
  8.2 5.7 %collective-permute-start = (bf16[144,256]{1,0:T(8,128)(2,1)S(1)}, bf16[144,256]{1,0:T(8,128)(2,1)S(1)}, u32[]{:S(2)}, u32[]{:S(2)}) collective-permute-start(bf16[144,256]{1,0:T(8,128)(2,1)S(1)} %constant_dynamic-slice_fusion), channel_id=1, source_target_pairs={{0,0},{8,32},{16,64},{24,96},{32,8},{40,40},{48,72},{56,104},{64,1... | collective-permute-start | bytes 221192 | tf_op jit(solution)/shard_map/ppermute | solution.py:1171
  13.9 0.9 constant_dynamic-slice_fusion.1
  14.8 4.3 %collective-permute-done = bf16[144,256]{1,0:T(8,128)(2,1)S(1)} collective-permute-done((bf16[144,256]{1,0:T(8,128)(2,1)S(1)}, bf16[144,256]{1,0:T(8,128)(2,1)S(1)}, u32[]{:S(2)}, u32[]{:S(2)}) %collective-permute-start) | collective-permute-done | bytes 73760 | tf_op jit(solution)/shard_map/ppermute | solution.py:1171
  19.2 1.6 pad_maximum_fusion
  20.8 0.0 all-gather.2.cloned.1.call-update
  20.8 0.0 reduce-scatter.3.cloned.1.call-start
  20.9 23.5 %gather_in.1 = (bf16[4,160,1024]{2,1,0:T(8,128)(2,1)}, bf16[32,32,512]{2,1,0:T(8,128)(2,1)}, s32[4,8,128]{2,1,0:T(8,128)}) custom-call(bf16[160,1024]{1,0:T(8,128)(2,1)} %bitcast.29, f32[1,1024]{1,0:T(1,128)} %bitcast.40, bf16[32,1024]{1,0:T(8,128)(2,1)} %w_q.1, bf16[32,512]{1,0:T(8,128)(2,1)} %w_k.1, bf16[32,512]{1,0:T(8,128)(2,1)} %w_v.1, s32[1,16]{1,0:T(1,128)} %pairs.1), custom_call_target="tpu_custom_call" | custom-call | tf_op jit(solution)/shard_map/gather_in/pallas_call | solution.py:382
  44.4 0.0 copy-done.4
  44.4 0.0 copy-done.3
  44.4 0.6 maximum_bitcast_fusion
  45.0 7.2 %project.1 = (bf16[16,240,128]{2,1,0:T(8,128)(2,1)}, f32[640,384]{1,0:T(8,128)}, f32[640,128]{1,0:T(8,128)}, f32[640,128]{1,0:T(8,128)}) custom-call(s32[32,128]{1,0:T(8,128)} %bitcast.37, bf16[640,1024]{1,0:T(8,128)(2,1)} %bitcast.25, bf16[1024,512]{1,0:T(8,128)(2,1)} %bitcast.27, f32[2560,128]{1,0:T(8,128)} %constant.20.clone.cos_t, ...), custom_call_target="tpu_custom_call" | custom-call | tf_op jit(solution)/shard_map/project/pallas_call | solution.py:432
  52.2 25.9 %to_heads.1 = (bf16[16,240,128]{2,1,0:T(8,128)(2,1)}, bf16[4,160,1024]{2,1,0:T(8,128)(2,1)}) custom-call(bf16[16,240,128]{2,1,0:T(8,128)(2,1)} %get-tuple-element.64.refs_0_, bf16[160,1024]{1,0:T(8,128)(2,1)} %bitcast.33), custom_call_target="tpu_custom_call" | custom-call | tf_op jit(solution)/shard_map/to_heads/pallas_call | solution.py:190
  78.1 10.8 %attend.1 = (bf16[16,80,128]{2,1,0:T(8,128)(2,1)}, bf16[2560,128]{1,0:T(8,128)(2,1)}, bf16[2560,128]{1,0:T(8,128)(2,1)}, bf16[2560,128]{1,0:T(8,128)(2,1)}, f32[64,2560]{1,0:T(8,128)}, /*index=5*/f32[8,2560]{1,0:T(8,128)}) custom-call(s32[32,128]{1,0:T(8,128)} %bitcast.38, bf16[16,240,128]{2,1,0:T(8,128)(2,1)} %get-tuple-element.65.recv), custom_call_target="tpu_custom_call" | custom-call | tf_op jit(solution)/shard_map/attend/pallas_call | solution.py:495
  88.8 14.3 %to_tokens.1.parts = bf16[16,80,128]{2,1,0:T(8,128)(2,1)} custom-call(bf16[16,80,128]{2,1,0:T(8,128)(2,1)} %get-tuple-element.66.refs_0_), custom_call_target="tpu_custom_call" | custom-call | tf_op jit(solution)/shard_map/to_tokens/pallas_call | solution.py:190
  103.2 0.0 all-gather.2.cloned.1.call-done.wide
  103.2 39.8 %middle_part.1 = (f32[160,1024]{1,0:T(8,128)}, bf16[4,160,1024]{2,1,0:T(8,128)(2,1)}, bf16[512,3456]{1,0:T(8,128)(2,1)}, f32[160,1024]{1,0:T(8,128)}, bf16[160,1...) custom-call(bf16[16,80,128]{2,1,0:T(8,128)(2,1)} %to_tokens.1.parts, ...), custom_call_target="tpu_custom_call" | custom-call | tf_op jit(solution)/shard_map/middle_part/pallas_call | solution.py:802
  143.0 0.0 reduce-scatter.3.cloned.1.call-update
  143.0 0.0 reduce-scatter.5.cloned.1.call-start
  143.1 16.4 %to_heads_back.1.recv = bf16[16,80,128]{2,1,0:T(8,128)(2,1)} custom-call(bf16[16,80,128]{2,1,0:T(8,128)(2,1)} %get-tuple-element.69.refs_0_), custom_call_target="tpu_custom_call" | custom-call | tf_op jit(solution)/shard_map/to_heads_back/pallas_call | solution.py:190
  159.5 18.1 %attend_back.1.refs_0_ = bf16[16,240,128]{2,1,0:T(8,128)(2,1)} custom-call(s32[32,128]{1,0:T(8,128)} %bitcast.39, bf16[16,80,128]{2,1,0:T(8,128)(2,1)} %to_heads_back.1.recv, bf16[2560,128]{1,0:T(8,128)(2,1)} %get-tuple-element.70.q_s, bf16[2560,128]{1,0:T(8,128)(2,1)} %get-tuple-element.71.k_s, bf16[2560,128]{1,0:T(8,128)(2,1)} %get-tuple-element.72.v_s, ...), custom_call_target="tpu_custom_call" | custom-call | tf_op jit(solution)/shard_map/attend_back/pallas_call | solution.py:566
  177.6 23.1 %to_tokens_back.1 = (bf16[16,240,128]{2,1,0:T(8,128)(2,1)}, bf16[4,160,1024]{2,1,0:T(8,128)(2,1)}, bf16[4,160,256]{2,1,0:T(8,128)(2,1)}) custom-call(bf16[16,240,128]{2,1,0:T(8,128)(2,1)} %attend_back.1.refs_0_, bf16[160,1024]{1,0:T(8,128)(2,1)} %get-tuple-element.75.refs_1_, bf16[4,160,256]{2,1,0:T(8,128)(2,1)} %get-tuple-element.76.refs_2_), custom_call_target="tpu_custom_call" | custom-call | tf_op jit(solution)/shard_map/to_tokens_back/pallas_call | solution.py:190
  200.7 0.0 reduce-scatter.3.cloned.1.call-done
  200.8 0.0 reduce-scatter.5.cloned.1.call-update
  200.8 39.7 %project_back.1 = (bf16[160,1024]{1,0:T(8,128)(2,1)}, bf16[160,1024]{1,0:T(8,128)(2,1)}, bf16[32,512]{1,0:T(8,128)(2,1)}, bf16[32,256]{1,0:T(8,128)(2,1)}, f32[24,128]{1,0:T(8,128)}) custom-call(bf16[16,240,128]{2,1,0:T(8,128)(2,1)} %get-tuple-element.78.recv, f32[640,384]{1,0:T(8,128)} %get-tuple-element.79.raw, bf16[640,1024]{1,0:T(8,128)(2,1)} %bitcast.26, ...), custom_call_target="tpu_custom_call" | custom-call | tf_op jit(solution)/shard_map/project_back/pallas_call | solution.py:1065
  240.5 0.0 copy-start.2
  240.5 0.0 copy-start.1
  240.5 0.0 reduce-scatter.5.cloned.1.call-done.refs_1_.refs_3_
  240.5 20.1 %gather_out.1 = (bf16[4,32,512]{2,1,0:T(8,128)(2,1)}, bf16[4,32,2304]{2,1,0:T(8,128)(2,1)}, bf16[4,32,256]{2,1,0:T(8,128)(2,1)}, bf16[4,32,1152]{2,1,0:T(8,128)(2,1)}, f32[4,24,128]{2,1,0:T(8,128)}) custom-call(bf16[32,512]{1,0:T(8,128)(2,1)} %get-tuple-element.90.refs_0_, bf16[32,3456]{1,0:T(8,128)(2,1)} %reduce-scatter.5.cloned.1.call-done.refs_1_.refs_3_, ...), custom_call_target="tpu_custom_call" | custom-call | tf_op jit(solution)/shard_map/gather_out/pallas_call | solution.py:190
  260.6 2.6 hand_out.1
  263.3 1.3 slice_bitcast_fusion
  264.6 0.0 copy-done.2
  264.6 0.7 copy.36
  265.3 0.0 copy-done.1
  265.3 0.7 copy.37
  (4 shorter events, 0.1 us)
Async XLA Ops:
  7.2 1.0 copy-start
  7.2 37.2 %copy-start.4 = (f32[64]{0:T(128)S(1)}, f32[64]{0:T(128)}, u32[]{:S(2)}) copy-start(f32[64]{0:T(128)} %param.27) | copy-start | bytes 772
  7.2 37.2 %copy-start.3 = (f32[64]{0:T(128)S(1)}, f32[64]{0:T(128)}, u32[]{:S(2)}) copy-start(f32[64]{0:T(128)} %param.26) | copy-start | bytes 772
  7.2 96.0 %all-gather.2.cloned.1.call-start = ((), (), s32[]{:S(2)}) async-start(), calls=%async_computation.2 | async-start | bytes 9461760 | tf_op jit(solution)/shard_map/all_gather | solution.py:1177
  8.2 11.0 %collective-permute-start = (bf16[144,256]{1,0:T(8,128)(2,1)S(1)}, bf16[144,256]{1,0:T(8,128)(2,1)S(1)}, u32[]{:S(2)}, u32[]{:S(2)}) collective-permute-start(bf16[144,256]{1,0:T(8,128)(2,1)S(1)} %constant_dynamic-slice_fusion), channel_id=1, source_target_pairs={{0,0},{8,32},{16,64},{24,96},{32,8},{40,40},{48,72},{56,104},{64,1... | collective-permute-start | bytes 221192 | tf_op jit(solution)/shard_map/ppermute | solution.py:1171
  20.8 179.9 %reduce-scatter.3.cloned.1.call-start = ((), (), s32[]{:S(2)}) async-start(), calls=%async_computation.3 | async-start | bytes 4423680 | tf_op jit(solution)/shard_map/reduce_scatter | solution.py:1190
  143.0 97.5 %reduce-scatter.5.cloned.1.call-start = ((), (), s32[]{:S(2)}) async-start(), calls=%async_computation.4 | async-start | bytes 1105920 | tf_op jit(solution)/shard_map/reduce_scatter | solution.py:1201
  240.5 24.1 %copy-start.2 = (bf16[160,1024]{1,0:T(8,128)(2,1)S(1)}, bf16[160,1024]{1,0:T(8,128)(2,1)}, u32[]{:S(2)}) copy-start(bf16[160,1024]{1,0:T(8,128)(2,1)} %get-tuple-element.88) | copy-start | bytes 983044
  240.5 24.8 %copy-start.1 = (bf16[160,1024]{1,0:T(8,128)(2,1)S(1)}, bf16[160,1024]{1,0:T(8,128)(2,1)}, u32[]{:S(2)}) copy-start(bf16[160,1024]{1,0:T(8,128)(2,1)} %get-tuple-element.89) | copy-start | bytes 983044
Sparse Core Ops, SparseCore 0:
  20.9 65.4 all-gather.1
  143.2 57.1 reduce-scatter.2
  202.8 30.9 reduce-scatter.4

commit v8 on v6

--- a/solution.py
+++ b/solution.py
@@ -737,14 +737,14 @@
             for rg in range(9):
                 for l in range(2):
                     row = o * 144 + rg * 16
-                    there = ((o % 2) * 16 + (o // 2) * 4 + q) * 32 + l * 16
+                    there = ((o % 2) * 16 + q * 4 + o // 2) * 32 + l * 16
                     dw[there : there + 16, 2 * FX + rg * 128 : 2 * FX + rg * 128 + 128] = grad[
                         row : row + 16, l * 128 : l * 128 + 128
                     ]
     to_sibling(9, down).start()
     h_rows = h_all[...].reshape(NX * ROWS, D).T
     for o in range(32):
-        there = ((o % 2) * 16 + (o // 2 % 4) * 4 + o // 8) * 32
+        there = ((o % 2) * 16 + o // 2) * 32
         h_t[there : there + 32, :] = h_rows[o * 32 : o * 32 + 32, :]
 
     def chunk(j):
@@ -878,6 +878,10 @@
     gains,
     sibling_gains,
     gains_all,
+    dwo,
+    sibling_dwo,
+    reduced_o,
+    dwo_parts,
     ss_r,
     rs_r,
     ss_h,
@@ -888,6 +892,8 @@
     rs_w,
     ss_g,
     rs_g,
+    ss_o,
+    rs_o,
 ):
     x, z, y, c = coords()
     ctx = z * 4 + y
@@ -918,7 +924,11 @@
         )
 
     def to_sibling(i):
-        src, dst = ((dw.at[1 - c], sibling_dw), (gains, sibling_gains))[i]
+        src, dst = (
+            (dw.at[1 - c], sibling_dw),
+            (gains, sibling_gains),
+            (dwo.at[1 - c], sibling_dwo),
+        )[i]
         return pltpu.make_async_remote_copy(
             src_ref=src,
             dst_ref=dst,
@@ -932,6 +942,7 @@
         src, dst, ss, rs = (
             (reduced.at[t], dw_parts, ss_w, rs_w),
             (gains, gains_all, ss_g, rs_g),
+            (reduced_o.at[t], dwo_parts, ss_o, rs_o),
         )[i]
         return pltpu.make_async_remote_copy(
             src_ref=src,
@@ -942,6 +953,17 @@
             device_id_type=MESH,
         )
 
+    for k in (1, 3, 2):
+        along_x(result, result_parts, ss_r, rs_r, lax.rem(x + k, NX), x).start()
+    grad_w = tn(
+        mixed_x[...].reshape(NX * ROWS, QX), branch_x[...].reshape(NX * ROWS, D)
+    ).astype(BF16)
+    for q in range(4):
+        for i in range(8):
+            dwo[i % 2, q * 4 + i // 2, :, :] = grad_w[
+                i * 32 : (i + 1) * 32, q * 256 : (q + 1) * 256
+            ]
+    to_sibling(2).start()
     m = low_half((ROWS, 2 * HD))
     mh = low_half((BLK, 2 * HD))
     gq_sum = jnp.zeros((1, 2 * HD), F32)
@@ -980,6 +1002,17 @@
             along_x(gh, gh_parts, ss_h, rs_h, s, x).start()
         term = jnp.sum(grad_h * h[at, :].astype(F32), axis=0, keepdims=True)
         attn[...] = term if n == 0 else attn[...] + term
+        if n == 0:
+            to_sibling(2).wait()
+
+            def send_o(k, carry):
+                t = lax.rem(ctx + k, 16)
+                both = dwo[c, t].astype(F32) + sibling_dwo[t].astype(F32)
+                reduced_o[t] = both.astype(BF16)
+                over_ctx(2, t, ctx).start()
+                return carry
+
+            lax.fori_loop(1, 16, send_o, 0)
     for i in range(8):
         cols = slice(i * 128, i * 128 + 128)
         gains[i : i + 1, :] = attn[:, cols] / g_attn[:, cols]
@@ -987,19 +1020,9 @@
     gains[16:, :] = jnp.concatenate([gq_sum, gk_sum, jnp.zeros((6, 2 * HD), F32)], 0)
     grad_w = tn(h[...], low[...]).astype(BF16)
     for i in range(32):
-        dw[i % 2, i // 2, :, : QX + 2 * KX] = grad_w[i * 32 : (i + 1) * 32, :]
-    grad_w = tn(
-        mixed_x[...].reshape(NX * ROWS, QX), branch_x[...].reshape(NX * ROWS, D)
-    ).astype(BF16)
-    for q in range(4):
-        for i in range(8):
-            dw[i % 2, q * 4 + i // 2, :, QX + 2 * KX :] = grad_w[
-                i * 32 : (i + 1) * 32, q * 256 : (q + 1) * 256
-            ]
+        dw[i % 2, i // 2, :, :] = grad_w[i * 32 : (i + 1) * 32, :]
     to_sibling(0).start()
     to_sibling(1).start()
-    for k in (1, 3, 2):
-        along_x(result, result_parts, ss_r, rs_r, lax.rem(x + k, NX), x).start()
     to_sibling(1).wait()
     gains[...] = gains[...] + sibling_gains[...]
     to_sibling(0).wait()
@@ -1013,6 +1036,7 @@
 
     lax.fori_loop(1, 16, send, 0)
     total = dw[c, ctx].astype(F32) + sibling_dw[ctx].astype(F32)
+    total_o = dwo[c, ctx].astype(F32) + sibling_dwo[ctx].astype(F32)
     all_gains = gains[...]
 
     grad_h = gh[x].astype(F32)
@@ -1038,17 +1062,23 @@
         t = lax.rem(ctx + k, 16)
         over_ctx(0, t, t).wait_recv()
         over_ctx(1, t, t).wait_recv()
-        return carry[0] + dw_parts[t].astype(F32), carry[1] + gains_all[t]
-
-    total, all_gains = lax.fori_loop(1, 16, collect, (total, all_gains))
-    qkv_o[...] = total[:, : QX + 2 * KX].astype(BF16)
-    wo_o[...] = total[:, QX + 2 * KX :].astype(BF16)
+        over_ctx(2, t, t).wait_recv()
+        return (
+            carry[0] + dw_parts[t].astype(F32),
+            carry[1] + gains_all[t],
+            carry[2] + dwo_parts[t].astype(F32),
+        )
+
+    total, all_gains, total_o = lax.fori_loop(1, 16, collect, (total, all_gains, total_o))
+    qkv_o[...] = total.astype(BF16)
+    wo_o[...] = total_o.astype(BF16)
     gains_o[...] = all_gains
 
     def drain(k, carry):
         t = lax.rem(ctx + k, 16)
         over_ctx(0, t, ctx).wait_send()
         over_ctx(1, t, ctx).wait_send()
+        over_ctx(2, t, ctx).wait_send()
         return carry
 
     lax.fori_loop(1, 16, drain, 0)
@@ -1061,7 +1091,7 @@
 def project_back(number, *operands):
     vmem = pl.BlockSpec(memory_space=pltpu.VMEM)
     tokens = (NX, ROWS, D)
-    wide = QX + 2 * KX + QX
+    wide = QX + 2 * KX
     return pl.pallas_call(
         project_back_kernel,
         in_specs=[vmem] * 16,
@@ -1086,8 +1116,12 @@
             pltpu.VMEM((24, 2 * HD), F32),
             pltpu.VMEM((24, 2 * HD), F32),
             pltpu.VMEM((16, 24, 2 * HD), F32),
+            pltpu.VMEM((2, 16, 32, QX), BF16),
+            pltpu.VMEM((16, 32, QX), BF16),
+            pltpu.VMEM((16, 32, QX), BF16),
+            pltpu.VMEM((16, 32, QX), BF16),
         ]
-        + [pltpu.SemaphoreType.DMA((n,)) for n in (NX, NX, NX, NX, 2, 2, 16, 16, 16, 16)],
+        + [pltpu.SemaphoreType.DMA((n,)) for n in (NX, NX, NX, NX, 3, 3) + (16,) * 6],
         compiler_params=pltpu.CompilerParams(
             collective_id=number, has_side_effects=True, vmem_limit_bytes=VMEM_BYTES
         ),
@@ -1187,8 +1221,7 @@
     middle, result4, grad_w_ffn, grad_middle, grad_branch, mixed, back_parts, gain_ffn = middle_part(
         4, mixed_parts, tokens[0], cot_all, g_ffn[None], wide
     )
-    sums = lax.psum_scatter(grad_w_ffn, "ctx_1", scatter_dimension=0, tiled=True)
-    sums = lax.psum_scatter(sums, "ctx_0", scatter_dimension=0, tiled=True)
+    sums = lax.psum_scatter(grad_w_ffn, CTX, scatter_dimension=0, tiled=True)
     (recv_g,) = exchange(6, "to_heads_back", ("r", "a2a", back_parts))
     sends_back = attend_back(pair, recv_g, q_s, k_s, v_s, o_t, inv)
     recv_back, branch_x, mixed_x = exchange(

time: 318 us -> 271 us (0.85)
  waiting for transfers between devices: 51.8 us -> 4.35 us
    reduce_scatter x2 -> x1, waiting for transfers between devices: 47.5 us -> 0.02 us  [body(): sums = lax.psum_scatter(grad_w_ffn, CTX, scatter_dimension=0, tiled=True)]
  transfers between devices with their start and end apart: 4 -> 3, of which waited for: 2 -> 1; matrix products, arithmetic and copies ran while one was open for 0% -> 1% of each run, Pallas kernels for 55% -> 66%
where the time goes in v8:
time: 271 us; the launch traced here: 270 us
  Pallas kernels  239 us (88%)
  between operations  14.2 us (5%)
  starting transfers between devices  5.81 us (2%)
  local copies, waits for them, and re-layouts  4.67 us (2%)
  waiting for transfers between devices  4.35 us (2%)
    pallas_call x5, Pallas kernels, exchange(): pl.pallas_call(functools.partial(exchange_kernel, items), out_shape=outs,...  97.8 us
    pallas_call x1, Pallas kernels, middle_part(): pl.pallas_call(middle_kernel, in_specs=[vmem] * 4 + [pl.BlockSpec(memory_...  39.8 us
    pallas_call x1, Pallas kernels, project_back(): pl.pallas_call(project_back_kernel, in_specs=[vmem] * 16, out_specs=[vmem...  39.1 us
    pallas_call x1, Pallas kernels, gather_in(): pl.pallas_call(gather_in_kernel, in_specs=[pl.BlockSpec(memory_space=pltp...  23.5 us
    pallas_call x1, Pallas kernels, attend_back(): pl.pallas_call(attend_back_kernel, grid_spec=pltpu.PrefetchScalarGridSpec...  18.1 us
    pallas_call x1, Pallas kernels, attend(): pl.pallas_call(attend_kernel, grid_spec=pltpu.PrefetchScalarGridSpec(num_...  10.8 us
    pallas_call x1, Pallas kernels, project(): pl.pallas_call(project_kernel, grid_spec=pltpu.PrefetchScalarGridSpec(num...  7.18 us
    ppermute x1, starting transfers between devices, body(): lax.ppermute(columns_of(w_down, x, D // 4), ('seq', 'ctx_0'), swap_xz)  5.73 us
  transfers between devices with their start and end apart: 3, of which 1 were waited for; matrix products, arithmetic and copies ran while one was open for 1% of the time, Pallas kernels for 66%

profile of v8, /device:TPU:4, one launch (start us, length us, event | category | flops | bytes accessed | tf_op | source)
XLA Modules:
  0.0 270.1 jit_solution(1410932571160318044)
XLA Ops:
  7.2 0.0 copy-start
  7.2 0.0 copy-start.4
  7.2 0.0 copy-start.3
  7.2 0.0 all-gather.2.cloned.1.call-start
  7.3 0.9 copy-done
  8.2 5.7 %collective-permute-start = (bf16[144,256]{1,0:T(8,128)(2,1)S(1)}, bf16[144,256]{1,0:T(8,128)(2,1)S(1)}, u32[]{:S(2)}, u32[]{:S(2)}) collective-permute-start(bf16[144,256]{1,0:T(8,128)(2,1)S(1)} %constant_dynamic-slice_fusion), channel_id=1, source_target_pairs={{0,0},{8,32},{16,64},{24,96},{32,8},{40,40},{48,72},{56,104},{64,1... | collective-permute-start | bytes 221192 | tf_op jit(solution)/shard_map/ppermute | solution.py:1205
  13.9 0.9 constant_dynamic-slice_fusion.1
  14.8 4.3 %collective-permute-done = bf16[144,256]{1,0:T(8,128)(2,1)S(1)} collective-permute-done((bf16[144,256]{1,0:T(8,128)(2,1)S(1)}, bf16[144,256]{1,0:T(8,128)(2,1)S(1)}, u32[]{:S(2)}, u32[]{:S(2)}) %collective-permute-start) | collective-permute-done | bytes 73760 | tf_op jit(solution)/shard_map/ppermute | solution.py:1205
  19.2 1.6 pad_maximum_fusion
  20.8 0.0 all-gather.2.cloned.1.call-update
  20.8 0.0 reduce-scatter.2.cloned.1.call-start
  20.9 23.5 %gather_in.1 = (bf16[4,160,1024]{2,1,0:T(8,128)(2,1)}, bf16[32,32,512]{2,1,0:T(8,128)(2,1)}, s32[4,8,128]{2,1,0:T(8,128)}) custom-call(bf16[160,1024]{1,0:T(8,128)(2,1)} %bitcast.29, f32[1,1024]{1,0:T(1,128)} %bitcast.40, bf16[32,1024]{1,0:T(8,128)(2,1)} %w_q.1, bf16[32,512]{1,0:T(8,128)(2,1)} %w_k.1, bf16[32,512]{1,0:T(8,128)(2,1)} %w_v.1, s32[1,16]{1,0:T(1,128)} %pairs.1), custom_call_target="tpu_custom_call" | custom-call | tf_op jit(solution)/shard_map/gather_in/pallas_call | solution.py:382
  44.4 0.0 copy-done.4
  44.4 0.0 copy-done.3
  44.4 0.6 maximum_bitcast_fusion
  45.0 7.2 %project.1 = (bf16[16,240,128]{2,1,0:T(8,128)(2,1)}, f32[640,384]{1,0:T(8,128)}, f32[640,128]{1,0:T(8,128)}, f32[640,128]{1,0:T(8,128)}) custom-call(s32[32,128]{1,0:T(8,128)} %bitcast.37, bf16[640,1024]{1,0:T(8,128)(2,1)} %bitcast.25, bf16[1024,512]{1,0:T(8,128)(2,1)} %bitcast.27, f32[2560,128]{1,0:T(8,128)} %constant.20.clone.cos_t, ...), custom_call_target="tpu_custom_call" | custom-call | tf_op jit(solution)/shard_map/project/pallas_call | solution.py:432
  52.2 25.9 %to_heads.1 = (bf16[16,240,128]{2,1,0:T(8,128)(2,1)}, bf16[4,160,1024]{2,1,0:T(8,128)(2,1)}) custom-call(bf16[16,240,128]{2,1,0:T(8,128)(2,1)} %get-tuple-element.62.refs_0_, bf16[160,1024]{1,0:T(8,128)(2,1)} %bitcast.33), custom_call_target="tpu_custom_call" | custom-call | tf_op jit(solution)/shard_map/to_heads/pallas_call | solution.py:190
  78.1 10.8 %attend.1 = (bf16[16,80,128]{2,1,0:T(8,128)(2,1)}, bf16[2560,128]{1,0:T(8,128)(2,1)}, bf16[2560,128]{1,0:T(8,128)(2,1)}, bf16[2560,128]{1,0:T(8,128)(2,1)}, f32[64,2560]{1,0:T(8,128)}, /*index=5*/f32[8,2560]{1,0:T(8,128)}) custom-call(s32[32,128]{1,0:T(8,128)} %bitcast.38, bf16[16,240,128]{2,1,0:T(8,128)(2,1)} %get-tuple-element.63.recv), custom_call_target="tpu_custom_call" | custom-call | tf_op jit(solution)/shard_map/attend/pallas_call | solution.py:495
  88.8 14.3 %to_tokens.1.parts = bf16[16,80,128]{2,1,0:T(8,128)(2,1)} custom-call(bf16[16,80,128]{2,1,0:T(8,128)(2,1)} %get-tuple-element.64.refs_0_), custom_call_target="tpu_custom_call" | custom-call | tf_op jit(solution)/shard_map/to_tokens/pallas_call | solution.py:190
  103.2 0.0 all-gather.2.cloned.1.call-done.wide
  103.2 39.8 %middle_part.1 = (f32[160,1024]{1,0:T(8,128)}, bf16[4,160,1024]{2,1,0:T(8,128)(2,1)}, bf16[512,3456]{1,0:T(8,128)(2,1)}, f32[160,1024]{1,0:T(8,128)}, bf16[160,1...) custom-call(bf16[16,80,128]{2,1,0:T(8,128)(2,1)} %to_tokens.1.parts, ...), custom_call_target="tpu_custom_call" | custom-call | tf_op jit(solution)/shard_map/middle_part/pallas_call | solution.py:802
  143.0 0.0 reduce-scatter.2.cloned.1.call-update
  143.0 16.4 %to_heads_back.1.recv = bf16[16,80,128]{2,1,0:T(8,128)(2,1)} custom-call(bf16[16,80,128]{2,1,0:T(8,128)(2,1)} %get-tuple-element.66.refs_0_), custom_call_target="tpu_custom_call" | custom-call | tf_op jit(solution)/shard_map/to_heads_back/pallas_call | solution.py:190
  159.4 18.1 %attend_back.1.refs_0_ = bf16[16,240,128]{2,1,0:T(8,128)(2,1)} custom-call(s32[32,128]{1,0:T(8,128)} %bitcast.39, bf16[16,80,128]{2,1,0:T(8,128)(2,1)} %to_heads_back.1.recv, bf16[2560,128]{1,0:T(8,128)(2,1)} %get-tuple-element.67.q_s, bf16[2560,128]{1,0:T(8,128)(2,1)} %get-tuple-element.68.k_s, bf16[2560,128]{1,0:T(8,128)(2,1)} %get-tuple-element.69.v_s, ...), custom_call_target="tpu_custom_call" | custom-call | tf_op jit(solution)/shard_map/attend_back/pallas_call | solution.py:566
  177.5 21.9 %to_tokens_back.1 = (bf16[16,240,128]{2,1,0:T(8,128)(2,1)}, bf16[4,160,1024]{2,1,0:T(8,128)(2,1)}, bf16[4,160,256]{2,1,0:T(8,128)(2,1)}) custom-call(bf16[16,240,128]{2,1,0:T(8,128)(2,1)} %attend_back.1.refs_0_, bf16[160,1024]{1,0:T(8,128)(2,1)} %get-tuple-element.72.refs_1_, bf16[4,160,256]{2,1,0:T(8,128)(2,1)} %get-tuple-element.73.refs_2_), custom_call_target="tpu_custom_call" | custom-call | tf_op jit(solution)/shard_map/to_tokens_back/pallas_call | solution.py:190
  199.5 39.1 %project_back.1 = (bf16[160,1024]{1,0:T(8,128)(2,1)}, bf16[160,1024]{1,0:T(8,128)(2,1)}, bf16[32,512]{1,0:T(8,128)(2,1)}, bf16[32,256]{1,0:T(8,128)(2,1)}, f32[24,128]{1,0:T(8,128)}) custom-call(bf16[16,240,128]{2,1,0:T(8,128)(2,1)} %get-tuple-element.74.recv, f32[640,384]{1,0:T(8,128)} %get-tuple-element.75.raw, bf16[640,1024]{1,0:T(8,128)(2,1)} %bitcast.26, ...), custom_call_target="tpu_custom_call" | custom-call | tf_op jit(solution)/shard_map/project_back/pallas_call | solution.py:1095
  238.6 0.0 copy-start.2
  238.6 0.0 copy-start.1
  238.6 0.0 reduce-scatter.2.cloned.1.call-done.refs_1_.refs_3_
  238.6 19.3 %gather_out.1 = (bf16[4,32,512]{2,1,0:T(8,128)(2,1)}, bf16[4,32,2304]{2,1,0:T(8,128)(2,1)}, bf16[4,32,256]{2,1,0:T(8,128)(2,1)}, bf16[4,32,1152]{2,1,0:T(8,128)(2,1)}, f32[4,24,128]{2,1,0:T(8,128)}) custom-call(bf16[32,512]{1,0:T(8,128)(2,1)} %get-tuple-element.86.refs_0_, bf16[32,3456]{1,0:T(8,128)(2,1)} %reduce-scatter.2.cloned.1.call-done.refs_1_.refs_3_, ...), custom_call_target="tpu_custom_call" | custom-call | tf_op jit(solution)/shard_map/gather_out/pallas_call | solution.py:190
  257.9 2.6 hand_out.1
  260.6 1.3 slice_bitcast_fusion
  261.9 0.0 copy-done.2
  261.9 0.7 copy.36
  262.6 0.0 copy-done.1
  262.6 0.7 copy.37
  (4 shorter events, 0.1 us)
Async XLA Ops:
  7.2 1.0 copy-start
  7.2 37.2 %copy-start.4 = (f32[64]{0:T(128)S(1)}, f32[64]{0:T(128)}, u32[]{:S(2)}) copy-start(f32[64]{0:T(128)} %param.27) | copy-start | bytes 772
  7.2 37.2 %copy-start.3 = (f32[64]{0:T(128)S(1)}, f32[64]{0:T(128)}, u32[]{:S(2)}) copy-start(f32[64]{0:T(128)} %param.26) | copy-start | bytes 772
  7.2 96.0 %all-gather.2.cloned.1.call-start = ((), (), s32[]{:S(2)}) async-start(), calls=%async_computation.1 | async-start | bytes 9461760 | tf_op jit(solution)/shard_map/all_gather | solution.py:1211
  8.2 11.0 %collective-permute-start = (bf16[144,256]{1,0:T(8,128)(2,1)S(1)}, bf16[144,256]{1,0:T(8,128)(2,1)S(1)}, u32[]{:S(2)}, u32[]{:S(2)}) collective-permute-start(bf16[144,256]{1,0:T(8,128)(2,1)S(1)} %constant_dynamic-slice_fusion), channel_id=1, source_target_pairs={{0,0},{8,32},{16,64},{24,96},{32,8},{40,40},{48,72},{56,104},{64,1... | collective-permute-start | bytes 221192 | tf_op jit(solution)/shard_map/ppermute | solution.py:1205
  20.8 217.8 %reduce-scatter.2.cloned.1.call-start = ((), (), s32[]{:S(2)}) async-start(), calls=%async_computation.2 | async-start | bytes 3760128 | tf_op jit(solution)/shard_map/reduce_scatter | solution.py:1224
  238.6 23.3 %copy-start.2 = (bf16[160,1024]{1,0:T(8,128)(2,1)S(1)}, bf16[160,1024]{1,0:T(8,128)(2,1)}, u32[]{:S(2)}) copy-start(bf16[160,1024]{1,0:T(8,128)(2,1)} %get-tuple-element.84) | copy-start | bytes 983044
  238.6 24.0 %copy-start.1 = (bf16[160,1024]{1,0:T(8,128)(2,1)S(1)}, bf16[160,1024]{1,0:T(8,128)(2,1)}, u32[]{:S(2)}) copy-start(bf16[160,1024]{1,0:T(8,128)(2,1)} %get-tuple-element.85) | copy-start | bytes 983044
Sparse Core Ops, SparseCore 0:
  20.9 65.4 all-gather.1
  143.2 94.9 reduce-scatter.1

commit v9 on v8

--- a/solution.py
+++ b/solution.py
@@ -611,15 +611,11 @@
     hid,
     h_t,
     hid_t,
-    dw,
-    sibling_dw,
     wsem,
     ss1,
     rs1,
     ss2,
     rs2,
-    ss3,
-    rs3,
 ):
     me, z, y, c = coords()
     barrier = pltpu.get_barrier_semaphore()
@@ -627,7 +623,6 @@
         pl.semaphore_signal(
             barrier, inc=1, device_id=(lax.rem(me + k, NX), z, y, c), device_id_type=MESH
         )
-    pl.semaphore_signal(barrier, inc=1, device_id=(me, z, y, 1 - c), device_id_type=MESH)
     loads = [
         pltpu.make_async_copy(wide.at[:, pl.ds(at, width)], there, wsem.at[i])
         for i, (at, width, there) in enumerate(
@@ -649,7 +644,7 @@
     mid_o[...] = middle
     r = lax.rsqrt(jnp.mean(middle * middle, axis=-1, keepdims=True) + EPSILON)
     h_all[me] = (middle * r * g_ffn[...]).astype(BF16)
-    pl.semaphore_wait(barrier, NX)
+    pl.semaphore_wait(barrier, NX - 1)
 
     def send_h(t, place):
         return pltpu.make_async_remote_copy(
@@ -718,17 +713,14 @@
 
     lax.fori_loop(0, NX, block, 0)
 
-    def to_sibling(i, at):
-        return pltpu.make_async_remote_copy(
-            src_ref=dw.at[pl.ds(pl.multiple_of((1 - c) * 512, 512), 512), at],
-            dst_ref=sibling_dw.at[:, at],
-            send_sem=ss3.at[i],
-            recv_sem=rs3.at[i],
-            device_id=(me, z, y, 1 - c),
-            device_id_type=MESH,
-        )
-
-    down = pl.ds(2 * FX, FX)
+    h_t[...] = h_all[...].reshape(NX * ROWS, D).T
+
+    def columns(j, carry):
+        at = pl.ds(pl.multiple_of(j * 256, 256), 256)
+        dw_o[:, at] = nn(h_t[...], ggu[:, at]).astype(BF16)
+        return carry
+
+    lax.fori_loop(0, 2 * FX // 256, columns, 0)
     hid_t[...] = hid[...].T
     for q in range(NX):
         cot_q = cot[:, :, q * 256 : (q + 1) * 256].reshape(NX * ROWS, 256)
@@ -736,26 +728,10 @@
         for o in range(8):
             for rg in range(9):
                 for l in range(2):
-                    row = o * 144 + rg * 16
-                    there = ((o % 2) * 16 + q * 4 + o // 2) * 32 + l * 16
-                    dw[there : there + 16, 2 * FX + rg * 128 : 2 * FX + rg * 128 + 128] = grad[
+                    row, there = o * 144 + rg * 16, (q * 8 + o) * 32 + l * 16
+                    dw_o[there : there + 16, 2 * FX + rg * 128 : 2 * FX + rg * 128 + 128] = grad[
                         row : row + 16, l * 128 : l * 128 + 128
                     ]
-    to_sibling(9, down).start()
-    h_rows = h_all[...].reshape(NX * ROWS, D).T
-    for o in range(32):
-        there = ((o % 2) * 16 + o // 2) * 32
-        h_t[there : there + 32, :] = h_rows[o * 32 : o * 32 + 32, :]
-
-    def chunk(j):
-        return pl.ds(pl.multiple_of(j * 256, 256), 256)
-
-    def columns(j, carry):
-        dw[:, chunk(j)] = nn(h_t[...], ggu[:, chunk(j)]).astype(BF16)
-        to_sibling(j, chunk(j)).start()
-        return carry
-
-    lax.fori_loop(0, 2 * FX // 256, columns, 0)
 
     grad_h = part[me].astype(F32)
     for k in (1, 3, 2):
@@ -780,20 +756,6 @@
             top, bottom = grad[:BLK, p * 128 : p * 128 + 128], grad[BLK:, p * 128 : p * 128 + 128]
             back_o[4 * q + 2 * p, :, :] = jnp.where(m, top, swap(bottom)).astype(BF16)
             back_o[4 * q + 2 * p + 1, :, :] = jnp.where(m, swap(top), bottom).astype(BF16)
-    half = pl.ds(pl.multiple_of(c * 512, 512), 512)
-
-    def both(at):
-        dw_o[:, at] = (dw[half, at].astype(F32) + sibling_dw[:, at].astype(F32)).astype(BF16)
-
-    to_sibling(9, down).wait()
-    both(down)
-
-    def add(j, carry):
-        to_sibling(j, chunk(j)).wait()
-        both(chunk(j))
-        return carry
-
-    lax.fori_loop(0, 2 * FX // 256, add, 0)
 
 
 def middle_part(number, parts, tokens, cot, g_ffn, wide):
@@ -806,7 +768,7 @@
         out_shape=[
             jax.ShapeDtypeStruct((ROWS, D), F32),
             jax.ShapeDtypeStruct(blocks, BF16),
-            jax.ShapeDtypeStruct((D // 2, 3 * FX), BF16),
+            jax.ShapeDtypeStruct((D, 3 * FX), BF16),
             jax.ShapeDtypeStruct((ROWS, D), F32),
             jax.ShapeDtypeStruct((ROWS, D), BF16),
             jax.ShapeDtypeStruct((NX, ROWS, QX), BF16),
@@ -827,15 +789,11 @@
             pltpu.VMEM((NX * ROWS, FX), BF16),
             pltpu.VMEM((D, NX * ROWS), BF16),
             pltpu.VMEM((FX, NX * ROWS), BF16),
-            pltpu.VMEM((D, 3 * FX), BF16),
-            pltpu.VMEM((D // 2, 3 * FX), BF16),
             pltpu.SemaphoreType.DMA((3,)),
             pltpu.SemaphoreType.DMA((NX,)),
             pltpu.SemaphoreType.DMA((NX,)),
             pltpu.SemaphoreType.DMA((NX,)),
             pltpu.SemaphoreType.DMA((NX,)),
-            pltpu.SemaphoreType.DMA((10,)),
-            pltpu.SemaphoreType.DMA((10,)),
         ],
         compiler_params=pltpu.CompilerParams(
             collective_id=number, has_side_effects=True, vmem_limit_bytes=VMEM_BYTES
@@ -1221,7 +1179,7 @@
     middle, result4, grad_w_ffn, grad_middle, grad_branch, mixed, back_parts, gain_ffn = middle_part(
         4, mixed_parts, tokens[0], cot_all, g_ffn[None], wide
     )
-    sums = lax.psum_scatter(grad_w_ffn, CTX, scatter_dimension=0, tiled=True)
+    sums = lax.psum_scatter(grad_w_ffn, CTX_FSDP, scatter_dimension=0, tiled=True)
     (recv_g,) = exchange(6, "to_heads_back", ("r", "a2a", back_parts))
     sends_back = attend_back(pair, recv_g, q_s, k_s, v_s, o_t, inv)
     recv_back, branch_x, mixed_x = exchange(

time: 271 us -> 272 us (level)
  waiting for transfers between devices: 4.35 us -> 17 us
  Pallas kernels: 239 us -> 228 us
    reduce_scatter x1, waiting for transfers between devices: 0.02 us -> 12.6 us  [body(): lax.psum_scatter(grad_w_ffn, CTX_FSDP, scatter_dimension=0, tiled=True)]
    pallas_call x5, Pallas kernels: 97.8 us -> 90.6 us  [exchange(): pl.pallas_call(functools.partial(exchange_kernel, items), out_shape=outs,...]
    pallas_call x1, Pallas kernels: 39.8 us -> 36.8 us  [middle_part(): pl.pallas_call(middle_kernel, in_specs=[vmem] * 4 + [pl.BlockSpec(memory_...]
  transfers between devices with their start and end apart: 3 -> 3, of which waited for: 1 -> 2; matrix products, arithmetic and copies ran while one was open for 1% -> 1% of each run, Pallas kernels for 66% -> 63%
where the time goes in v9:
time: 272 us; the launch traced here: 271 us
  Pallas kernels  228 us (84%)
  waiting for transfers between devices  17 us (6%)
  between operations  14.2 us (5%)
  starting transfers between devices  5.81 us (2%)
  local copies, waits for them, and re-layouts  4.67 us (2%)
    pallas_call x5, Pallas kernels, exchange(): pl.pallas_call(functools.partial(exchange_kernel, items), out_shape=outs,...  90.6 us
    pallas_call x1, Pallas kernels, project_back(): pl.pallas_call(project_back_kernel, in_specs=[vmem] * 16, out_specs=[vmem...  37.8 us
    pallas_call x1, Pallas kernels, middle_part(): pl.pallas_call(middle_kernel, in_specs=[vmem] * 4 + [pl.BlockSpec(memory_...  36.8 us
    pallas_call x1, Pallas kernels, gather_in(): pl.pallas_call(gather_in_kernel, in_specs=[pl.BlockSpec(memory_space=pltp...  23.5 us
    pallas_call x1, Pallas kernels, attend_back(): pl.pallas_call(attend_back_kernel, grid_spec=pltpu.PrefetchScalarGridSpec...  18.2 us
    reduce_scatter x1, waiting for transfers between devices, body(): lax.psum_scatter(grad_w_ffn, CTX_FSDP, scatter_dimension=0, tiled=True)  12.6 us
    pallas_call x1, Pallas kernels, attend(): pl.pallas_call(attend_kernel, grid_spec=pltpu.PrefetchScalarGridSpec(num_...  10.7 us
    pallas_call x1, Pallas kernels, project(): pl.pallas_call(project_kernel, grid_spec=pltpu.PrefetchScalarGridSpec(num...  7.18 us
  transfers between devices with their start and end apart: 3, of which 2 were waited for; matrix products, arithmetic and copies ran while one was open for 1% of the time, Pallas kernels for 63%

profile of v9, /device:TPU:4, one launch (start us, length us, event | category | flops | bytes accessed | tf_op | source)
XLA Modules:
  0.0 271.4 jit_solution(2544997537260092761)
XLA Ops:
  7.2 0.0 copy-start
  7.2 0.0 copy-start.4
  7.2 0.0 copy-start.3
  7.2 0.0 all-gather.2.cloned.1.call-start
  7.3 0.9 copy-done
  8.2 5.7 %collective-permute-start = (bf16[144,256]{1,0:T(8,128)(2,1)S(1)}, bf16[144,256]{1,0:T(8,128)(2,1)S(1)}, u32[]{:S(2)}, u32[]{:S(2)}) collective-permute-start(bf16[144,256]{1,0:T(8,128)(2,1)S(1)} %constant_dynamic-slice_fusion), channel_id=1, source_target_pairs={{0,0},{8,32},{16,64},{24,96},{32,8},{40,40},{48,72},{56,104},{64,1... | collective-permute-start | bytes 221192 | tf_op jit(solution)/shard_map/ppermute | solution.py:1163
  13.9 0.9 constant_dynamic-slice_fusion.1
  14.8 4.3 %collective-permute-done = bf16[144,256]{1,0:T(8,128)(2,1)S(1)} collective-permute-done((bf16[144,256]{1,0:T(8,128)(2,1)S(1)}, bf16[144,256]{1,0:T(8,128)(2,1)S(1)}, u32[]{:S(2)}, u32[]{:S(2)}) %collective-permute-start) | collective-permute-done | bytes 73760 | tf_op jit(solution)/shard_map/ppermute | solution.py:1163
  19.2 1.6 pad_maximum_fusion
  20.8 0.0 all-gather.2.cloned.1.call-update
  20.8 0.0 reduce-scatter.2.cloned.1.call-start
  20.9 23.5 %gather_in.1 = (bf16[4,160,1024]{2,1,0:T(8,128)(2,1)}, bf16[32,32,512]{2,1,0:T(8,128)(2,1)}, s32[4,8,128]{2,1,0:T(8,128)}) custom-call(bf16[160,1024]{1,0:T(8,128)(2,1)} %bitcast.29, f32[1,1024]{1,0:T(1,128)} %bitcast.40, bf16[32,1024]{1,0:T(8,128)(2,1)} %w_q.1, bf16[32,512]{1,0:T(8,128)(2,1)} %w_k.1, bf16[32,512]{1,0:T(8,128)(2,1)} %w_v.1, s32[1,16]{1,0:T(1,128)} %pairs.1), custom_call_target="tpu_custom_call" | custom-call | tf_op jit(solution)/shard_map/gather_in/pallas_call | solution.py:382
  44.4 0.0 copy-done.4
  44.4 0.0 copy-done.3
  44.4 0.6 maximum_bitcast_fusion
  45.0 7.2 %project.1 = (bf16[16,240,128]{2,1,0:T(8,128)(2,1)}, f32[640,384]{1,0:T(8,128)}, f32[640,128]{1,0:T(8,128)}, f32[640,128]{1,0:T(8,128)}) custom-call(s32[32,128]{1,0:T(8,128)} %bitcast.37, bf16[640,1024]{1,0:T(8,128)(2,1)} %bitcast.25, bf16[1024,512]{1,0:T(8,128)(2,1)} %bitcast.27, f32[2560,128]{1,0:T(8,128)} %constant.20.clone.cos_t, ...), custom_call_target="tpu_custom_call" | custom-call | tf_op jit(solution)/shard_map/project/pallas_call | solution.py:432
  52.2 25.9 %to_heads.1 = (bf16[16,240,128]{2,1,0:T(8,128)(2,1)}, bf16[4,160,1024]{2,1,0:T(8,128)(2,1)}) custom-call(bf16[16,240,128]{2,1,0:T(8,128)(2,1)} %get-tuple-element.62.refs_0_, bf16[160,1024]{1,0:T(8,128)(2,1)} %bitcast.33), custom_call_target="tpu_custom_call" | custom-call | tf_op jit(solution)/shard_map/to_heads/pallas_call | solution.py:190
  78.1 10.7 %attend.1 = (bf16[16,80,128]{2,1,0:T(8,128)(2,1)}, bf16[2560,128]{1,0:T(8,128)(2,1)}, bf16[2560,128]{1,0:T(8,128)(2,1)}, bf16[2560,128]{1,0:T(8,128)(2,1)}, f32[64,2560]{1,0:T(8,128)}, /*index=5*/f32[8,2560]{1,0:T(8,128)}) custom-call(s32[32,128]{1,0:T(8,128)} %bitcast.38, bf16[16,240,128]{2,1,0:T(8,128)(2,1)} %get-tuple-element.63.recv), custom_call_target="tpu_custom_call" | custom-call | tf_op jit(solution)/shard_map/attend/pallas_call | solution.py:495
  88.8 14.3 %to_tokens.1.parts = bf16[16,80,128]{2,1,0:T(8,128)(2,1)} custom-call(bf16[16,80,128]{2,1,0:T(8,128)(2,1)} %get-tuple-element.64.refs_0_), custom_call_target="tpu_custom_call" | custom-call | tf_op jit(solution)/shard_map/to_tokens/pallas_call | solution.py:190
  103.2 0.0 all-gather.2.cloned.1.call-done.wide
  103.2 36.8 %middle_part.1 = (f32[160,1024]{1,0:T(8,128)}, bf16[4,160,1024]{2,1,0:T(8,128)(2,1)}, bf16[1024,3456]{1,0:T(8,128)(2,1)}, f32[160,1024]{1,0:T(8,128)}, bf16[160,...) custom-call(bf16[16,80,128]{2,1,0:T(8,128)(2,1)} %to_tokens.1.parts, ...), custom_call_target="tpu_custom_call" | custom-call | tf_op jit(solution)/shard_map/middle_part/pallas_call | solution.py:764
  140.0 0.0 reduce-scatter.2.cloned.1.call-update
  140.0 15.7 %to_heads_back.1.recv = bf16[16,80,128]{2,1,0:T(8,128)(2,1)} custom-call(bf16[16,80,128]{2,1,0:T(8,128)(2,1)} %get-tuple-element.66.refs_0_), custom_call_target="tpu_custom_call" | custom-call | tf_op jit(solution)/shard_map/to_heads_back/pallas_call | solution.py:190
  155.7 18.2 %attend_back.1.refs_0_ = bf16[16,240,128]{2,1,0:T(8,128)(2,1)} custom-call(s32[32,128]{1,0:T(8,128)} %bitcast.39, bf16[16,80,128]{2,1,0:T(8,128)(2,1)} %to_heads_back.1.recv, bf16[2560,128]{1,0:T(8,128)(2,1)} %get-tuple-element.67.q_s, bf16[2560,128]{1,0:T(8,128)(2,1)} %get-tuple-element.68.k_s, bf16[2560,128]{1,0:T(8,128)(2,1)} %get-tuple-element.69.v_s, ...), custom_call_target="tpu_custom_call" | custom-call | tf_op jit(solution)/shard_map/attend_back/pallas_call | solution.py:566
  174.0 16.9 %to_tokens_back.1 = (bf16[16,240,128]{2,1,0:T(8,128)(2,1)}, bf16[4,160,1024]{2,1,0:T(8,128)(2,1)}, bf16[4,160,256]{2,1,0:T(8,128)(2,1)}) custom-call(bf16[16,240,128]{2,1,0:T(8,128)(2,1)} %attend_back.1.refs_0_, bf16[160,1024]{1,0:T(8,128)(2,1)} %get-tuple-element.72.refs_1_, bf16[4,160,256]{2,1,0:T(8,128)(2,1)} %get-tuple-element.73.refs_2_), custom_call_target="tpu_custom_call" | custom-call | tf_op jit(solution)/shard_map/to_tokens_back/pallas_call | solution.py:190
  190.8 37.8 %project_back.1 = (bf16[160,1024]{1,0:T(8,128)(2,1)}, bf16[160,1024]{1,0:T(8,128)(2,1)}, bf16[32,512]{1,0:T(8,128)(2,1)}, bf16[32,256]{1,0:T(8,128)(2,1)}, f32[24,128]{1,0:T(8,128)}) custom-call(bf16[16,240,128]{2,1,0:T(8,128)(2,1)} %get-tuple-element.74.recv, f32[640,384]{1,0:T(8,128)} %get-tuple-element.75.raw, bf16[640,1024]{1,0:T(8,128)(2,1)} %bitcast.26, ...), custom_call_target="tpu_custom_call" | custom-call | tf_op jit(solution)/shard_map/project_back/pallas_call | solution.py:1053
  228.7 0.0 copy-start.2
  228.7 0.0 copy-start.1
  228.7 12.6 %reduce-scatter.2.cloned.1.call-done.refs_1_.refs_3_ = bf16[32,3456]{1,0:T(8,128)(2,1)} async-done(((bf16[1024,3456]{1,0:T(8,128)(2,1)}), bf16[32,3456]{1,0:T(8,128)(2,1)}) %reduce-scatter.2.cloned.1.call-update) | async-done | bytes 221200 | tf_op jit(solution)/shard_map/reduce_scatter | solution.py:1182
  241.3 17.8 %gather_out.1 = (bf16[4,32,512]{2,1,0:T(8,128)(2,1)}, bf16[4,32,2304]{2,1,0:T(8,128)(2,1)}, bf16[4,32,256]{2,1,0:T(8,128)(2,1)}, bf16[4,32,1152]{2,1,0:T(8,128)(2,1)}, f32[4,24,128]{2,1,0:T(8,128)}) custom-call(bf16[32,512]{1,0:T(8,128)(2,1)} %get-tuple-element.86.refs_0_, bf16[32,3456]{1,0:T(8,128)(2,1)} %reduce-scatter.2.cloned.1.call-done.refs_1_.refs_3_, ...), custom_call_target="tpu_custom_call" | custom-call | tf_op jit(solution)/shard_map/gather_out/pallas_call | solution.py:190
  259.2 2.6 hand_out.1
  261.8 1.3 slice_bitcast_fusion
  263.1 0.0 copy-done.2
  263.1 0.7 copy.36
  263.8 0.0 copy-done.1
  263.8 0.7 copy.37
  (4 shorter events, 0.1 us)
Async XLA Ops:
  7.2 1.0 copy-start
  7.2 37.2 %copy-start.4 = (f32[64]{0:T(128)S(1)}, f32[64]{0:T(128)}, u32[]{:S(2)}) copy-start(f32[64]{0:T(128)} %param.27) | copy-start | bytes 772
  7.2 37.2 %copy-start.3 = (f32[64]{0:T(128)S(1)}, f32[64]{0:T(128)}, u32[]{:S(2)}) copy-start(f32[64]{0:T(128)} %param.26) | copy-start | bytes 772
  7.2 96.0 %all-gather.2.cloned.1.call-start = ((), (), s32[]{:S(2)}) async-start(), calls=%async_computation.1 | async-start | bytes 9461760 | tf_op jit(solution)/shard_map/all_gather | solution.py:1169
  8.2 11.0 %collective-permute-start = (bf16[144,256]{1,0:T(8,128)(2,1)S(1)}, bf16[144,256]{1,0:T(8,128)(2,1)S(1)}, u32[]{:S(2)}, u32[]{:S(2)}) collective-permute-start(bf16[144,256]{1,0:T(8,128)(2,1)S(1)} %constant_dynamic-slice_fusion), channel_id=1, source_target_pairs={{0,0},{8,32},{16,64},{24,96},{32,8},{40,40},{48,72},{56,104},{64,1... | collective-permute-start | bytes 221192 | tf_op jit(solution)/shard_map/ppermute | solution.py:1163
  20.8 220.5 %reduce-scatter.2.cloned.1.call-start = ((), (), s32[]{:S(2)}) async-start(), calls=%async_computation.2 | async-start | bytes 7299072 | tf_op jit(solution)/shard_map/reduce_scatter | solution.py:1182
  228.7 34.4 %copy-start.2 = (bf16[160,1024]{1,0:T(8,128)(2,1)S(1)}, bf16[160,1024]{1,0:T(8,128)(2,1)}, u32[]{:S(2)}) copy-start(bf16[160,1024]{1,0:T(8,128)(2,1)} %get-tuple-element.84) | copy-start | bytes 983044
  228.7 35.1 %copy-start.1 = (bf16[160,1024]{1,0:T(8,128)(2,1)S(1)}, bf16[160,1024]{1,0:T(8,128)(2,1)}, u32[]{:S(2)}) copy-start(bf16[160,1024]{1,0:T(8,128)(2,1)} %get-tuple-element.85) | copy-start | bytes 983044
Sparse Core Ops, SparseCore 0:
  20.9 65.4 all-gather.1
  140.1 101.1 reduce-scatter.1
